TPU v7x, 256 devices: a whole 4x4x8 slice. The times are simulated.
256 devices in a mesh: dom: 64 (over y, z, core), rep: 4 (over x).
Axes of the slice: x: 4, y: 4, z: 8, core: 2. Of those that a mesh axis runs over, the one named last changes fastest.
Arguments:
- features: bfloat16 [1048576, 128], P(('dom', 'rep')), may hold values from -6 to 6
- out_grad: bfloat16 [1048576, 256], P(('dom', 'rep')), may hold values from -6 to 6
- w_self: bfloat16 [128, 256], replicated, may hold values from -0.5 to 0.5
- w_nbr: bfloat16 [128, 256], replicated, may hold values from -0.5 to 0.5
- hub_rows: int32 [4096], P(('dom', 'rep')), may hold values from 0 to 4095
- send_rows: int32 [16384, 32], P(('dom', 'rep')), may hold values from 0 to 4095
- send_counts: int32 [16384], P(('dom', 'rep')), may hold values from 0 to 32
- tile_targets: int32 [32768], P(('dom', 'rep')), may hold values from 0 to 31, as said below
- tile_sources: int32 [32768], P(('dom', 'rep')), may hold values from 0 to 79
- tile_count: int32 [256], P(('dom', 'rep')), may hold values from 32 to 128, as said below
- tile_weights: bfloat16 [32768, 128, 128], P(('dom', 'rep')), may hold values from 0 to 1, as said below
Outputs:
- hidden_out: bfloat16 [1048576, 256], P(('dom', 'rep'))
- grad_features: float32 [1048576, 128], P(('dom', 'rep'))
- grad_w_self: float32 [128, 256], replicated
- grad_w_nbr: float32 [128, 256], replicated
Inputs may be any that keep to these rules, and one draw needn't show every extreme that they name: `hub_rows`: rows of the device that owns the entry. `send_rows`: rows of the sending device; list q of a device goes to the device at dom index q with the same rep index. `tile_targets`: the first 32 slots of each device name its 32 target blocks in order. `tile_sources`: source blocks 0 to 31 are the device's own rows, then come the hub rows, then the halo slots. `tile_count`: some device uses all 128 slots and some only 32. `tile_weights`: Nonnegative; most entries are zero.
All inputs are finite; a program needn't handle non-finite values.
Results may differ from a plain program's by a relative error of at most 0.0051.
Values may be sent and summed in bfloat16 or wider, within the bound.
No kernel may reach another device: no remote copies, remote signals or barrier semaphores. Data moves between devices by JAX's collectives and lax.ppermute only.
A program may use at most 128 MiB of HBM per device.

v0:
```python
import math

import jax
import jax.numpy as jnp
from jax import lax
from jax.sharding import PartitionSpec as P


def silu_slope(preact):
    sigmoid = jax.nn.sigmoid(preact)
    return sigmoid * (1.0 + preact * (1.0 - sigmoid))


def shards(
    features,
    out_grad,
    w_self,
    w_nbr,
    hub_rows,
    send_rows,
    send_counts,
    tile_targets,
    tile_sources,
    tile_count,
    tile_weights,
):
    highest = lax.Precision.HIGHEST
    node_rows, feature_width = features.shape
    block_rows = tile_weights.shape[1]
    dom_size = lax.axis_size("dom")
    rep_size = lax.axis_size("rep")
    slots = send_rows.shape[1]
    own_hubs = jnp.take(features, hub_rows, 0)
    hub_feats = lax.all_gather(own_hubs, ("dom", "rep"), axis=0, tiled=True)
    slot_live = jnp.arange(slots, dtype=jnp.int32)[None, :] < send_counts[:, None]
    outgoing = jnp.take(features, send_rows.reshape(-1), 0).reshape(dom_size, slots, feature_width)
    outgoing = outgoing * slot_live[:, :, None].astype(features.dtype)
    halo_feats = lax.all_to_all(outgoing, "dom", split_axis=0, concat_axis=0, tiled=True).reshape(
        dom_size * slots, feature_width
    )
    sources = jnp.concatenate([features, hub_feats, halo_feats], 0)
    source_blocks = sources.shape[0] // block_rows
    target_blocks = node_rows // block_rows
    picked = jnp.take(sources.reshape(source_blocks, block_rows, feature_width), tile_sources, 0)
    tile_live = jnp.arange(tile_targets.shape[0], dtype=jnp.int32) < tile_count[0]
    target_hot = (
        (tile_targets[:, None] == jnp.arange(target_blocks, dtype=jnp.int32)[None, :])
        & tile_live[:, None]
    ).astype(jnp.float32)
    products = jnp.einsum("tij,tjf->tif", tile_weights, picked, preferred_element_type=jnp.float32)
    numerator = jnp.einsum("tb,tif->bif", target_hot, products, precision=highest).reshape(
        node_rows, feature_width
    )
    row_sums = jnp.einsum(
        "tb,ti->bi", target_hot, jnp.sum(tile_weights, 2, dtype=jnp.float32), precision=highest
    ).reshape(node_rows)
    denominator = jnp.maximum(row_sums, 1.0)
    aggregate = (numerator / denominator[:, None]).astype(jnp.bfloat16)
    preact = jnp.dot(features, w_self, preferred_element_type=jnp.float32) + jnp.dot(
        aggregate, w_nbr, preferred_element_type=jnp.float32
    )
    hidden_out = jax.nn.silu(preact).astype(jnp.bfloat16)
    grad_preact = (out_grad.astype(jnp.float32) * silu_slope(preact)).astype(jnp.bfloat16)
    self_term = jnp.einsum("nf,nh->fh", features, grad_preact, preferred_element_type=jnp.float32)
    nbr_term = jnp.einsum("nf,nh->fh", aggregate, grad_preact, preferred_element_type=jnp.float32)
    self_sum, nbr_sum = lax.psum((self_term, nbr_term), ("dom", "rep"))
    grad_scale = 1.0 / math.sqrt(node_rows * dom_size * rep_size)
    grad_w_self = self_sum * grad_scale
    grad_w_nbr = nbr_sum * grad_scale
    grad_agg = (
        jnp.einsum("nh,fh->nf", grad_preact, w_nbr, preferred_element_type=jnp.float32)
        / denominator[:, None]
    ).astype(jnp.bfloat16)
    grad_tiles = jnp.take(
        grad_agg.reshape(target_blocks, block_rows, feature_width), tile_targets, 0
    ) * tile_live[:, None, None].astype(jnp.bfloat16)
    grad_products = jnp.einsum(
        "tij,tif->tjf", tile_weights, grad_tiles, preferred_element_type=jnp.float32
    )
    source_hot = (
        tile_sources[:, None] == jnp.arange(source_blocks, dtype=jnp.int32)[None, :]
    ).astype(jnp.float32)
    grad_sources = jnp.einsum("ts,tjf->sjf", source_hot, grad_products, precision=highest).reshape(
        source_blocks * block_rows, feature_width
    )
    hub_total = hub_feats.shape[0]
    hub_term = grad_sources[node_rows : node_rows + hub_total]
    halo_term = grad_sources[node_rows + hub_total :].reshape(dom_size, slots, feature_width)
    own_hub_grads = lax.psum_scatter(hub_term, ("dom", "rep"), scatter_dimension=0, tiled=True)
    returned = lax.all_to_all(
        halo_term.astype(jnp.bfloat16), "dom", split_axis=0, concat_axis=0, tiled=True
    ).astype(halo_term.dtype) * slot_live[:, :, None].astype(jnp.float32)
    grad_features = (
        jnp.einsum("nh,fh->nf", grad_preact, w_self, preferred_element_type=jnp.float32)
        + grad_sources[:node_rows]
    )
    grad_features = grad_features + jax.ops.segment_sum(
        own_hub_grads, hub_rows, num_segments=node_rows
    )
    grad_features = grad_features + jax.ops.segment_sum(
        returned.reshape(-1, feature_width), send_rows.reshape(-1), num_segments=node_rows
    )
    return (hidden_out, grad_features, grad_w_self, grad_w_nbr)


def solution(mesh):
    return jax.shard_map(
        shards,
        mesh=mesh,
        in_specs=(
            P(("dom", "rep"), None),
            P(("dom", "rep"), None),
            P(),
            P(),
            P(("dom", "rep")),
            P(("dom", "rep"), None),
            P(("dom", "rep")),
            P(("dom", "rep")),
            P(("dom", "rep")),
            P(("dom", "rep")),
            P(("dom", "rep"), None, None),
        ),
        out_specs=(P(("dom", "rep"), None), P(("dom", "rep"), None), P(), P()),
        check_vma=False,
    )
```

profile of v0, /device:TPU:32, one launch (start us, length us, event | category | flops | bytes accessed | tf_op | source)
XLA Modules:
  0.0 1724.9 jit_solution(5630084148629157819)
XLA Ops:
  7.2 0.7 compare_and_fusion.2
  7.9 0.7 compare_select_fusion.3
  8.6 1.9 gather_fusion
  10.5 0.7 broadcast_select_fusion
  11.2 0.7 compare_and_fusion
  11.9 0.8 copy.23
  12.7 0.1 copy.22
  12.9 0.7 fusion.23
  13.7 7.0 gather_fusion.1
  20.7 1.4 select_multiply_fusion
  22.1 11.8 all-to-all-start
  34.6 3.4 convert_reduce_fusion
  38.0 0.1 fusion.16
  38.2 2.6 fusion.38
  40.8 10.2 all-to-all-done
  51.0 66.6 %all-gather.2.cloned.1.call-done = bf16[4096,128]{1,0:T(8,128)(2,1)} async-done(((bf16[16,128]{1,0:T(8,128)(2,1)}), bf16[4096,128]{1,0:T(8,128)(2,1)}) %all-gather.2.cloned.1.call-update) | async-done | bytes 1048592 | tf_op jit(solution)/shard_map/all_gather | solution.py:34
  117.6 11.3 pad_maximum_fusion
  128.9 4.8 gather_fusion.2
  133.6 9.9 fusion.8
  143.6 9.3 copy.31
  152.8 5.4 fusion.2
  158.3 1.2 copy.24
  159.5 0.9 fusion.12
  160.5 0.7 copy-done.9
  161.2 3.3 multiply_convert_fusion
  164.5 1.6 fusion.39
  166.1 1.4 convolution_bitcast_fusion
  167.5 0.9 fusion.4
  168.4 3.0 gather_fusion.3
  171.4 8.5 fusion.5
  180.0 9.3 copy.32
  189.2 9.4 fusion
  198.7 4.0 fusion.37
  202.7 2.6 copy.26
  205.3 1.3 slice.34
  206.6 0.9 copy.27
  207.5 8.5 all-to-all-start.1
  216.2 2.8 copy.25
  219.0 2.0 convolution_add_fusion.1
  221.0 227.4 %all-reduce.3.cloned.1.call-done = (f32[128,256]{0,1:T(8,128)}, f32[128,256]{0,1:T(8,128)}) async-done(((f32[128,256]{0,1:T(8,128)}, f32[128,256]{0,1:T(8,128)}), (f32[128,256]{0,1:T(8,128)}, f32[128,256]{0,1:T(8,128)})) %all-reduce.3.cloned.1.call-update) | async-done | bytes 262160 | tf_op jit(solution)/shard_map/psum | solution.py:66
  448.5 0.9 broadcast_multiply_fusion.1
  449.4 0.8 copy.29
  450.1 0.9 broadcast_multiply_fusion
  451.0 0.8 copy.30
  451.8 0.8 copy-done.4
  452.6 1.4 convert_multiply_fusion
  454.0 1248.0 %reduce-scatter.2.cloned.1.call-done = f32[16,128]{1,0:T(8,128)} async-done(((f32[4096,128]{1,0:T(8,128)}), f32[16,128]{1,0:T(8,128)}) %reduce-scatter.2.cloned.1.call-update) | async-done | bytes 8208 | tf_op jit(solution)/shard_map/reduce_scatter | solution.py:89
  1701.9 16.5 scatter_custom_fusion
  (37 shorter events, 0.5 us)
Async XLA Ops:
  7.2 153.3 %copy-start = (bf16[128,256]{1,0:T(8,128)(2,1)S(1)}, bf16[128,256]{1,0:T(8,128)(2,1)}, u32[]{:S(2)}) copy-start(bf16[128,256]{1,0:T(8,128)(2,1)} %param.14) | copy-start | bytes 196612
  7.2 27.4 %copy-start.6 = (s32[128]{0:T(128)S(1)}, s32[128]{0:T(128)}, u32[]{:S(2)}) copy-start(s32[128]{0:T(128)} %param.18) | copy-start | bytes 1540
  7.2 27.4 %copy-start.7 = (s32[128]{0:T(128)S(1)}, s32[128]{0:T(128)}, u32[]{:S(2)}) copy-start(s32[128]{0:T(128)} %param.19) | copy-start | bytes 1540
  7.2 110.4 %all-gather.2.cloned.1.call-start = ((), (), s32[]{:S(2)}) async-start(), calls=%async_computation.3 | async-start | bytes 1052672 | tf_op jit(solution)/shard_map/all_gather | solution.py:34
  20.6 17.5 %copy-start.2 = (bf16[4096,128]{1,0:T(8,128)(2,1)S(1)}, bf16[4096,128]{1,0:T(8,128)(2,1)}, u32[]{:S(2)}) copy-start(bf16[4096,128]{1,0:T(8,128)(2,1)} %param.11) | copy-start | bytes 3145732
  20.7 17.5 %copy-start.5 = (bf16[128,256]{1,0:T(8,128)(2,1)S(1)}, bf16[128,256]{1,0:T(8,128)(2,1)}, u32[]{:S(2)}) copy-start(bf16[128,256]{1,0:T(8,128)(2,1)} %param.13) | copy-start | bytes 196612
  22.1 28.9 %all-to-all-start = ((bf16[64,32,128]{2,1,0:T(8,128)(2,1)}), bf16[64,32,128]{2,1,0:T(8,128)(2,1)S(1)}, u32[]{:S(2)}, u32[]{:S(2)}) async-start(bf16[64,32,128]{2,1,0:T(8,128)(2,1)} %select_multiply_fusion), calls=%async_computation | async-start | bytes 1048576 | tf_op jit(solution)/shard_map/all_to_all | solution.py:38
  33.8 414.6 %all-reduce.3.cloned.1.call-start = ((), (), s32[]{:S(2)}) async-start(), calls=%async_computation.5 | async-start | bytes 524288 | tf_op jit(solution)/shard_map/psum | solution.py:66
  158.3 2.2 copy-start.3
  158.3 2.9 copy-start.9
  198.6 1503.3 %reduce-scatter.2.cloned.1.call-start = ((), (), s32[]{:S(2)}) async-start(), calls=%async_computation.4 | async-start | bytes 2105344 | tf_op jit(solution)/shard_map/reduce_scatter | solution.py:89
  202.7 13.4 copy-start.8
  207.5 244.3 %all-to-all-start.1 = ((bf16[64,32,128]{2,1,0:T(8,128)(2,1)}), bf16[64,32,128]{2,1,0:T(8,128)(2,1)S(1)}, u32[]{:S(2)}, u32[]{:S(2)}) async-start(bf16[64,32,128]{2,1,0:T(8,128)(2,1)} %bitcast.15), calls=%async_computation.2 | async-start | bytes 1048576 | tf_op jit(solution)/shard_map/all_to_all | solution.py:90
  219.0 1499.4 %copy-start.1 = (bf16[128,256]{1,0:T(8,128)(2,1)S(1)}, bf16[128,256]{1,0:T(8,128)(2,1)}, u32[]{:S(2)}) copy-start(bf16[128,256]{1,0:T(8,128)(2,1)} %param.14) | copy-start | bytes 196612
  451.8 0.8 copy-start.4
Sparse Core Ops, SparseCore 0:
  12.3 105.2 all-gather.1
  198.7 249.6 all-reduce.2
  450.9 1250.9 reduce-scatter.1
where the time goes:
time: 1740 us; the launch traced here: 1720 us
  waiting for transfers between devices  1550 us (89%)
  local copies, waits for them, and re-layouts  52.2 us (3%)
  matrix products  45.3 us (3%)
  other arithmetic  40.2 us (2%)
  starting transfers between devices  20.4 us (1%)
    reduce_scatter x1, waiting for transfers between devices, shards(): lax.psum_scatter(hub_term, ('dom', 'rep'), scatter_dimension=0, tiled=True)  1250 us
    psum x1, waiting for transfers between devices, shards(): self_sum, nbr_sum = lax.psum((self_term, nbr_term), ('dom', 'rep'))  227 us
    all_gather x1, waiting for transfers between devices, shards(): hub_feats = lax.all_gather(own_hubs, ('dom', 'rep'), axis=0, tiled=True)  66.6 us
  transfers between devices with their start and end apart: 5, of which 4 were waited for; matrix products, arithmetic and copies ran while one was open for 2% of the time, Pallas kernels for 0%

commit v1 on v0

v1 whole, which is shorter than its diff:
```python
import math

import jax
import jax.numpy as jnp
from jax import lax
from jax.experimental import pallas as pl
from jax.experimental.pallas import tpu as pltpu
from jax.sharding import PartitionSpec as P

BF16 = jnp.bfloat16
F32 = jnp.float32
UNROLL = 4
WEIGHT_CHUNK = 16
ROWS = 256


def smem():
    return pl.BlockSpec(memory_space=pltpu.SMEM)


def vmem():
    return pl.BlockSpec(memory_space=pltpu.VMEM)


def hbm():
    return pl.BlockSpec(memory_space=pl.ANY)


def params(mebibytes):
    return pltpu.CompilerParams(vmem_limit_bytes=mebibytes * 1024 * 1024)


def rows_at(index, size):
    return pl.ds(pl.multiple_of(index * size, size), size)


def pack_kernel(hub_rows, send_rows, send_counts, features, out, wide, staged):
    node_rows = features.shape[0]
    peers, slots = send_rows.shape
    hubs = hub_rows.shape[0]
    wide[:node_rows] = features[...].astype(F32)
    wide[node_rows:] = jnp.zeros((wide.shape[0] - node_rows, wide.shape[1]), F32)
    for h in range(hubs):
        staged[h : h + 1] = wide[pl.ds(hub_rows[h], 1)]
    own_hubs = staged[:hubs].astype(BF16)

    def peer(p, carry):
        live = send_counts[p]
        base = p * slots
        for k in range(slots):
            row = jnp.where(k < live, send_rows[p, k], node_rows)
            staged[pl.ds(base + k, 1)] = wide[pl.ds(row, 1)]
        return carry

    lax.fori_loop(0, peers, peer, 0)

    def emit(p, carry):
        out[p, :slots] = staged[rows_at(p, slots)].astype(BF16)
        out[p, slots:] = own_hubs
        return carry

    lax.fori_loop(0, peers, emit, 0)


def pack(hub_rows, send_rows, send_counts, features):
    peers, slots = send_rows.shape
    hubs = hub_rows.shape[0]
    node_rows, width = features.shape
    return pl.pallas_call(
        pack_kernel,
        out_shape=jax.ShapeDtypeStruct((peers, slots + hubs, width), BF16),
        in_specs=[smem(), smem(), smem(), vmem()],
        out_specs=vmem(),
        scratch_shapes=[
            pltpu.VMEM((node_rows + 8, width), F32),
            pltpu.VMEM((peers * slots, width), F32),
        ],
        compiler_params=params(24),
        name="pack",
    )(hub_rows, send_rows, send_counts, features)


def start_weights(weights, held, sems):
    copies = []
    for c in range(weights.shape[0] // WEIGHT_CHUNK):
        part = pl.ds(c * WEIGHT_CHUNK, WEIGHT_CHUNK)
        copies.append(pltpu.make_async_copy(weights.at[part], held.at[part], sems.at[c]))
        copies[-1].start()
    return copies


def forward_kernel(
    targets,
    sources,
    count,
    weights,
    features,
    received,
    hub1,
    hub2,
    hub3,
    out_grad,
    w_self,
    w_nbr,
    hidden,
    grad_agg,
    grad_self,
    grad_w,
    held,
    source_rows,
    totals,
    w_both,
    grad_total,
    weight_sems,
    feature_sem,
):
    block = weights.shape[1]
    node_rows, width = features.shape
    target_blocks = node_rows // block
    peers = received.shape[0]
    hubs = hub1.shape[1]
    slots = received.shape[1] - hubs
    reps = 4
    weight_copies = start_weights(weights, held, weight_sems)
    feature_copy = pltpu.make_async_copy(features, source_rows.at[pl.ds(0, node_rows)], feature_sem)
    feature_copy.start()
    rep = lax.axis_index("rep")
    hub_base = node_rows
    halo_base = node_rows + peers * reps * hubs

    def place(p, carry):
        source_rows[pl.ds(pl.multiple_of(halo_base + p * slots, slots), slots)] = received[p, :slots]
        for i, piece in enumerate((received, hub1, hub2, hub3)):
            from_rep = lax.rem(rep - i + reps, reps)
            at = pl.multiple_of(hub_base + (p * reps + from_rep) * hubs, hubs)
            source_rows[pl.ds(at, hubs)] = piece[p, slots:] if i == 0 else piece[p]
        return carry

    lax.fori_loop(0, peers, place, 0)
    w_both[: w_self.shape[0]] = w_self[...]
    w_both[w_self.shape[0] :] = w_nbr[...]
    ones = jnp.ones((block, width), BF16)

    def product(t):
        picked = jnp.concatenate([source_rows[rows_at(sources[t], block)], ones], 1)
        return jnp.dot(held[t], picked, preferred_element_type=F32)

    feature_copy.wait()
    leading = target_blocks // WEIGHT_CHUNK
    for copy in weight_copies[:leading]:
        copy.wait()

    def first(g, carry):
        for u in range(UNROLL):
            t = g * UNROLL + u
            totals[t] = product(t)
        return carry

    lax.fori_loop(0, target_blocks // UNROLL, first, 0)
    for copy in weight_copies[leading:]:
        copy.wait()
    live = count[0]

    def more(g, carry):
        slots_at = [target_blocks + g * UNROLL + u for u in range(UNROLL)]
        products = [product(t) for t in slots_at]
        for t, value in zip(slots_at, products):
            target = jnp.where(t < live, targets[t], target_blocks)
            totals[target] += value
        return carry

    lax.fori_loop(0, (live - target_blocks + UNROLL - 1) // UNROLL, more, 0)
    grad_total[...] = jnp.zeros_like(grad_total)
    per_chunk = ROWS // block

    def dense(c, carry):
        rows = rows_at(c, ROWS)
        total = totals[pl.ds(c * per_chunk, per_chunk)].reshape(ROWS, 2 * width)
        inverse = 1.0 / jnp.maximum(total[:, width:], 1.0)
        aggregate = (total[:, :width] * inverse).astype(BF16)
        both = jnp.concatenate([source_rows[rows], aggregate], 1)
        preact = jnp.dot(both, w_both[...], preferred_element_type=F32)
        sigmoid = 1.0 / (1.0 + jnp.exp(-preact))
        activated = preact * sigmoid
        hidden[rows] = activated.astype(BF16)
        slope = sigmoid + activated * (1.0 - sigmoid)
        grad_preact = (out_grad[rows].astype(F32) * slope).astype(BF16)
        grad_total[...] += lax.dot_general(
            both, grad_preact, (((0,), (0,)), ((), ())), preferred_element_type=F32
        )
        back = lax.dot_general(
            grad_preact, w_both[...], (((1,), (1,)), ((), ())), preferred_element_type=F32
        )
        grad_self[rows] = back[:, :width]
        grad_agg[rows] = (back[:, width:] * inverse).astype(BF16)
        return carry

    lax.fori_loop(0, node_rows // ROWS, dense, 0)
    half = grad_total.shape[1] // 2
    grad_w[: grad_total.shape[0]] = grad_total[:, :half]
    grad_w[grad_total.shape[0] :] = grad_total[:, half:]


def forward(targets, sources, count, weights, features, received, pieces, out_grad, w_self, w_nbr):
    node_rows, width = features.shape
    tiles, block, _ = weights.shape
    hidden_width = w_self.shape[1]
    peers = received.shape[0]
    hubs = pieces[0].shape[1]
    slots = received.shape[1] - hubs
    source_rows = node_rows + peers * 4 * hubs + peers * slots
    return pl.pallas_call(
        forward_kernel,
        out_shape=(
            jax.ShapeDtypeStruct((node_rows, hidden_width), BF16),
            jax.ShapeDtypeStruct((node_rows, width), BF16),
            jax.ShapeDtypeStruct((node_rows, width), F32),
            jax.ShapeDtypeStruct((4 * width, hidden_width // 2), F32),
        ),
        in_specs=[smem()] * 3 + [hbm()] * 2 + [vmem()] * 7,
        out_specs=(vmem(),) * 4,
        scratch_shapes=[
            pltpu.VMEM((tiles, block, block), BF16),
            pltpu.VMEM((source_rows, width), BF16),
            pltpu.VMEM((node_rows // block + 1, block, 2 * width), F32),
            pltpu.VMEM((2 * width, hidden_width), BF16),
            pltpu.VMEM((2 * width, hidden_width), F32),
            pltpu.SemaphoreType.DMA((tiles // WEIGHT_CHUNK,)),
            pltpu.SemaphoreType.DMA,
        ],
        compiler_params=params(40),
        name="forward",
    )(targets, sources, count, weights, features, received, *pieces, out_grad, w_self, w_nbr)


def backward_kernel(
    targets,
    sources,
    count,
    weights,
    grad_agg,
    grad_self,
    grad_own,
    halo,
    hub0,
    hub1,
    hub2,
    hub3,
    held,
    totals,
    weight_sems,
):
    block = weights.shape[1]
    node_rows, width = grad_agg.shape
    peers, hubs, _ = hub0.shape
    peers = peers - 1
    slots = halo.shape[1]
    reps = 4
    weight_copies = start_weights(weights, held, weight_sems)
    rep = lax.axis_index("rep")
    totals[:node_rows] = grad_self[...]
    totals[node_rows:] = jnp.zeros((totals.shape[0] - node_rows, width), F32)
    spare = totals.shape[0] // block - 1
    for copy in weight_copies:
        copy.wait()
    live = count[0]

    def step(g, carry):
        slots_at = [g * UNROLL + u for u in range(UNROLL)]
        products = [
            lax.dot_general(
                held[t],
                grad_agg[rows_at(targets[t], block)],
                (((0,), (0,)), ((), ())),
                preferred_element_type=F32,
            )
            for t in slots_at
        ]
        for t, value in zip(slots_at, products):
            source = jnp.where(t < live, sources[t], spare)
            totals[rows_at(source, block)] += value
        return carry

    lax.fori_loop(0, (live + UNROLL - 1) // UNROLL, step, 0)
    grad_own[...] = totals[:node_rows]
    hub_base = node_rows
    halo_base = node_rows + peers * reps * hubs

    def emit(p, carry):
        at = pl.multiple_of(halo_base + p * slots, slots)
        halo[p] = totals[pl.ds(at, slots)].astype(BF16)
        for i, piece in enumerate((hub0, hub1, hub2, hub3)):
            to_rep = lax.rem(rep + i, reps)
            at = pl.multiple_of(hub_base + (p * reps + to_rep) * hubs, hubs)
            piece[p] = totals[pl.ds(at, hubs)].astype(BF16)
        return carry

    lax.fori_loop(0, peers, emit, 0)
    for piece in (hub0, hub1, hub2, hub3):
        piece[peers] = jnp.zeros((hubs, width), BF16)


def backward(targets, sources, count, weights, grad_agg, grad_self, peers, slots, hubs):
    node_rows, width = grad_agg.shape
    tiles, block, _ = weights.shape
    total_rows = node_rows + peers * 4 * hubs + peers * slots + block
    piece = jax.ShapeDtypeStruct((peers + 1, hubs, width), BF16)
    return pl.pallas_call(
        backward_kernel,
        out_shape=(
            jax.ShapeDtypeStruct((node_rows, width), F32),
            jax.ShapeDtypeStruct((peers, slots, width), BF16),
            piece,
            piece,
            piece,
            piece,
        ),
        in_specs=[smem()] * 3 + [hbm()] + [vmem()] * 2,
        out_specs=(vmem(),) * 6,
        scratch_shapes=[
            pltpu.VMEM((tiles, block, block), BF16),
            pltpu.VMEM((total_rows, width), F32),
            pltpu.SemaphoreType.DMA((tiles // WEIGHT_CHUNK,)),
        ],
        compiler_params=params(40),
        name="backward",
    )(targets, sources, count, weights, grad_agg, grad_self)


def merge_kernel(halo, hub0, hub1, hub2, hub3, out, w_parts):
    peers, slots, width = halo.shape
    hubs = hub0.shape[1]
    half = hubs // 2
    reps = 4
    rep = lax.axis_index("rep")
    pieces = (hub0, hub1, hub2, hub3)
    for i, piece in enumerate(pieces):
        pair = piece[peers].astype(F32)
        w_parts[lax.rem(rep - i + reps, reps)] = pair[:half] + pair[half:]
    w_total = ((w_parts[0] + w_parts[1]) + w_parts[2]) + w_parts[3]
    high = w_total.astype(BF16)
    low = (w_total - high.astype(F32)).astype(BF16)
    w_rows = jnp.concatenate([high.astype(F32), low.astype(F32)], 0).astype(BF16)

    def peer(p, carry):
        out[p, :slots] = halo[p]
        total = (hub0[p].astype(F32) + hub1[p].astype(F32)) + (
            hub2[p].astype(F32) + hub3[p].astype(F32)
        )
        out[p, slots : slots + hubs] = total.astype(BF16)
        out[p, slots + hubs :] = w_rows
        return carry

    lax.fori_loop(0, peers, peer, 0)


def merge(halo, pieces):
    peers, slots, width = halo.shape
    hubs = pieces[0].shape[1]
    return pl.pallas_call(
        merge_kernel,
        out_shape=jax.ShapeDtypeStruct((peers, slots + 2 * hubs, width), BF16),
        in_specs=[vmem()] * 5,
        out_specs=vmem(),
        scratch_shapes=[pltpu.VMEM((4, hubs // 2, width), F32)],
        compiler_params=params(24),
        name="merge",
    )(halo, *pieces)


def finish_kernel(hub_rows, send_ids, received, grad_own, out, grad_w, rows, grad_scale):
    peers, message, width = received.shape
    hubs = hub_rows.shape[0]
    slots = message - 2 * hubs
    half = hubs // 2
    node_rows = out.shape[0]

    def place(p, carry):
        rows[rows_at(p, slots)] = received[p, :slots]
        pair = received[p, slots + hubs :].astype(F32)
        grad_w[rows_at(p, half)] = (pair[:half] + pair[half:]) * grad_scale
        return carry + received[p, slots : slots + hubs].astype(F32)

    hub_total = lax.fori_loop(0, peers, place, jnp.zeros((hubs, width), F32))

    def scatter(c, carry):
        at = rows_at(c, ROWS)
        ids = lax.broadcasted_iota(jnp.int32, (ROWS, peers * slots), 0) + c * ROWS
        hot = (ids == send_ids[...]).astype(F32).astype(BF16)
        out[at] = grad_own[at] + jnp.dot(hot, rows[...], preferred_element_type=F32)
        return carry

    lax.fori_loop(0, node_rows // ROWS, scatter, 0)
    for h in range(hubs):
        out[pl.ds(hub_rows[h], 1)] += hub_total[h : h + 1]


def finish(hub_rows, send_ids, received, grad_own, grad_scale):
    peers, message, width = received.shape
    hubs = hub_rows.shape[0]
    slots = message - 2 * hubs

    def body(*refs):
        finish_kernel(*refs, grad_scale)

    return pl.pallas_call(
        body,
        out_shape=(
            jax.ShapeDtypeStruct(grad_own.shape, F32),
            jax.ShapeDtypeStruct((peers * hubs // 2, width), F32),
        ),
        in_specs=[smem()] + [vmem()] * 3,
        out_specs=(vmem(),) * 2,
        scratch_shapes=[pltpu.VMEM((peers * slots, width), BF16)],
        compiler_params=params(40),
        name="finish",
    )(hub_rows, send_ids, received, grad_own)


def rep_shift(value, shift, size):
    return lax.ppermute(value, "rep", [(j, (j + shift) % size) for j in range(size)])


def shards(
    features,
    out_grad,
    w_self,
    w_nbr,
    hub_rows,
    send_rows,
    send_counts,
    tile_targets,
    tile_sources,
    tile_count,
    tile_weights,
):
    node_rows, width = features.shape
    dom_size = lax.axis_size("dom")
    rep_size = lax.axis_size("rep")
    peers, slots = send_rows.shape
    hubs = hub_rows.shape[0]
    outgoing = pack(hub_rows, send_rows, send_counts, features)
    received = lax.all_to_all(outgoing, "dom", split_axis=0, concat_axis=0, tiled=True)
    own_rep = received[:, slots:]
    pieces = [rep_shift(own_rep, i, rep_size) for i in range(1, rep_size)]
    hidden, grad_agg, grad_self, grad_w = forward(
        tile_targets, tile_sources, tile_count, tile_weights, features, received, pieces,
        out_grad, w_self, w_nbr,
    )
    w_slices = lax.all_to_all(
        grad_w.reshape(dom_size, -1, width), "dom", split_axis=0, concat_axis=0, tiled=True
    )
    grad_own, halo, *hub_pieces = backward(
        tile_targets, tile_sources, tile_count, tile_weights, grad_agg, grad_self, peers, slots, hubs
    )
    w_slice = jnp.sum(w_slices, 0)
    high = w_slice.astype(BF16)
    low = (w_slice - high.astype(F32)).astype(BF16)
    w_pair = jnp.concatenate([high, low], 0)
    hub_pieces = [piece.at[dom_size].set(w_pair) for piece in hub_pieces]
    hub_pieces = hub_pieces[:1] + [
        rep_shift(hub_pieces[i], i, rep_size) for i in range(1, rep_size)
    ]
    back = lax.all_to_all(merge(halo, hub_pieces), "dom", split_axis=0, concat_axis=0, tiled=True)
    slot_live = jnp.arange(slots, dtype=jnp.int32)[None, :] < send_counts[:, None]
    send_ids = jnp.where(slot_live, send_rows, node_rows).reshape(1, -1)
    grad_scale = 1.0 / math.sqrt(node_rows * dom_size * rep_size)
    grad_features, grad_w = finish(hub_rows, send_ids, back, grad_own, grad_scale)
    both = jnp.concatenate([grad_w[: 2 * width], grad_w[2 * width :]], 1)
    return (hidden, grad_features, both[:width], both[width:])


def solution(mesh):
    return jax.shard_map(
        shards,
        mesh=mesh,
        in_specs=(
            P(("dom", "rep"), None),
            P(("dom", "rep"), None),
            P(),
            P(),
            P(("dom", "rep")),
            P(("dom", "rep"), None),
            P(("dom", "rep")),
            P(("dom", "rep")),
            P(("dom", "rep")),
            P(("dom", "rep")),
            P(("dom", "rep"), None, None),
        ),
        out_specs=(P(("dom", "rep"), None), P(("dom", "rep"), None), P(), P()),
        check_vma=False,
    )
```

time: 1740 us -> 175 us (0.10)
  waiting for transfers between devices: 1550 us -> 51.9 us
  matrix products: 45.3 us -> 0 us
  other arithmetic: 40.2 us -> 2.36 us
  local copies, waits for them, and re-layouts: 52.2 us -> 14.8 us
  blocking collectives: 0 us -> 34.2 us
  Pallas kernels: 0 us -> 32.7 us
    reduce_scatter x1 -> x0, waiting for transfers between devices: 1250 us -> none  [shards(): lax.psum_scatter(hub_term, ('dom', 'rep'), scatter_dimension=0, tiled=True)]
    psum x1 -> x0, waiting for transfers between devices: 227 us -> none  [shards(): self_sum, nbr_sum = lax.psum((self_term, nbr_term), ('dom', 'rep'))]
    all_gather x1 -> x0, waiting for transfers between devices: 66.6 us -> none  [shards(): hub_feats = lax.all_gather(own_hubs, ('dom', 'rep'), axis=0, tiled=True)]
    dot_general x11 -> x0, matrix products: 45.3 us -> none  [the longest x1 9.91 us: shards(): jnp.einsum('tij,tjf->tif', tile_weights, picked, preferred_element_type=j...]
    all_to_all x0 -> x1, blocking collectives: none -> 34.2 us  [shards(): lax.all_to_all(outgoing, 'dom', split_axis=0, concat_axis=0, tiled=True)]
    pallas_call x0 -> x5, Pallas kernels: none -> 32.7 us  [the longest x1 13.2 us: forward(): pl.pallas_call(forward_kernel, out_shape=(jax.ShapeDtypeStruct((node_rows...]
    ppermute x0 -> x6, waiting for transfers between devices: none -> 23.5 us  [rep_shift(): lax.ppermute(value, 'rep', [(j, (j + shift) % size) for j in range(size)])]
    dot_general x3 -> x0, local copies, waits for them, and re-layouts: 19.8 us -> none  [the longest x1 9.27 us: shards(): jnp.einsum('tij,tjf->tif', tile_weights, picked, preferred_element_type=j...]
  transfers between devices with their start and end apart: 5 -> 8, of which waited for: 4 -> 6; matrix products, arithmetic and copies ran while one was open for 2% -> 0% of each run, Pallas kernels for 0% -> 2%
where the time goes in v1:
time: 175 us; the launch traced here: 172 us
  waiting for transfers between devices  51.9 us (30%)
  starting transfers between devices  34.5 us (20%)
  blocking collectives  34.2 us (20%)
  Pallas kernels  32.7 us (19%)
  local copies, waits for them, and re-layouts  14.8 us (8%)
  other arithmetic  2.36 us (1%)
    all_to_all x1, blocking collectives, shards(): lax.all_to_all(outgoing, 'dom', split_axis=0, concat_axis=0, tiled=True)  34.2 us
    all_to_all x1, waiting for transfers between devices, shards(): lax.all_to_all(merge(halo, hub_pieces), 'dom', split_axis=0, concat_axis=...  27.7 us
    ppermute x6, waiting for transfers between devices, rep_shift(): lax.ppermute(value, 'rep', [(j, (j + shift) % size) for j in range(size)])  23.5 us
    unnamed x43, local copies, waits for them, and re-layouts  14.6 us
    pallas_call x1, Pallas kernels, forward(): pl.pallas_call(forward_kernel, out_shape=(jax.ShapeDtypeStruct((node_rows...  13.2 us
    ppermute x6, starting transfers between devices, rep_shift(): lax.ppermute(value, 'rep', [(j, (j + shift) % size) for j in range(size)])  11.5 us
    all_to_all x1, starting transfers between devices, shards(): lax.all_to_all(grad_w.reshape(dom_size, -1, width), 'dom', split_axis=0,...  11.5 us
    all_to_all x1, starting transfers between devices, shards(): lax.all_to_all(merge(halo, hub_pieces), 'dom', split_axis=0, concat_axis=...  11.5 us
  transfers between devices with their start and end apart: 8, of which 6 were waited for; matrix products, arithmetic and copies ran while one was open for 0% of the time, Pallas kernels for 2%

profile of v1, /device:TPU:32, one launch (start us, length us, event | category | flops | bytes accessed | tf_op | source)
XLA Modules:
  0.0 171.9 jit_solution(14732538850859429175)
XLA Ops:
  0.7 0.8 copy.17.send_rows
  1.5 1.2 copy-done.2
  2.7 0.7 copy-done.13
  3.3 0.7 copy-done.15
  4.0 4.6 %pack.1 = bf16[64,48,128]{2,1,0:T(8,128)(2,1)S(1)} custom-call(s32[16]{0:T(128)S(1)} %copy-done.15, s32[64,32]{1,0:T(8,128)S(1)} %copy.17.send_rows, s32[64]{0:T(128)S(1)} %copy-done.13, bf16[4096,128]{1,0:T(8,128)(2,1)S(1)} %copy-done.2), custom_call_target="tpu_custom_call" | custom-call | tf_op jit(solution)/shard_map/pack/pallas_call | solution.py:69
  8.7 34.2 %all_to_all.15.received = bf16[64,48,128]{2,1,0:T(8,128)(2,1)S(1)} all-to-all(bf16[64,48,128]{2,1,0:T(8,128)(2,1)S(1)} %pack.1), channel_id=1, replica_groups=mesh['dom'=64,'rep'=4] {'dom'}, dimensions={0} | all-to-all | bytes 1572864 | tf_op jit(solution)/shard_map/all_to_all | solution.py:443
  42.9 2.8 %collective-permute-start.2 = (bf16[64,16,128]{2,1,0:T(8,128)(2,1)S(1)}, bf16[64,16,128]{2,1,0:T(8,128)(2,1)S(1)}, u32[]{:S(2)}, u32[]{:S(2)}) collective-permute-start(bf16[64,16,128]{2,1,0:T(8,128)(2,1)S(1)} %slice.100), channel_id=1, source_target_pairs={{0,3},{1,0},{2,1},{3,2},{4,7},{5,4},{6,5},{7,6},{8,11},{9,8},{10,9... | collective-permute-start | bytes 786440 | tf_op jit(solution)/shard_map/ppermute | solution.py:421
  45.7 0.8 collective-permute-start.1
  46.5 0.9 collective-permute-start
  48.0 8.7 %collective-permute-done.2.hub3 = bf16[64,16,128]{2,1,0:T(8,128)(2,1)S(1)} collective-permute-done((bf16[64,16,128]{2,1,0:T(8,128)(2,1)S(1)}, bf16[64,16,128]{2,1,0:T(8,128)(2,1)S(1)}, u32[]{:S(2)}, u32[]{:S(2)}) %collective-permute-start.2) | collective-permute-done | bytes 262176 | tf_op jit(solution)/shard_map/ppermute | solution.py:421
  56.7 0.0 collective-permute-done.1.hub2
  56.7 3.7 %collective-permute-done.hub1 = bf16[64,16,128]{2,1,0:T(8,128)(2,1)S(1)} collective-permute-done((bf16[64,16,128]{2,1,0:T(8,128)(2,1)S(1)}, bf16[64,16,128]{2,1,0:T(8,128)(2,1)S(1)}, u32[]{:S(2)}, u32[]{:S(2)}) %collective-permute-start) | collective-permute-done | bytes 262176 | tf_op jit(solution)/shard_map/ppermute | solution.py:421
  60.4 0.0 copy-done.4
  60.4 0.0 copy-done.9
  60.4 0.0 copy-done.10
  60.4 0.0 copy-start
  60.5 2.2 %copy-done = bf16[128,128,128]{2,1,0:T(8,128)(2,1)S(1)} copy-done((bf16[128,128,128]{2,1,0:T(8,128)(2,1)S(1)}, bf16[128,128,128]{2,1,0:T(8,128)(2,1)}, u32[]{:S(2)}) %copy-start) | copy-done | bytes 4194328
  62.6 13.2 %forward.1 = (bf16[4096,256]{1,0:T(8,128)(2,1)}, bf16[4096,128]{1,0:T(8,128)(2,1)S(1)}, f32[4096,128]{1,0:T(8,128)S(1)}, f32[512,128]{1,0:T(8,128)}) custom-call(s32[128]{0:T(128)S(1)} %copy-done.11, s32[128]{0:T(128)S(1)} %copy-done.12, s32[1]{0:T(128)S(6)} %copy.23.count, bf16[128,128,128]{2,1,0:T(8,128)(2,1)S(1)} %copy-done, ...), custom_call_target="tpu_custom_call" | custom-call | tf_op jit(solution)/shard_map/forward/pallas_call | solution.py:212
  75.8 0.0 copy-start.5
  75.8 1.3 copy-done.5
  77.2 11.5 %all-to-all-start.1 = ((f32[64,8,128]{2,1,0:T(8,128)}), f32[64,8,128]{2,1,0:T(8,128)}, u32[]{:S(2)}, u32[]{:S(2)}) async-start(f32[64,8,128]{2,1,0:T(8,128)} %bitcast), calls=%async_computation.1 | async-start | bytes 524288 | tf_op jit(solution)/shard_map/all_to_all | solution.py:450
  88.6 0.0 copy-start.1
  88.7 2.2 %copy-done.1 = bf16[128,128,128]{2,1,0:T(8,128)(2,1)S(1)} copy-done((bf16[128,128,128]{2,1,0:T(8,128)(2,1)S(1)}, bf16[128,128,128]{2,1,0:T(8,128)(2,1)}, u32[]{:S(2)}) %copy-start.1) | copy-done | bytes 4194328
  90.8 1.6 copy-done.6
  92.4 4.2 %backward.1 = (f32[4096,128]{1,0:T(8,128)S(1)}, bf16[64,32,128]{2,1,0:T(8,128)(2,1)S(1)}, bf16[65,16,128]{2,1,0:T(8,128)(2,1)S(1)}, bf16[65,16,128]{2,1,0:T(8,12...) custom-call(s32[128]{0:T(128)S(1)} %copy-done.11, s32[128]{0:T(128)S(1)} %copy-done.12, ...), custom_call_target="tpu_custom_call" | custom-call | tf_op jit(solution)/shard_map/backward/pallas_call | solution.py:308
  96.7 0.0 copy-start.7
  96.7 0.8 copy-done.7
  97.5 0.7 copy-done.17
  98.2 0.7 copy-done.18
  98.9 0.7 copy-done.19
  99.6 0.7 all-to-all-done.1
  100.3 1.0 reduce_sum.9
  101.3 0.6 constant_dynamic-update-slice_fusion
  102.0 0.8 collective-permute-start.5
  102.7 1.3 collective-permute-start.3
  104.0 5.0 %collective-permute-start.4 = (bf16[65,16,128]{2,1,0:T(8,128)(2,1)}, bf16[65,16,128]{2,1,0:T(8,128)(2,1)S(1)}, u32[]{:S(2)}, u32[]{:S(2)}) collective-permute-start(bf16[65,16,128]{2,1,0:T(8,128)(2,1)} %get-tuple-element.82), channel_id=1, source_target_pairs={{0,2},{1,3},{2,0},{3,1},{4,6},{5,7},{6,4},{7,5},{8,10},{9,11},{10,... | collective-permute-start | bytes 798728 | tf_op jit(solution)/shard_map/ppermute | solution.py:421
  109.0 2.5 %collective-permute-done.5.hub3 = bf16[65,16,128]{2,1,0:T(8,128)(2,1)S(1)} collective-permute-done((bf16[65,16,128]{2,1,0:T(8,128)(2,1)}, bf16[65,16,128]{2,1,0:T(8,128)(2,1)S(1)}, u32[]{:S(2)}, u32[]{:S(2)}) %collective-permute-start.5) | collective-permute-done | bytes 266272 | tf_op jit(solution)/shard_map/ppermute | solution.py:421
  111.4 8.7 %collective-permute-done.3.hub1 = bf16[65,16,128]{2,1,0:T(8,128)(2,1)S(1)} collective-permute-done((bf16[65,16,128]{2,1,0:T(8,128)(2,1)}, bf16[65,16,128]{2,1,0:T(8,128)(2,1)S(1)}, u32[]{:S(2)}, u32[]{:S(2)}) %collective-permute-start.3) | collective-permute-done | bytes 266272 | tf_op jit(solution)/shard_map/ppermute | solution.py:421
  120.1 0.0 collective-permute-done.4.hub2
  120.1 1.0 copy-done.8
  121.2 1.5 merge.1
  122.7 11.5 %all-to-all-start.2 = ((bf16[64,64,128]{2,1,0:T(8,128)(2,1)}), bf16[64,64,128]{2,1,0:T(8,128)(2,1)S(1)}, u32[]{:S(2)}, u32[]{:S(2)}) async-start(bf16[64,64,128]{2,1,0:T(8,128)(2,1)} %merge.1), calls=%async_computation.2 | async-start | bytes 2097152 | tf_op jit(solution)/shard_map/all_to_all | solution.py:464
  134.2 0.1 copy.18
  134.3 0.1 reshape.119.refs_1_
  134.4 27.7 %all-to-all-done.2.refs_2_ = bf16[64,64,128]{2,1,0:T(8,128)(2,1)S(1)} async-done(((bf16[64,64,128]{2,1,0:T(8,128)(2,1)}), bf16[64,64,128]{2,1,0:T(8,128)(2,1)S(1)}, u32[]{:S(2)}, u32[]{:S(2)}) %all-to-all-start.2) | async-done | bytes 1048608 | tf_op jit(solution)/shard_map/all_to_all | solution.py:464
  162.0 0.0 copy-done.16
  162.0 9.2 %finish.1 = (f32[4096,128]{1,0:T(8,128)}, f32[512,128]{1,0:T(8,128)S(1)}) custom-call(s32[16]{0:T(128)S(1)} %copy-done.16, s32[1,2048]{1,0:T(1,128)S(1)} %reshape.119.refs_1_, bf16[64,64,128]{2,1,0:T(8,128)(2,1)S(1)} %all-to-all-done.2.refs_2_, f32[4096,128]{1,0:T(8,128)S(1)} %get-tuple-element.73.refs_3_), custom_call_target="tpu_custom_call" | custom-call | tf_op jit(solution)/shard_map/finish/pallas_call | solution.py:406
  171.2 0.7 pad_maximum_fusion
  (26 shorter events, 0.1 us)
Async XLA Ops:
  0.6 59.8 %copy-start.12 = (s32[128]{0:T(128)S(1)}, s32[128]{0:T(128)}, u32[]{:S(2)}) copy-start(s32[128]{0:T(128)} %sources.3) | copy-start | bytes 1540
  0.6 59.8 %copy-start.11 = (s32[128]{0:T(128)S(1)}, s32[128]{0:T(128)}, u32[]{:S(2)}) copy-start(s32[128]{0:T(128)} %targets.3) | copy-start | bytes 1540
  1.5 1.2 copy-start.2
  2.7 0.7 copy-start.13
  3.3 0.7 copy-start.15
  4.0 56.4 %copy-start.3 = (bf16[4096,128]{1,0:T(8,128)(2,1)S(1)}, bf16[4096,128]{1,0:T(8,128)(2,1)}, u32[]{:S(2)}) copy-start(bf16[4096,128]{1,0:T(8,128)(2,1)} %features.3) | copy-start | bytes 3145732
  4.0 56.4 %copy-start.4 = (bf16[4096,256]{1,0:T(8,128)(2,1)S(1)}, bf16[4096,256]{1,0:T(8,128)(2,1)}, u32[]{:S(2)}) copy-start(bf16[4096,256]{1,0:T(8,128)(2,1)} %out_grad.1) | copy-start | bytes 6291460
  4.0 56.4 %copy-start.9 = (bf16[128,256]{1,0:T(8,128)(2,1)S(1)}, bf16[128,256]{1,0:T(8,128)(2,1)}, u32[]{:S(2)}) copy-start(bf16[128,256]{1,0:T(8,128)(2,1)} %w_self.1) | copy-start | bytes 196612
  4.0 56.4 %copy-start.10 = (bf16[128,256]{1,0:T(8,128)(2,1)S(1)}, bf16[128,256]{1,0:T(8,128)(2,1)}, u32[]{:S(2)}) copy-start(bf16[128,256]{1,0:T(8,128)(2,1)} %w_nbr.1) | copy-start | bytes 196612
  42.9 13.9 %collective-permute-start.2 = (bf16[64,16,128]{2,1,0:T(8,128)(2,1)S(1)}, bf16[64,16,128]{2,1,0:T(8,128)(2,1)S(1)}, u32[]{:S(2)}, u32[]{:S(2)}) collective-permute-start(bf16[64,16,128]{2,1,0:T(8,128)(2,1)S(1)} %slice.100), channel_id=1, source_target_pairs={{0,3},{1,0},{2,1},{3,2},{4,7},{5,4},{6,5},{7,6},{8,11},{9,8},{10,9... | collective-permute-start | bytes 786440 | tf_op jit(solution)/shard_map/ppermute | solution.py:421
  45.7 11.0 %collective-permute-start.1 = (bf16[64,16,128]{2,1,0:T(8,128)(2,1)S(1)}, bf16[64,16,128]{2,1,0:T(8,128)(2,1)S(1)}, u32[]{:S(2)}, u32[]{:S(2)}) collective-permute-start(bf16[64,16,128]{2,1,0:T(8,128)(2,1)S(1)} %slice.100), channel_id=1, source_target_pairs={{0,2},{1,3},{2,0},{3,1},{4,6},{5,7},{6,4},{7,5},{8,10},{9,11},{10,... | collective-permute-start | bytes 786440 | tf_op jit(solution)/shard_map/ppermute | solution.py:421
  46.5 13.9 %collective-permute-start = (bf16[64,16,128]{2,1,0:T(8,128)(2,1)S(1)}, bf16[64,16,128]{2,1,0:T(8,128)(2,1)S(1)}, u32[]{:S(2)}, u32[]{:S(2)}) collective-permute-start(bf16[64,16,128]{2,1,0:T(8,128)(2,1)S(1)} %slice.100), channel_id=1, source_target_pairs={{0,1},{1,2},{2,3},{3,0},{4,5},{5,6},{6,7},{7,4},{8,9},{9,10},{10,1... | collective-permute-start | bytes 786440 | tf_op jit(solution)/shard_map/ppermute | solution.py:421
  60.4 2.2 %copy-start = (bf16[128,128,128]{2,1,0:T(8,128)(2,1)S(1)}, bf16[128,128,128]{2,1,0:T(8,128)(2,1)}, u32[]{:S(2)}) copy-start(bf16[128,128,128]{2,1,0:T(8,128)(2,1)} %weights.3) | copy-start | bytes 12582916
  75.8 1.3 copy-start.5
  77.2 23.2 %all-to-all-start.1 = ((f32[64,8,128]{2,1,0:T(8,128)}), f32[64,8,128]{2,1,0:T(8,128)}, u32[]{:S(2)}, u32[]{:S(2)}) async-start(f32[64,8,128]{2,1,0:T(8,128)} %bitcast), calls=%async_computation.1 | async-start | bytes 524288 | tf_op jit(solution)/shard_map/all_to_all | solution.py:450
  88.6 2.2 %copy-start.1 = (bf16[128,128,128]{2,1,0:T(8,128)(2,1)S(1)}, bf16[128,128,128]{2,1,0:T(8,128)(2,1)}, u32[]{:S(2)}) copy-start(bf16[128,128,128]{2,1,0:T(8,128)(2,1)} %weights.3) | copy-start | bytes 12582916
  90.8 1.6 copy-start.6
  96.7 0.8 copy-start.7
  97.5 0.7 copy-start.17
  98.2 0.7 copy-start.18
  98.9 0.7 copy-start.19
  102.0 9.5 %collective-permute-start.5 = (bf16[65,16,128]{2,1,0:T(8,128)(2,1)}, bf16[65,16,128]{2,1,0:T(8,128)(2,1)S(1)}, u32[]{:S(2)}, u32[]{:S(2)}) collective-permute-start(bf16[65,16,128]{2,1,0:T(8,128)(2,1)} %get-tuple-element.80), channel_id=1, source_target_pairs={{0,3},{1,0},{2,1},{3,2},{4,7},{5,4},{6,5},{7,6},{8,11},{9,8},{10,9... | collective-permute-start | bytes 798728 | tf_op jit(solution)/shard_map/ppermute | solution.py:421
  102.7 17.4 %collective-permute-start.3 = (bf16[65,16,128]{2,1,0:T(8,128)(2,1)}, bf16[65,16,128]{2,1,0:T(8,128)(2,1)S(1)}, u32[]{:S(2)}, u32[]{:S(2)}) collective-permute-start(bf16[65,16,128]{2,1,0:T(8,128)(2,1)} %get-tuple-element.81), channel_id=1, source_target_pairs={{0,1},{1,2},{2,3},{3,0},{4,5},{5,6},{6,7},{7,4},{8,9},{9,10},{10,1... | collective-permute-start | bytes 798728 | tf_op jit(solution)/shard_map/ppermute | solution.py:421
  104.0 16.1 %collective-permute-start.4 = (bf16[65,16,128]{2,1,0:T(8,128)(2,1)}, bf16[65,16,128]{2,1,0:T(8,128)(2,1)S(1)}, u32[]{:S(2)}, u32[]{:S(2)}) collective-permute-start(bf16[65,16,128]{2,1,0:T(8,128)(2,1)} %get-tuple-element.82), channel_id=1, source_target_pairs={{0,2},{1,3},{2,0},{3,1},{4,6},{5,7},{6,4},{7,5},{8,10},{9,11},{10,... | collective-permute-start | bytes 798728 | tf_op jit(solution)/shard_map/ppermute | solution.py:421
  120.1 1.0 copy-start.8
  121.1 13.0 %copy-start.14 = (s32[64]{0:T(128)S(1)}, s32[64]{0:T(128)}, u32[]{:S(2)}) copy-start(s32[64]{0:T(128)} %send_counts.1) | copy-start | bytes 772
  121.1 13.0 %copy-start.20 = (s32[64,32]{0,1:T(8,128)S(1)}, s32[64,32]{0,1:T(8,128)}, u32[]{:S(2)}) copy-start(s32[64,32]{0,1:T(8,128)} %param.24) | copy-start | bytes 24580
  121.1 40.9 %copy-start.16 = (s32[16]{0:T(128)S(1)}, s32[16]{0:T(128)}, u32[]{:S(2)}) copy-start(s32[16]{0:T(128)} %refs_0_.1) | copy-start | bytes 196
  122.7 39.4 %all-to-all-start.2 = ((bf16[64,64,128]{2,1,0:T(8,128)(2,1)}), bf16[64,64,128]{2,1,0:T(8,128)(2,1)S(1)}, u32[]{:S(2)}, u32[]{:S(2)}) async-start(bf16[64,64,128]{2,1,0:T(8,128)(2,1)} %merge.1), calls=%async_computation.2 | async-start | bytes 2097152 | tf_op jit(solution)/shard_map/all_to_all | solution.py:464

commit v2 on v0

v2 whole, which is shorter than its diff:
```python
import math

import jax
import jax.numpy as jnp
from jax import lax
from jax.experimental import pallas as pl
from jax.experimental.pallas import tpu as pltpu
from jax.sharding import Mesh
from jax.sharding import PartitionSpec as P

BF16 = jnp.bfloat16
F32 = jnp.float32
CHUNK = 16
ROWS = 1024
NEAR = 16
WHOLE = 60
REPS = 4
CORES = 2
GROUP = "group"
DOM = ("group", "core")


def smem():
    return pl.BlockSpec(memory_space=pltpu.SMEM)


def vmem():
    return pl.BlockSpec(memory_space=pltpu.VMEM)


def hbm():
    return pl.BlockSpec(memory_space=pl.ANY)


def params(mebibytes):
    return pltpu.CompilerParams(vmem_limit_bytes=mebibytes * 1024 * 1024)


def rows_at(index, size):
    return pl.ds(pl.multiple_of(index * size, size), size)


def hub_pack_kernel(hub_rows, features, out, near, wide, sems):
    hubs = hub_rows.shape[0]
    copies = []
    for h in range(hubs):
        start = pl.multiple_of(hub_rows[h] // NEAR * NEAR, NEAR)
        copies.append(
            pltpu.make_async_copy(
                features.at[pl.ds(start, NEAR)], near.at[pl.ds(h * NEAR, NEAR)], sems.at[h]
            )
        )
        copies[-1].start()
    for copy in copies:
        copy.wait()
    wide[hubs:] = near[...].astype(F32)
    for h in range(hubs):
        row = hubs + h * NEAR + hub_rows[h] % NEAR
        wide[h : h + 1] = wide[pl.ds(row, 1)]
    own_hubs = wide[:hubs].astype(BF16)

    def emit(p, carry):
        out[p] = own_hubs
        return carry

    lax.fori_loop(0, out.shape[0], emit, 0)


def hub_pack(hub_rows, features, peers):
    hubs = hub_rows.shape[0]
    width = features.shape[1]
    return pl.pallas_call(
        hub_pack_kernel,
        out_shape=jax.ShapeDtypeStruct((peers, hubs, width), BF16),
        in_specs=[smem(), hbm()],
        out_specs=vmem(),
        scratch_shapes=[
            pltpu.VMEM((hubs * NEAR, width), BF16),
            pltpu.VMEM((hubs + hubs * NEAR, width), F32),
            pltpu.SemaphoreType.DMA((hubs,)),
        ],
        compiler_params=params(WHOLE),
        name="hub_pack",
    )(hub_rows, features)


def halo_pack_kernel(send_slots, send_counts, features, out, wide, staged):
    slots, peers = send_slots.shape
    wide[...] = features[...].astype(F32)

    def peer(p, carry):
        for k in range(slots):
            staged[pl.ds(p * slots + k, 1)] = wide[pl.ds(send_slots[k, p], 1)]
        return carry

    lax.fori_loop(0, peers, peer, 0)
    slot = lax.broadcasted_iota(jnp.int32, (slots, out.shape[2]), 0)

    def emit(p, carry):
        rows = staged[rows_at(p, slots)]
        out[p] = jnp.where(slot < send_counts[p], rows, 0.0).astype(BF16)
        return carry

    lax.fori_loop(0, peers, emit, 0)


def halo_pack(send_rows, send_counts, features):
    peers, slots = send_rows.shape
    node_rows, width = features.shape
    return pl.pallas_call(
        halo_pack_kernel,
        out_shape=jax.ShapeDtypeStruct((peers, slots, width), BF16),
        in_specs=[smem(), smem(), vmem()],
        out_specs=vmem(),
        scratch_shapes=[
            pltpu.VMEM((node_rows, width), F32),
            pltpu.VMEM((peers * slots, width), F32),
        ],
        compiler_params=params(WHOLE),
        name="halo_pack",
    )(send_rows.T, send_counts, features)


def weight_copy(c, weights, held, sems):
    part = rows_at(c, CHUNK)
    return pltpu.make_async_copy(weights.at[part], held.at[part], sems.at[c])


def start_weights(chunks, weights, held, sems):
    def start(c, carry):
        weight_copy(c, weights, held, sems).start()
        return carry

    lax.fori_loop(0, chunks, start, 0)


def forward_kernel(
    targets,
    sources,
    count,
    weights,
    features,
    halo,
    *refs,
):
    hubs, refs = refs[: REPS * CORES], refs[REPS * CORES :]
    out_grad, w_self, w_nbr, hidden, grad_agg, grad_self, grad_w, *refs = refs
    held, source_rows, totals, w_both, grads_in, grad_total, hidden_all, *refs = refs
    agg_all, self_all, w_all, weight_sems, sems, out_sems = refs
    block = weights.shape[1]
    target_blocks, parts, part_rows, width = features.shape
    hub_blocks = hubs[0].shape[0]
    halo_blocks = halo.shape[0]
    node_rows = target_blocks * block
    rep = lax.axis_index("rep")
    core = lax.axis_index("core")
    pieces = [(features, source_rows.at[pl.ds(0, target_blocks)])]
    for c in range(CORES):
        for i in range(REPS):
            from_core = lax.rem(core + c, CORES)
            from_rep = lax.rem(rep - i + REPS, REPS)
            part = from_core * REPS + from_rep
            pieces.append(
                (hubs[c * REPS + i], source_rows.at[pl.ds(target_blocks, hub_blocks), part])
            )
    pieces.append((halo, source_rows.at[pl.ds(target_blocks + hub_blocks, halo_blocks)]))
    early = [pltpu.make_async_copy(x, y, sems.at[n]) for n, (x, y) in enumerate(pieces)]
    for copy in early:
        copy.start()
    live = count[0]
    chunks = (live + CHUNK - 1) // CHUNK
    start_weights(chunks, weights, held, weight_sems)
    late = [
        pltpu.make_async_copy(x, y, sems.at[len(pieces) + n])
        for n, (x, y) in enumerate(
            (
                (w_self, w_both.at[pl.ds(0, width)]),
                (w_nbr, w_both.at[pl.ds(width, width)]),
                (out_grad, grads_in),
            )
        )
    ]
    for copy in late:
        copy.start()
    ones = jnp.ones((block, width), BF16)

    def product(t):
        picked = source_rows[sources[t]].reshape(block, width)
        return jnp.dot(
            held[t], jnp.concatenate([picked, ones], 1), preferred_element_type=F32
        )

    for copy in early:
        copy.wait()
    leading = target_blocks // CHUNK

    def first(c, carry):
        weight_copy(c, weights, held, weight_sems).wait()
        for u in range(CHUNK):
            totals[c * CHUNK + u] = product(c * CHUNK + u)
        return carry

    lax.fori_loop(0, leading, first, 0)

    def more(c, carry):
        weight_copy(c, weights, held, weight_sems).wait()
        products = [product(c * CHUNK + u) for u in range(CHUNK)]
        for u, value in enumerate(products):
            t = c * CHUNK + u
            target = jnp.where(t < live, targets[t], target_blocks)
            totals[target] += value
        return carry

    lax.fori_loop(leading, chunks, more, 0)
    grad_total[...] = jnp.zeros_like(grad_total)
    per_chunk = ROWS // block
    for copy in late:
        copy.wait()

    def outs(c):
        rows = rows_at(c, ROWS)
        return [
            pltpu.make_async_copy(x.at[rows], y.at[rows], out_sems.at[n])
            for n, (x, y) in enumerate(
                ((hidden_all, hidden), (agg_all, grad_agg), (self_all, grad_self))
            )
        ]

    def dense(c, carry):
        rows = rows_at(c, ROWS)
        blocks_at = pl.ds(c * per_chunk, per_chunk)
        total = totals[blocks_at].reshape(ROWS, 2 * width)
        inverse = 1.0 / jnp.maximum(total[:, width:], 1.0)
        aggregate = (total[:, :width] * inverse).astype(BF16)
        own = source_rows[blocks_at].reshape(ROWS, width)
        both = jnp.concatenate([own, aggregate], 1)
        preact = jnp.dot(both, w_both[...], preferred_element_type=F32)
        sigmoid = 0.5 * jnp.tanh(0.5 * preact) + 0.5
        activated = preact * sigmoid
        hidden_all[rows] = activated.astype(BF16)
        slope = sigmoid + activated * (1.0 - sigmoid)
        grad_preact = (grads_in[rows].astype(F32) * slope).astype(BF16)
        grad_total[...] += lax.dot_general(
            both, grad_preact, (((0,), (0,)), ((), ())), preferred_element_type=F32
        )
        back = lax.dot_general(
            grad_preact, w_both[...], (((1,), (1,)), ((), ())), preferred_element_type=F32
        )
        self_all[rows] = back[:, :width]
        agg_all[rows] = (back[:, width:] * inverse).astype(BF16)
        for copy in outs(c):
            copy.start()
        return carry

    steps = node_rows // ROWS
    lax.fori_loop(0, steps, dense, 0)
    half = grad_total.shape[1] // 2
    w_all[: grad_total.shape[0]] = grad_total[:, :half]
    w_all[grad_total.shape[0] :] = grad_total[:, half:]
    w_copy = pltpu.make_async_copy(w_all, grad_w, sems.at[0])
    w_copy.start()

    def drain(c, carry):
        for copy in outs(c):
            copy.wait()
        return carry

    lax.fori_loop(0, steps, drain, 0)
    w_copy.wait()


def forward(targets, sources, count, weights, features, halo, hubs, out_grad, w_self, w_nbr):
    node_rows, width = features.shape
    tiles, block, _ = weights.shape
    hidden_width = w_self.shape[1]
    parts = REPS * CORES
    part_rows = block // parts
    in_blocks = lambda value: value.reshape(-1, parts, part_rows, width)
    features = in_blocks(features)
    halo = in_blocks(halo)
    source_blocks = features.shape[0] + hubs[0].shape[0] + halo.shape[0]
    shapes = (
        jax.ShapeDtypeStruct((node_rows, hidden_width), BF16),
        jax.ShapeDtypeStruct((node_rows, width), BF16),
        jax.ShapeDtypeStruct((node_rows, width), F32),
        jax.ShapeDtypeStruct((4 * width, hidden_width // 2), F32),
    )
    return pl.pallas_call(
        forward_kernel,
        out_shape=shapes,
        in_specs=[smem()] * 3 + [hbm()] * (6 + parts),
        out_specs=(hbm(),) * 4,
        scratch_shapes=[
            pltpu.VMEM((tiles, block, block), BF16),
            pltpu.VMEM((source_blocks, parts, part_rows, width), BF16),
            pltpu.VMEM((node_rows // block + 1, block, 2 * width), F32),
            pltpu.VMEM((2 * width, hidden_width), BF16),
            pltpu.VMEM((node_rows, hidden_width), BF16),
            pltpu.VMEM((2 * width, hidden_width), F32),
        ]
        + [pltpu.VMEM(shape.shape, shape.dtype) for shape in shapes]
        + [
            pltpu.SemaphoreType.DMA((tiles // CHUNK,)),
            pltpu.SemaphoreType.DMA((5 + parts,)),
            pltpu.SemaphoreType.DMA((3,)),
        ],
        compiler_params=params(WHOLE),
        name="forward",
    )(targets, sources, count, weights, features, halo, *hubs, out_grad, w_self, w_nbr)


def backward_kernel(
    targets,
    sources,
    count,
    weights,
    grad_agg,
    grad_self,
    grad_own,
    halo,
    near,
    far,
    held,
    agg,
    totals,
    weight_sems,
    sems,
):
    block = weights.shape[1]
    node_rows, width = grad_agg.shape
    peers, slots, _ = halo.shape
    _, groups, hubs, _ = near.shape
    agg_copy = pltpu.make_async_copy(grad_agg, agg, sems.at[0])
    self_copy = pltpu.make_async_copy(grad_self, totals.at[pl.ds(0, node_rows)], sems.at[1])
    agg_copy.start()
    self_copy.start()
    live = count[0]
    chunks = (live + CHUNK - 1) // CHUNK
    start_weights(chunks, weights, held, weight_sems)
    rep = lax.axis_index("rep")
    core = lax.axis_index("core")
    totals[node_rows:] = jnp.zeros((totals.shape[0] - node_rows, width), F32)
    spare = totals.shape[0] // block - 1
    agg_copy.wait()
    self_copy.wait()

    def step(c, carry):
        weight_copy(c, weights, held, weight_sems).wait()
        products = [
            lax.dot_general(
                held[c * CHUNK + u],
                agg[rows_at(targets[c * CHUNK + u], block)],
                (((0,), (0,)), ((), ())),
                preferred_element_type=F32,
            )
            for u in range(CHUNK)
        ]
        for u, value in enumerate(products):
            t = c * CHUNK + u
            source = jnp.where(t < live, sources[t], spare)
            totals[rows_at(source, block)] += value
        return carry

    lax.fori_loop(0, chunks, step, 0)
    own_copy = pltpu.make_async_copy(totals.at[pl.ds(0, node_rows)], grad_own, sems.at[0])
    own_copy.start()
    hub_base = node_rows
    halo_base = hub_base + groups * CORES * REPS * hubs

    def emit_halo(p, carry):
        at = pl.multiple_of(halo_base + p * slots, slots)
        halo[p] = totals[pl.ds(at, slots)].astype(BF16)
        return carry

    lax.fori_loop(0, peers, emit_halo, 0)

    def emit_hub(p, carry):
        for c, piece in enumerate((near, far)):
            to_core = lax.rem(core + c, CORES)
            for i in range(REPS):
                to_rep = lax.rem(rep + i, REPS)
                part = (p * CORES + to_core) * REPS + to_rep
                at = pl.multiple_of(hub_base + part * hubs, hubs)
                piece[i, p] = totals[pl.ds(at, hubs)].astype(BF16)
        return carry

    lax.fori_loop(0, groups, emit_hub, 0)
    own_copy.wait()


def backward(targets, sources, count, weights, grad_agg, grad_self, peers, slots, hubs):
    node_rows, width = grad_agg.shape
    tiles, block, _ = weights.shape
    groups = peers // CORES
    total_rows = node_rows + peers * REPS * hubs + peers * slots + block
    piece = jax.ShapeDtypeStruct((REPS, groups, hubs, width), BF16)
    return pl.pallas_call(
        backward_kernel,
        out_shape=(
            jax.ShapeDtypeStruct((node_rows, width), F32),
            jax.ShapeDtypeStruct((peers, slots, width), BF16),
            piece,
            piece,
        ),
        in_specs=[smem()] * 3 + [hbm()] * 3,
        out_specs=(hbm(), vmem(), vmem(), vmem()),
        scratch_shapes=[
            pltpu.VMEM((tiles, block, block), BF16),
            pltpu.VMEM((node_rows, width), BF16),
            pltpu.VMEM((total_rows, width), F32),
            pltpu.SemaphoreType.DMA((tiles // CHUNK,)),
            pltpu.SemaphoreType.DMA((2,)),
        ],
        compiler_params=params(WHOLE),
        name="backward",
    )(targets, sources, count, weights, grad_agg, grad_self)


def split_pair(total):
    high = total.astype(BF16)
    return high, (total - high.astype(F32)).astype(BF16)


def fold_kernel(slices, out):
    def peer(p, total):
        return total + slices[p]

    total = lax.fori_loop(0, slices.shape[0], peer, jnp.zeros(slices.shape[1:], F32))
    out[0], out[1] = split_pair(total)


def fold(slices):
    return pl.pallas_call(
        fold_kernel,
        out_shape=jax.ShapeDtypeStruct((2, *slices.shape[1:]), BF16),
        in_specs=[vmem()],
        out_specs=vmem(),
        compiler_params=params(8),
        name="fold",
    )(slices)


def join_kernel(near, far, w_near, w_far, *outs):
    groups = near.shape[1]
    total = (w_near[0].astype(F32) + w_near[1].astype(F32)) + (
        w_far[0].astype(F32) + w_far[1].astype(F32)
    )
    high, low = split_pair(total)
    for out in outs:
        out[groups] = high
        out[groups + 1] = low

    def group(p, carry):
        for i, out in enumerate(outs):
            out[p] = (near[i, p].astype(F32) + far[i, p].astype(F32)).astype(BF16)
        return carry

    lax.fori_loop(0, groups, group, 0)


def join(near, far, w_near, w_far):
    reps, groups, hubs, width = near.shape
    piece = jax.ShapeDtypeStruct((groups + 2, hubs, width), BF16)
    return pl.pallas_call(
        join_kernel,
        out_shape=(piece,) * reps,
        in_specs=[vmem()] * 4,
        out_specs=(vmem(),) * reps,
        compiler_params=params(8),
        name="join",
    )(near, far, w_near, w_far)


def merge_kernel(hub0, hub1, hub2, hub3, out, w_parts):
    groups, message, width = out.shape
    hubs = hub0.shape[1]
    rep = lax.axis_index("rep")
    for i, piece in enumerate((hub0, hub1, hub2, hub3)):
        w_parts[lax.rem(rep - i + REPS, REPS)] = piece[groups].astype(F32) + piece[
            groups + 1
        ].astype(F32)
    w_total = (((w_parts[0] + w_parts[1]) + w_parts[2]) + w_parts[3]).astype(BF16)

    def group(p, carry):
        total = (hub0[p].astype(F32) + hub1[p].astype(F32)) + (
            hub2[p].astype(F32) + hub3[p].astype(F32)
        )
        out[p, :hubs] = total.astype(BF16)
        out[p, hubs:] = w_total
        return carry

    lax.fori_loop(0, groups, group, 0)


def merge(pieces):
    groups, hubs, width = pieces[0].shape
    return pl.pallas_call(
        merge_kernel,
        out_shape=jax.ShapeDtypeStruct((groups - 2, 2 * hubs, width), BF16),
        in_specs=[vmem()] * 4,
        out_specs=vmem(),
        scratch_shapes=[pltpu.VMEM((REPS, hubs, width), F32)],
        compiler_params=params(8),
        name="merge",
    )(*pieces)


def scatter_kernel(send_ids, received, grad_own, out):
    peers, slots, width = received.shape
    rows = received[...].reshape(peers * slots, width)

    def scatter(c, carry):
        at = rows_at(c, ROWS)
        ids = lax.broadcasted_iota(jnp.int32, (ROWS, peers * slots), 0) + c * ROWS
        hot = (ids == send_ids[...]).astype(F32).astype(BF16)
        out[at] = grad_own[at] + jnp.dot(hot, rows, preferred_element_type=F32)
        return carry

    lax.fori_loop(0, out.shape[0] // ROWS, scatter, 0)


def scatter(send_ids, received, grad_own):
    return pl.pallas_call(
        scatter_kernel,
        out_shape=jax.ShapeDtypeStruct(grad_own.shape, F32),
        in_specs=[vmem()] * 3,
        out_specs=vmem(),
        compiler_params=params(32),
        name="scatter",
    )(send_ids, received, grad_own)


def finish(hub_rows, received, grad_nodes, hidden_width, grad_scale):
    peers, message, width = received.shape
    hubs = hub_rows.shape[0]
    half = message - hubs

    def body(hub_rows, received, grad_nodes, out, grad_self, grad_nbr, held):
        out[...] = grad_nodes[...]

        def place(p, total):
            held[rows_at(p, half)] = received[p, hubs:].astype(F32) * grad_scale
            return total + received[p, :hubs].astype(F32)

        total = lax.fori_loop(0, peers, place, jnp.zeros((hubs, width), F32))
        for h in range(hubs):
            out[pl.ds(hub_rows[h], 1)] += total[h : h + 1]
        for k in range(hidden_width // width):
            columns = pl.ds(k * width, width)
            grad_self[:, columns] = held[2 * k * width : (2 * k + 1) * width]
            grad_nbr[:, columns] = held[(2 * k + 1) * width : (2 * k + 2) * width]

    return pl.pallas_call(
        body,
        out_shape=(
            jax.ShapeDtypeStruct(grad_nodes.shape, F32),
            jax.ShapeDtypeStruct((width, hidden_width), F32),
            jax.ShapeDtypeStruct((width, hidden_width), F32),
        ),
        in_specs=[smem()] + [vmem()] * 2,
        out_specs=(vmem(),) * 3,
        scratch_shapes=[pltpu.VMEM((peers * half, width), F32)],
        compiler_params=params(24),
        name="finish",
    )(hub_rows, received, grad_nodes)


def rep_shift(value, shift):
    return lax.ppermute(value, "rep", [(j, (j + shift) % REPS) for j in range(REPS)])


def core_swap(value):
    return lax.ppermute(value, "core", [(0, 1), (1, 0)])


def swap(value, axes):
    return lax.all_to_all(value, axes, split_axis=0, concat_axis=0, tiled=True)


def shards(
    features,
    out_grad,
    w_self,
    w_nbr,
    hub_rows,
    send_rows,
    send_counts,
    tile_targets,
    tile_sources,
    tile_count,
    tile_weights,
):
    node_rows, width = features.shape
    peers, slots = send_rows.shape
    hubs = hub_rows.shape[0]
    groups = peers // CORES
    own_rep = swap(hub_pack(hub_rows, features, groups), GROUP)
    halo = swap(halo_pack(send_rows, send_counts, features), DOM)
    near = [own_rep] + [rep_shift(own_rep, i) for i in range(1, REPS)]
    far = [core_swap(piece) for piece in near]
    hidden, grad_agg, grad_self, grad_w = forward(
        tile_targets, tile_sources, tile_count, tile_weights, features, halo, near + far,
        out_grad, w_self, w_nbr,
    )
    w_slices = swap(grad_w.reshape(groups, -1, width), GROUP)
    grad_own, grad_halo, near, far = backward(
        tile_targets, tile_sources, tile_count, tile_weights, grad_agg, grad_self, peers, slots, hubs
    )
    returned = swap(grad_halo, DOM)
    w_pair = fold(w_slices)
    pieces = join(near, core_swap(far), w_pair, core_swap(w_pair))
    pieces = [pieces[0]] + [rep_shift(pieces[i], i) for i in range(1, REPS)]
    merged = swap(merge(pieces), GROUP)
    slot_live = jnp.arange(slots, dtype=jnp.int32)[None, :] < send_counts[:, None]
    send_ids = jnp.where(slot_live, send_rows, node_rows).reshape(1, -1)
    grad_nodes = scatter(send_ids, returned, grad_own)
    grad_scale = 1.0 / math.sqrt(node_rows * peers * REPS)
    grad_features, grad_w_self, grad_w_nbr = finish(
        hub_rows, merged, grad_nodes, w_self.shape[1], grad_scale
    )
    return (hidden, grad_features, grad_w_self, grad_w_nbr)


def solution(mesh):
    fine = Mesh(mesh.devices.reshape(-1, CORES, REPS), ("group", "core", "rep"))
    every = ("group", "core", "rep")
    return jax.shard_map(
        shards,
        mesh=fine,
        in_specs=(
            P(every, None),
            P(every, None),
            P(),
            P(),
            P(every),
            P(every, None),
            P(every),
            P(every),
            P(every),
            P(every),
            P(every, None, None),
        ),
        out_specs=(P(every, None), P(every, None), P(), P()),
        check_vma=False,
    )
```

time: 1740 us -> 122 us (0.07)
  waiting for transfers between devices: 1550 us -> 34.4 us
  local copies, waits for them, and re-layouts: 52.2 us -> 3.57 us
  matrix products: 45.3 us -> 0 us
  other arithmetic: 40.2 us -> 0.01 us
  Pallas kernels: 0 us -> 34.8 us
  starting transfers between devices: 20.4 us -> 46.3 us
    reduce_scatter x1 -> x0, waiting for transfers between devices: 1250 us -> none  [shards(): lax.psum_scatter(hub_term, ('dom', 'rep'), scatter_dimension=0, tiled=True)]
    psum x1 -> x0, waiting for transfers between devices: 227 us -> none  [shards(): self_sum, nbr_sum = lax.psum((self_term, nbr_term), ('dom', 'rep'))]
    all_gather x1 -> x0, waiting for transfers between devices: 66.6 us -> none  [shards(): hub_feats = lax.all_gather(own_hubs, ('dom', 'rep'), axis=0, tiled=True)]
    dot_general x11 -> x0, matrix products: 45.3 us -> none  [the longest x1 9.91 us: shards(): jnp.einsum('tij,tjf->tif', tile_weights, picked, preferred_element_type=j...]
    pallas_call x0 -> x9, Pallas kernels: none -> 34.8 us  [the longest x1 10.2 us: forward(): pl.pallas_call(forward_kernel, out_shape=shapes, in_specs=[smem()] * 3 +...]
    dot_general x3 -> x0, local copies, waits for them, and re-layouts: 19.8 us -> none  [the longest x1 9.27 us: shards(): jnp.einsum('tij,tjf->tif', tile_weights, picked, preferred_element_type=j...]
    all_to_all x2 -> x5, starting transfers between devices: 20.3 us -> 35.3 us  [swap(): return lax.all_to_all(value, axes, split_axis=0, concat_axis=0, tiled=True)]
  transfers between devices with their start and end apart: 5 -> 17, of which waited for: 4 -> 13; matrix products, arithmetic and copies ran while one was open for 2% -> 0% of each run, Pallas kernels for 0% -> 16%
where the time goes in v2:
time: 122 us; the launch traced here: 121 us
  starting transfers between devices  46.3 us (38%)
  Pallas kernels  34.8 us (29%)
  waiting for transfers between devices  34.4 us (28%)
  local copies, waits for them, and re-layouts  3.57 us (3%)
  between operations  1.58 us (1%)
    all_to_all x5, starting transfers between devices, swap(): return lax.all_to_all(value, axes, split_axis=0, concat_axis=0, tiled=True)  35.3 us
    all_to_all x5, waiting for transfers between devices, swap(): return lax.all_to_all(value, axes, split_axis=0, concat_axis=0, tiled=True)  19.7 us
    ppermute x6, waiting for transfers between devices, rep_shift(): lax.ppermute(value, 'rep', [(j, (j + shift) % REPS) for j in range(REPS)])  12.8 us
    pallas_call x1, Pallas kernels, forward(): pl.pallas_call(forward_kernel, out_shape=shapes, in_specs=[smem()] * 3 +...  10.2 us
    ppermute x6, starting transfers between devices, rep_shift(): lax.ppermute(value, 'rep', [(j, (j + shift) % REPS) for j in range(REPS)])  10.2 us
    pallas_call x1, Pallas kernels, backward(): pl.pallas_call(backward_kernel, out_shape=(jax.ShapeDtypeStruct((node_row...  8.03 us
    pallas_call x1, Pallas kernels, scatter(): pl.pallas_call(scatter_kernel, out_shape=jax.ShapeDtypeStruct(grad_own.sh...  5.1 us
    pallas_call x1, Pallas kernels, halo_pack(): pl.pallas_call(halo_pack_kernel, out_shape=jax.ShapeDtypeStruct((peers, s...  5.1 us
  transfers between devices with their start and end apart: 17, of which 13 were waited for; matrix products, arithmetic and copies ran while one was open for 0% of the time, Pallas kernels for 16%

profile of v2, /device:TPU:32, one launch (start us, length us, event | category | flops | bytes accessed | tf_op | source)
XLA Modules:
  0.0 120.6 jit_solution(2755061302156459360)
XLA Ops:
  0.6 2.6 %hub_pack.1 = bf16[32,16,128]{2,1,0:T(8,128)(2,1)} custom-call(s32[16]{0:T(128)} %hub_rows.3, bf16[4096,128]{1,0:T(8,128)(2,1)} %features.3), custom_call_target="tpu_custom_call" | custom-call | tf_op jit(solution)/shard_map/hub_pack/pallas_call | solution.py:72
  3.2 11.4 %all-to-all-start.1 = ((bf16[32,16,128]{2,1,0:T(8,128)(2,1)}), bf16[32,16,128]{2,1,0:T(8,128)(2,1)S(1)}, u32[]{:S(2)}, u32[]{:S(2)}) async-start(bf16[32,16,128]{2,1,0:T(8,128)(2,1)} %hub_pack.1), calls=%async_computation.1 | async-start | bytes 262144 | tf_op jit(solution)/shard_map/all_to_all | solution.py:577
  14.6 5.1 %halo_pack.1 = bf16[64,32,128]{2,1,0:T(8,128)(2,1)} custom-call(s32[32,64]{1,0:T(8,128)} %bitcast.7, s32[64]{0:T(128)} %send_counts.1, bf16[4096,128]{1,0:T(8,128)(2,1)} %features.3), custom_call_target="tpu_custom_call" | custom-call | tf_op jit(solution)/shard_map/halo_pack/pallas_call | solution.py:110
  19.7 4.7 %all-to-all-done.1.refs_0_ = bf16[32,16,128]{2,1,0:T(8,128)(2,1)S(1)} async-done(((bf16[32,16,128]{2,1,0:T(8,128)(2,1)}), bf16[32,16,128]{2,1,0:T(8,128)(2,1)S(1)}, u32[]{:S(2)}, u32[]{:S(2)}) %all-to-all-start.1) | async-done | bytes 131104 | tf_op jit(solution)/shard_map/all_to_all | solution.py:577
  24.4 5.5 %all-to-all-start = ((bf16[64,32,128]{2,1,0:T(8,128)(2,1)}), bf16[64,32,128]{2,1,0:T(8,128)(2,1)S(1)}, u32[]{:S(2)}, u32[]{:S(2)}) async-start(bf16[64,32,128]{2,1,0:T(8,128)(2,1)} %halo_pack.1), calls=%async_computation | async-start | bytes 1048576 | tf_op jit(solution)/shard_map/all_to_all | solution.py:577
  29.9 2.8 %collective-permute-start.2 = (bf16[32,16,128]{2,1,0:T(8,128)(2,1)S(1)}, bf16[32,16,128]{2,1,0:T(8,128)(2,1)S(1)}, u32[]{:S(2)}, u32[]{:S(2)}) collective-permute-start(bf16[32,16,128]{2,1,0:T(8,128)(2,1)S(1)} %all-to-all-done.1.refs_0_), channel_id=1, source_target_pairs={{0,3},{1,0},{2,1},{3,2},{4,7},{5,4},{6,5},{7,6},{8,11},{9,8},{10,9... | collective-permute-start | bytes 393224 | tf_op jit(solution)/shard_map/ppermute | solution.py:569
  32.8 0.8 collective-permute-start.1
  33.6 0.9 collective-permute-start
  34.4 4.2 %collective-permute-done.2.refs_3_ = bf16[32,16,128]{2,1,0:T(8,128)(2,1)S(1)} collective-permute-done((bf16[32,16,128]{2,1,0:T(8,128)(2,1)S(1)}, bf16[32,16,128]{2,1,0:T(8,128)(2,1)S(1)}, u32[]{:S(2)}, u32[]{:S(2)}) %collective-permute-start.2) | collective-permute-done | bytes 131104 | tf_op jit(solution)/shard_map/ppermute | solution.py:569
  38.7 0.0 collective-permute-start.6
  38.7 2.0 %collective-permute-done.1.refs_2_ = bf16[32,16,128]{2,1,0:T(8,128)(2,1)S(1)} collective-permute-done((bf16[32,16,128]{2,1,0:T(8,128)(2,1)S(1)}, bf16[32,16,128]{2,1,0:T(8,128)(2,1)S(1)}, u32[]{:S(2)}, u32[]{:S(2)}) %collective-permute-start.1) | collective-permute-done | bytes 131104 | tf_op jit(solution)/shard_map/ppermute | solution.py:569
  40.6 0.0 collective-permute-start.5
  40.6 1.7 %collective-permute-done.refs_1_ = bf16[32,16,128]{2,1,0:T(8,128)(2,1)S(1)} collective-permute-done((bf16[32,16,128]{2,1,0:T(8,128)(2,1)S(1)}, bf16[32,16,128]{2,1,0:T(8,128)(2,1)S(1)}, u32[]{:S(2)}, u32[]{:S(2)}) %collective-permute-start) | collective-permute-done | bytes 131104 | tf_op jit(solution)/shard_map/ppermute | solution.py:569
  42.3 0.0 collective-permute-start.4
  43.1 0.0 collective-permute-done.6.refs_7_
  43.1 0.0 collective-permute-done.5.refs_6_
  43.1 0.6 collective-permute-done.4.refs_5_
  43.7 3.3 %all-to-all-done = bf16[64,32,128]{2,1,0:T(8,128)(2,1)S(1)} async-done(((bf16[64,32,128]{2,1,0:T(8,128)(2,1)}), bf16[64,32,128]{2,1,0:T(8,128)(2,1)S(1)}, u32[]{:S(2)}, u32[]{:S(2)}) %all-to-all-start) | async-done | bytes 524320 | tf_op jit(solution)/shard_map/all_to_all | solution.py:577
  47.1 0.7 copy-done.3
  47.8 10.2 %forward.1 = (bf16[4096,256]{1,0:T(8,128)(2,1)}, bf16[4096,128]{1,0:T(8,128)(2,1)}, f32[4096,128]{1,0:T(8,128)}, f32[512,128]{1,0:T(8,128)}) custom-call(s32[128]{0:T(128)} %targets.3, s32[128]{0:T(128)} %sources.3, s32[1]{0:T(128)S(6)} %copy.17.count, bf16[128,128,128]{2,1,0:T(8,128)(2,1)} %weights.3, bf16[32,8,16,128]{3,2,1,0:T(8,128)(2,1)} %bitcast.4, ...), custom_call_target="tpu_custom_call" | custom-call | tf_op jit(solution)/shard_map/forward/pallas_call | solution.py:288
  58.0 5.3 %all-to-all-start.2 = ((f32[32,16,128]{2,1,0:T(8,128)}), f32[32,16,128]{2,1,0:T(8,128)S(1)}, u32[]{:S(2)}, u32[]{:S(2)}) async-start(f32[32,16,128]{2,1,0:T(8,128)} %bitcast.6), calls=%async_computation.2 | async-start | bytes 524288 | tf_op jit(solution)/shard_map/all_to_all | solution.py:577
  63.4 8.0 %backward.1 = (f32[4096,128]{1,0:T(8,128)}, bf16[64,32,128]{2,1,0:T(8,128)(2,1)}, bf16[4,32,16,128]{3,2,1,0:T(8,128)(2,1)}, bf16[4,32,16,128]{3,2,1,0:T(8,128)(2,1)}) custom-call(s32[128]{0:T(128)} %targets.3, s32[128]{0:T(128)} %sources.3, s32[1]{0:T(128)S(6)} %copy.17.count, bf16[128,128,128]{2,1,0:T(8,128)(2,1)} %weights.3, ...), custom_call_target="tpu_custom_call" | custom-call | tf_op jit(solution)/shard_map/backward/pallas_call | solution.py:397
  71.4 0.0 copy-start.12
  71.4 0.0 copy-start.13
  71.5 4.8 %all-to-all-done.2.slices = f32[32,16,128]{2,1,0:T(8,128)S(1)} async-done(((f32[32,16,128]{2,1,0:T(8,128)}), f32[32,16,128]{2,1,0:T(8,128)S(1)}, u32[]{:S(2)}, u32[]{:S(2)}) %all-to-all-start.2) | async-done | bytes 262176 | tf_op jit(solution)/shard_map/all_to_all | solution.py:577
  76.3 5.1 %all-to-all-start.4 = ((bf16[64,32,128]{2,1,0:T(8,128)(2,1)}), bf16[64,32,128]{2,1,0:T(8,128)(2,1)S(1)}, u32[]{:S(2)}, u32[]{:S(2)}) async-start(bf16[64,32,128]{2,1,0:T(8,128)(2,1)} %get-tuple-element.29), calls=%async_computation.4 | async-start | bytes 1048576 | tf_op jit(solution)/shard_map/all_to_all | solution.py:577
  81.4 0.2 collective-permute-start.7
  81.7 0.2 fold.1.w_near
  81.8 0.4 collective-permute-start.8
  82.3 1.2 collective-permute-done.8.w_far
  83.5 0.2 collective-permute-done.7.far
  83.7 1.0 copy-done.1
  84.7 0.3 join.1
  85.0 1.1 collective-permute-start.9
  86.1 2.8 %collective-permute-start.10 = (bf16[34,16,128]{2,1,0:T(8,128)(2,1)S(1)}, bf16[34,16,128]{2,1,0:T(8,128)(2,1)S(1)}, u32[]{:S(2)}, u32[]{:S(2)}) collective-permute-start(bf16[34,16,128]{2,1,0:T(8,128)(2,1)S(1)} %get-tuple-element.27), channel_id=1, source_target_pairs={{0,2},{1,3},{2,0},{3,1},{4,6},{5,7},{6,4},{7,5},{8,10},{9,11},{10,... | collective-permute-start | bytes 417800 | tf_op jit(solution)/shard_map/ppermute | solution.py:569
  89.0 1.7 %collective-permute-start.11 = (bf16[34,16,128]{2,1,0:T(8,128)(2,1)S(1)}, bf16[34,16,128]{2,1,0:T(8,128)(2,1)S(1)}, u32[]{:S(2)}, u32[]{:S(2)}) collective-permute-start(bf16[34,16,128]{2,1,0:T(8,128)(2,1)S(1)} %get-tuple-element.28), channel_id=1, source_target_pairs={{0,3},{1,0},{2,1},{3,2},{4,7},{5,4},{6,5},{7,6},{8,11},{9,8},{10,9... | collective-permute-start | bytes 417800 | tf_op jit(solution)/shard_map/ppermute | solution.py:569
  90.7 1.5 %collective-permute-done.9.hub1 = bf16[34,16,128]{2,1,0:T(8,128)(2,1)S(1)} collective-permute-done((bf16[34,16,128]{2,1,0:T(8,128)(2,1)S(1)}, bf16[34,16,128]{2,1,0:T(8,128)(2,1)S(1)}, u32[]{:S(2)}, u32[]{:S(2)}) %collective-permute-start.9) | collective-permute-done | bytes 139296 | tf_op jit(solution)/shard_map/ppermute | solution.py:569
  92.2 3.5 %collective-permute-done.10.hub2 = bf16[34,16,128]{2,1,0:T(8,128)(2,1)S(1)} collective-permute-done((bf16[34,16,128]{2,1,0:T(8,128)(2,1)S(1)}, bf16[34,16,128]{2,1,0:T(8,128)(2,1)S(1)}, u32[]{:S(2)}, u32[]{:S(2)}) %collective-permute-start.10) | collective-permute-done | bytes 139296 | tf_op jit(solution)/shard_map/ppermute | solution.py:569
  95.6 0.0 collective-permute-done.11.hub3
  95.6 1.0 merge.1
  96.6 1.9 %all-to-all-done.4.received = bf16[64,32,128]{2,1,0:T(8,128)(2,1)S(1)} async-done(((bf16[64,32,128]{2,1,0:T(8,128)(2,1)}), bf16[64,32,128]{2,1,0:T(8,128)(2,1)S(1)}, u32[]{:S(2)}, u32[]{:S(2)}) %all-to-all-start.4) | async-done | bytes 524320 | tf_op jit(solution)/shard_map/all_to_all | solution.py:577
  98.5 8.0 %all-to-all-start.3 = ((bf16[32,32,128]{2,1,0:T(8,128)(2,1)}), bf16[32,32,128]{2,1,0:T(8,128)(2,1)S(1)}, u32[]{:S(2)}, u32[]{:S(2)}) async-start(bf16[32,32,128]{2,1,0:T(8,128)(2,1)} %merge.1), calls=%async_computation.3 | async-start | bytes 524288 | tf_op jit(solution)/shard_map/all_to_all | solution.py:577
  106.6 0.1 copy.16
  106.7 0.1 reshape.24.send_ids
  106.8 1.6 %copy-done = f32[4096,128]{1,0:T(8,128)S(1)} copy-done((f32[4096,128]{1,0:T(8,128)S(1)}, f32[4096,128]{1,0:T(8,128)}, u32[]{:S(2)}) %copy-start) | copy-done | bytes 2097176
  108.3 5.1 %scatter.1.grad_nodes = f32[4096,128]{1,0:T(8,128)S(1)} custom-call(s32[1,2048]{1,0:T(1,128)S(1)} %reshape.24.send_ids, bf16[64,32,128]{2,1,0:T(8,128)(2,1)S(1)} %all-to-all-done.4.received, f32[4096,128]{1,0:T(8,128)S(1)} %copy-done), custom_call_target="tpu_custom_call" | custom-call | tf_op jit(solution)/shard_map/scatter/pallas_call | solution.py:523
  113.5 4.9 %all-to-all-done.3.received = bf16[32,32,128]{2,1,0:T(8,128)(2,1)S(1)} async-done(((bf16[32,32,128]{2,1,0:T(8,128)(2,1)}), bf16[32,32,128]{2,1,0:T(8,128)(2,1)S(1)}, u32[]{:S(2)}, u32[]{:S(2)}) %all-to-all-start.3) | async-done | bytes 262176 | tf_op jit(solution)/shard_map/all_to_all | solution.py:577
  118.3 2.3 %finish.1 = (f32[4096,128]{1,0:T(8,128)}, f32[128,256]{1,0:T(8,128)}, f32[128,256]{1,0:T(8,128)}) custom-call(s32[16]{0:T(128)S(1)} %copy-done.2, bf16[32,32,128]{2,1,0:T(8,128)(2,1)S(1)} %all-to-all-done.3.received, f32[4096,128]{1,0:T(8,128)S(1)} %scatter.1.grad_nodes), custom_call_target="tpu_custom_call" | custom-call | tf_op jit(solution)/shard_map/finish/pallas_call | solution.py:553
  (26 shorter events, 0.1 us)
Async XLA Ops:
  3.2 21.2 %all-to-all-start.1 = ((bf16[32,16,128]{2,1,0:T(8,128)(2,1)}), bf16[32,16,128]{2,1,0:T(8,128)(2,1)S(1)}, u32[]{:S(2)}, u32[]{:S(2)}) async-start(bf16[32,16,128]{2,1,0:T(8,128)(2,1)} %hub_pack.1), calls=%async_computation.1 | async-start | bytes 262144 | tf_op jit(solution)/shard_map/all_to_all | solution.py:577
  24.4 22.6 %copy-start.4 = (bf16[32,16,128]{2,1,0:T(8,128)(2,1)}, bf16[32,16,128]{2,1,0:T(8,128)(2,1)S(1)}, u32[]{:S(2)}) copy-start(bf16[32,16,128]{2,1,0:T(8,128)(2,1)S(1)} %all-to-all-done.1.refs_0_) | copy-start | bytes 393220
  24.4 22.6 %all-to-all-start = ((bf16[64,32,128]{2,1,0:T(8,128)(2,1)}), bf16[64,32,128]{2,1,0:T(8,128)(2,1)S(1)}, u32[]{:S(2)}, u32[]{:S(2)}) async-start(bf16[64,32,128]{2,1,0:T(8,128)(2,1)} %halo_pack.1), calls=%async_computation | async-start | bytes 1048576 | tf_op jit(solution)/shard_map/all_to_all | solution.py:577
  29.9 8.7 %collective-permute-start.2 = (bf16[32,16,128]{2,1,0:T(8,128)(2,1)S(1)}, bf16[32,16,128]{2,1,0:T(8,128)(2,1)S(1)}, u32[]{:S(2)}, u32[]{:S(2)}) collective-permute-start(bf16[32,16,128]{2,1,0:T(8,128)(2,1)S(1)} %all-to-all-done.1.refs_0_), channel_id=1, source_target_pairs={{0,3},{1,0},{2,1},{3,2},{4,7},{5,4},{6,5},{7,6},{8,11},{9,8},{10,9... | collective-permute-start | bytes 393224 | tf_op jit(solution)/shard_map/ppermute | solution.py:569
  32.8 7.9 %collective-permute-start.1 = (bf16[32,16,128]{2,1,0:T(8,128)(2,1)S(1)}, bf16[32,16,128]{2,1,0:T(8,128)(2,1)S(1)}, u32[]{:S(2)}, u32[]{:S(2)}) collective-permute-start(bf16[32,16,128]{2,1,0:T(8,128)(2,1)S(1)} %all-to-all-done.1.refs_0_), channel_id=1, source_target_pairs={{0,2},{1,3},{2,0},{3,1},{4,6},{5,7},{6,4},{7,5},{8,10},{9,11},{10,... | collective-permute-start | bytes 393224 | tf_op jit(solution)/shard_map/ppermute | solution.py:569
  33.6 8.8 %collective-permute-start = (bf16[32,16,128]{2,1,0:T(8,128)(2,1)S(1)}, bf16[32,16,128]{2,1,0:T(8,128)(2,1)S(1)}, u32[]{:S(2)}, u32[]{:S(2)}) collective-permute-start(bf16[32,16,128]{2,1,0:T(8,128)(2,1)S(1)} %all-to-all-done.1.refs_0_), channel_id=1, source_target_pairs={{0,1},{1,2},{2,3},{3,0},{4,5},{5,6},{6,7},{7,4},{8,9},{9,10},{10,1... | collective-permute-start | bytes 393224 | tf_op jit(solution)/shard_map/ppermute | solution.py:569
  34.4 8.6 %collective-permute-start.3 = (bf16[32,16,128]{2,1,0:T(8,128)(2,1)S(1)}, bf16[32,16,128]{2,1,0:T(8,128)(2,1)S(1)}, u32[]{:S(2)}, u32[]{:S(2)}) collective-permute-start(bf16[32,16,128]{2,1,0:T(8,128)(2,1)S(1)} %all-to-all-done.1.refs_0_), channel_id=1, source_target_pairs={{0,4},{4,0},{1,5},{5,1},{2,6},{6,2},{3,7},{7,3},{8,12},{12,8},{9,1... | collective-permute-start | bytes 393224 | tf_op jit(solution)/shard_map/ppermute | solution.py:573
  38.7 8.4 %copy-start.5 = (bf16[32,16,128]{2,1,0:T(8,128)(2,1)}, bf16[32,16,128]{2,1,0:T(8,128)(2,1)S(1)}, u32[]{:S(2)}) copy-start(bf16[32,16,128]{2,1,0:T(8,128)(2,1)S(1)} %collective-permute-done.2.refs_3_) | copy-start | bytes 393220
  38.7 4.4 %collective-permute-start.6 = (bf16[32,16,128]{2,1,0:T(8,128)(2,1)S(1)}, bf16[32,16,128]{2,1,0:T(8,128)(2,1)S(1)}, u32[]{:S(2)}, u32[]{:S(2)}) collective-permute-start(bf16[32,16,128]{2,1,0:T(8,128)(2,1)S(1)} %collective-permute-done.2.refs_3_), channel_id=1, source_target_pairs={{0,4},{4,0},{1,5},{5,1},{2,6},{6,2},{3,7},{7,3},{8,12},{12,8},{9,1... | collective-permute-start | bytes 393224 | tf_op jit(solution)/shard_map/ppermute | solution.py:573
  40.6 6.4 %copy-start.6 = (bf16[32,16,128]{2,1,0:T(8,128)(2,1)}, bf16[32,16,128]{2,1,0:T(8,128)(2,1)S(1)}, u32[]{:S(2)}) copy-start(bf16[32,16,128]{2,1,0:T(8,128)(2,1)S(1)} %collective-permute-done.1.refs_2_) | copy-start | bytes 393220
  40.6 2.5 %collective-permute-start.5 = (bf16[32,16,128]{2,1,0:T(8,128)(2,1)S(1)}, bf16[32,16,128]{2,1,0:T(8,128)(2,1)S(1)}, u32[]{:S(2)}, u32[]{:S(2)}) collective-permute-start(bf16[32,16,128]{2,1,0:T(8,128)(2,1)S(1)} %collective-permute-done.1.refs_2_), channel_id=1, source_target_pairs={{0,4},{4,0},{1,5},{5,1},{2,6},{6,2},{3,7},{7,3},{8,12},{12,8},{9,1... | collective-permute-start | bytes 393224 | tf_op jit(solution)/shard_map/ppermute | solution.py:573
  42.3 4.7 %copy-start.7 = (bf16[32,16,128]{2,1,0:T(8,128)(2,1)}, bf16[32,16,128]{2,1,0:T(8,128)(2,1)S(1)}, u32[]{:S(2)}) copy-start(bf16[32,16,128]{2,1,0:T(8,128)(2,1)S(1)} %collective-permute-done.refs_1_) | copy-start | bytes 393220
  42.3 1.3 %collective-permute-start.4 = (bf16[32,16,128]{2,1,0:T(8,128)(2,1)S(1)}, bf16[32,16,128]{2,1,0:T(8,128)(2,1)S(1)}, u32[]{:S(2)}, u32[]{:S(2)}) collective-permute-start(bf16[32,16,128]{2,1,0:T(8,128)(2,1)S(1)} %collective-permute-done.refs_1_), channel_id=1, source_target_pairs={{0,4},{4,0},{1,5},{5,1},{2,6},{6,2},{3,7},{7,3},{8,12},{12,8},{9,1... | collective-permute-start | bytes 393224 | tf_op jit(solution)/shard_map/ppermute | solution.py:573
  43.1 4.0 %copy-start.8 = (bf16[32,16,128]{2,1,0:T(8,128)(2,1)}, bf16[32,16,128]{2,1,0:T(8,128)(2,1)S(1)}, u32[]{:S(2)}) copy-start(bf16[32,16,128]{2,1,0:T(8,128)(2,1)S(1)} %collective-permute-done.3.refs_4_) | copy-start | bytes 393220
  43.1 4.0 %copy-start.9 = (bf16[32,16,128]{2,1,0:T(8,128)(2,1)}, bf16[32,16,128]{2,1,0:T(8,128)(2,1)S(1)}, u32[]{:S(2)}) copy-start(bf16[32,16,128]{2,1,0:T(8,128)(2,1)S(1)} %collective-permute-done.6.refs_7_) | copy-start | bytes 393220
  43.1 4.0 %copy-start.10 = (bf16[32,16,128]{2,1,0:T(8,128)(2,1)}, bf16[32,16,128]{2,1,0:T(8,128)(2,1)S(1)}, u32[]{:S(2)}) copy-start(bf16[32,16,128]{2,1,0:T(8,128)(2,1)S(1)} %collective-permute-done.5.refs_6_) | copy-start | bytes 393220
  43.7 3.4 %copy-start.11 = (bf16[32,16,128]{2,1,0:T(8,128)(2,1)}, bf16[32,16,128]{2,1,0:T(8,128)(2,1)S(1)}, u32[]{:S(2)}) copy-start(bf16[32,16,128]{2,1,0:T(8,128)(2,1)S(1)} %collective-permute-done.4.refs_5_) | copy-start | bytes 393220
  47.0 0.8 copy-start.3
  58.0 18.3 %all-to-all-start.2 = ((f32[32,16,128]{2,1,0:T(8,128)}), f32[32,16,128]{2,1,0:T(8,128)S(1)}, u32[]{:S(2)}, u32[]{:S(2)}) async-start(f32[32,16,128]{2,1,0:T(8,128)} %bitcast.6), calls=%async_computation.2 | async-start | bytes 524288 | tf_op jit(solution)/shard_map/all_to_all | solution.py:577
  71.4 35.1 %copy-start.12 = (s32[64,32]{0,1:T(8,128)S(1)}, s32[64,32]{0,1:T(8,128)}, u32[]{:S(2)}) copy-start(s32[64,32]{0,1:T(8,128)} %param.16) | copy-start | bytes 24580
  71.4 35.1 %copy-start.13 = (s32[64]{0:T(128)S(1)}, s32[64]{0:T(128)}, u32[]{:S(2)}) copy-start(s32[64]{0:T(128)} %send_counts.1) | copy-start | bytes 772
  76.3 22.2 %all-to-all-start.4 = ((bf16[64,32,128]{2,1,0:T(8,128)(2,1)}), bf16[64,32,128]{2,1,0:T(8,128)(2,1)S(1)}, u32[]{:S(2)}, u32[]{:S(2)}) async-start(bf16[64,32,128]{2,1,0:T(8,128)(2,1)} %get-tuple-element.29), calls=%async_computation.4 | async-start | bytes 1048576 | tf_op jit(solution)/shard_map/all_to_all | solution.py:577
  81.4 2.2 %collective-permute-start.7 = (bf16[4,32,16,128]{3,2,1,0:T(8,128)(2,1)}, bf16[4,32,16,128]{3,2,1,0:T(8,128)(2,1)S(1)}, u32[]{:S(2)}, u32[]{:S(2)}) collective-permute-start(bf16[4,32,16,128]{3,2,1,0:T(8,128)(2,1)} %get-tuple-element.23), channel_id=1, source_target_pairs={{0,4},{4,0},{1,5},{5,1},{2,6},{6,2},{3,7},{7,3},{8,12},{12,8},{9,1... | collective-permute-start | bytes 1572872 | tf_op jit(solution)/shard_map/ppermute | solution.py:573
  81.8 1.6 %collective-permute-start.8 = (bf16[2,16,128]{2,1,0:T(8,128)(2,1)S(1)}, bf16[2,16,128]{2,1,0:T(8,128)(2,1)S(1)}, u32[]{:S(2)}, u32[]{:S(2)}) collective-permute-start(bf16[2,16,128]{2,1,0:T(8,128)(2,1)S(1)} %fold.1.w_near), channel_id=1, source_target_pairs={{0,4},{4,0},{1,5},{5,1},{2,6},{6,2},{3,7},{7,3},{8,12},{12,8},{9,1... | collective-permute-start | bytes 24584 | tf_op jit(solution)/shard_map/ppermute | solution.py:573
  83.7 1.0 copy-start.1
  85.0 7.2 %collective-permute-start.9 = (bf16[34,16,128]{2,1,0:T(8,128)(2,1)S(1)}, bf16[34,16,128]{2,1,0:T(8,128)(2,1)S(1)}, u32[]{:S(2)}, u32[]{:S(2)}) collective-permute-start(bf16[34,16,128]{2,1,0:T(8,128)(2,1)S(1)} %get-tuple-element.26), channel_id=1, source_target_pairs={{0,1},{1,2},{2,3},{3,0},{4,5},{5,6},{6,7},{7,4},{8,9},{9,10},{10,1... | collective-permute-start | bytes 417800 | tf_op jit(solution)/shard_map/ppermute | solution.py:569
  86.1 9.5 %collective-permute-start.10 = (bf16[34,16,128]{2,1,0:T(8,128)(2,1)S(1)}, bf16[34,16,128]{2,1,0:T(8,128)(2,1)S(1)}, u32[]{:S(2)}, u32[]{:S(2)}) collective-permute-start(bf16[34,16,128]{2,1,0:T(8,128)(2,1)S(1)} %get-tuple-element.27), channel_id=1, source_target_pairs={{0,2},{1,3},{2,0},{3,1},{4,6},{5,7},{6,4},{7,5},{8,10},{9,11},{10,... | collective-permute-start | bytes 417800 | tf_op jit(solution)/shard_map/ppermute | solution.py:569
  89.0 6.7 %collective-permute-start.11 = (bf16[34,16,128]{2,1,0:T(8,128)(2,1)S(1)}, bf16[34,16,128]{2,1,0:T(8,128)(2,1)S(1)}, u32[]{:S(2)}, u32[]{:S(2)}) collective-permute-start(bf16[34,16,128]{2,1,0:T(8,128)(2,1)S(1)} %get-tuple-element.28), channel_id=1, source_target_pairs={{0,3},{1,0},{2,1},{3,2},{4,7},{5,4},{6,5},{7,6},{8,11},{9,8},{10,9... | collective-permute-start | bytes 417800 | tf_op jit(solution)/shard_map/ppermute | solution.py:569
  98.5 19.8 %all-to-all-start.3 = ((bf16[32,32,128]{2,1,0:T(8,128)(2,1)}), bf16[32,32,128]{2,1,0:T(8,128)(2,1)S(1)}, u32[]{:S(2)}, u32[]{:S(2)}) async-start(bf16[32,32,128]{2,1,0:T(8,128)(2,1)} %merge.1), calls=%async_computation.3 | async-start | bytes 524288 | tf_op jit(solution)/shard_map/all_to_all | solution.py:577
  106.7 1.6 %copy-start = (f32[4096,128]{1,0:T(8,128)S(1)}, f32[4096,128]{1,0:T(8,128)}, u32[]{:S(2)}) copy-start(f32[4096,128]{1,0:T(8,128)} %get-tuple-element.30.grad_own) | copy-start | bytes 6291460
  108.3 10.0 %copy-start.2 = (s32[16]{0:T(128)S(1)}, s32[16]{0:T(128)}, u32[]{:S(2)}) copy-start(s32[16]{0:T(128)} %hub_rows.3) | copy-start | bytes 196

commit v3 on v2

--- a/solution.py
+++ b/solution.py
@@ -13,6 +13,7 @@
 CHUNK = 16
 ROWS = 1024
 NEAR = 16
+PARTS = 4
 WHOLE = 60
 REPS = 4
 CORES = 2
@@ -126,12 +127,12 @@
     return pltpu.make_async_copy(weights.at[part], held.at[part], sems.at[c])
 
 
-def start_weights(chunks, weights, held, sems):
+def start_weights(first, chunks, weights, held, sems):
     def start(c, carry):
         weight_copy(c, weights, held, sems).start()
         return carry
 
-    lax.fori_loop(0, chunks, start, 0)
+    lax.fori_loop(first, chunks, start, 0)
 
 
 def forward_kernel(
@@ -169,7 +170,7 @@
         copy.start()
     live = count[0]
     chunks = (live + CHUNK - 1) // CHUNK
-    start_weights(chunks, weights, held, weight_sems)
+    start_weights(0, chunks, weights, held, weight_sems)
     late = [
         pltpu.make_async_copy(x, y, sems.at[len(pieces) + n])
         for n, (x, y) in enumerate(
@@ -255,8 +256,8 @@
     steps = node_rows // ROWS
     lax.fori_loop(0, steps, dense, 0)
     half = grad_total.shape[1] // 2
-    w_all[: grad_total.shape[0]] = grad_total[:, :half]
-    w_all[grad_total.shape[0] :] = grad_total[:, half:]
+    w_all[: grad_total.shape[0]] = grad_total[:, :half].astype(BF16)
+    w_all[grad_total.shape[0] :] = grad_total[:, half:].astype(BF16)
     w_copy = pltpu.make_async_copy(w_all, grad_w, sems.at[0])
     w_copy.start()
 
@@ -283,7 +284,7 @@
         jax.ShapeDtypeStruct((node_rows, hidden_width), BF16),
         jax.ShapeDtypeStruct((node_rows, width), BF16),
         jax.ShapeDtypeStruct((node_rows, width), F32),
-        jax.ShapeDtypeStruct((4 * width, hidden_width // 2), F32),
+        jax.ShapeDtypeStruct((4 * width, hidden_width // 2), BF16),
     )
     return pl.pallas_call(
         forward_kernel,
@@ -309,17 +310,168 @@
     )(targets, sources, count, weights, features, halo, *hubs, out_grad, w_self, w_nbr)
 
 
-def backward_kernel(
+def collect(live, wanted, order):
+    def look(t, found):
+        order[found] = t
+        return found + wanted(t).astype(jnp.int32)
+
+    found = lax.fori_loop(0, live, look, 0)
+    for u in range(CHUNK):
+        order[found + u] = 0
+    return found
+
+
+def add_tiles(found, order, chunks, targets, held, agg, totals, place, spare, arrived):
+    block = held.shape[1]
+
+    def step(c, waited):
+        at = [order[c * CHUNK + u] for u in range(CHUNK)]
+        last = order[jnp.minimum(c * CHUNK + CHUNK, found) - 1]
+        needed = last // CHUNK + 1
+
+        def wait(n, carry):
+            arrived(n)
+            return carry
+
+        lax.fori_loop(waited, needed, wait, 0)
+        products = [
+            lax.dot_general(
+                held[t],
+                agg[rows_at(targets[t], block)],
+                (((0,), (0,)), ((), ())),
+                preferred_element_type=F32,
+            )
+            for t in at
+        ]
+        for u, value in enumerate(products):
+            block_at = jnp.where(c * CHUNK + u < found, place(at[u]), spare)
+            totals[rows_at(block_at, block)] += value
+        return needed
+
+    waited = lax.fori_loop(0, (found + CHUNK - 1) // CHUNK, step, 0)
+
+    def rest(n, carry):
+        arrived(n)
+        return carry
+
+    lax.fori_loop(waited, chunks, rest, 0)
+
+
+def backward_far_kernel(
+    targets,
+    sources,
+    count,
+    weights,
+    grad_agg,
+    halo,
+    near,
+    far,
+    order,
+    held,
+    agg,
+    totals,
+    halo_all,
+    near_all,
+    far_all,
+    weight_sems,
+    sems,
+):
+    block = weights.shape[1]
+    node_rows, width = grad_agg.shape
+    own_blocks = node_rows // block
+    peers, slots, _ = halo.shape
+    _, groups, hubs, _ = near.shape
+    agg_copy = pltpu.make_async_copy(grad_agg, agg, sems.at[0])
+    agg_copy.start()
+    live = count[0]
+    chunks = (live + CHUNK - 1) // CHUNK
+    start_weights(0, chunks, weights, held, weight_sems)
+    rep = lax.axis_index("rep")
+    core = lax.axis_index("core")
+    totals[...] = jnp.zeros_like(totals)
+    found = collect(live, lambda t: sources[t] >= own_blocks, order)
+    agg_copy.wait()
+    add_tiles(
+        found,
+        order,
+        chunks,
+        targets,
+        held,
+        agg,
+        totals,
+        lambda t: sources[t] - own_blocks,
+        totals.shape[0] // block - 1,
+        lambda n: weight_copy(n, weights, held, weight_sems).wait(),
+    )
+    outs = [
+        pltpu.make_async_copy(x, y, sems.at[n])
+        for n, (x, y) in enumerate(((far_all, far), (halo_all, halo), (near_all, near)))
+    ]
+    halo_base = groups * CORES * REPS * hubs
+
+    def emit_hub(piece, to_core):
+        def emit(p, carry):
+            for i in range(REPS):
+                to_rep = lax.rem(rep + i, REPS)
+                part = (p * CORES + to_core) * REPS + to_rep
+                piece[i, p] = totals[rows_at(part, hubs)].astype(BF16)
+            return carry
+
+        lax.fori_loop(0, groups, emit, 0, unroll=4)
+
+    def emit_halo(p, carry):
+        at = pl.multiple_of(halo_base + p * slots, slots)
+        halo_all[p] = totals[pl.ds(at, slots)].astype(BF16)
+        return carry
+
+    emit_hub(far_all, 1 - core)
+    outs[0].start()
+    lax.fori_loop(0, peers, emit_halo, 0, unroll=8)
+    outs[1].start()
+    emit_hub(near_all, core)
+    outs[2].start()
+    for copy in outs:
+        copy.wait()
+
+
+def backward_far(targets, sources, count, weights, grad_agg, peers, slots, hubs):
+    node_rows, width = grad_agg.shape
+    tiles, block, _ = weights.shape
+    groups = peers // CORES
+    total_rows = peers * REPS * hubs + peers * slots + block
+    halo = jax.ShapeDtypeStruct((peers, slots, width), BF16)
+    piece = jax.ShapeDtypeStruct((REPS, groups, hubs, width), BF16)
+    return pl.pallas_call(
+        backward_far_kernel,
+        out_shape=(halo, piece, piece),
+        in_specs=[smem()] * 3 + [hbm()] * 2,
+        out_specs=(hbm(),) * 3,
+        scratch_shapes=[
+            pltpu.SMEM((tiles + CHUNK,), jnp.int32),
+            pltpu.VMEM((tiles, block, block), BF16),
+            pltpu.VMEM((node_rows, width), BF16),
+            pltpu.VMEM((total_rows, width), F32),
+            pltpu.VMEM(halo.shape, BF16),
+            pltpu.VMEM(piece.shape, BF16),
+            pltpu.VMEM(piece.shape, BF16),
+            pltpu.SemaphoreType.DMA((tiles // CHUNK,)),
+            pltpu.SemaphoreType.DMA((3,)),
+        ],
+        compiler_params=params(WHOLE),
+        name="backward_far",
+    )(targets, sources, count, weights, grad_agg)
+
+
+def backward_own_kernel(
     targets,
     sources,
     count,
     weights,
     grad_agg,
     grad_self,
+    after,
     grad_own,
-    halo,
-    near,
-    far,
+    order,
     held,
     agg,
     totals,
@@ -328,92 +480,56 @@
 ):
     block = weights.shape[1]
     node_rows, width = grad_agg.shape
-    peers, slots, _ = halo.shape
-    _, groups, hubs, _ = near.shape
-    agg_copy = pltpu.make_async_copy(grad_agg, agg, sems.at[0])
-    self_copy = pltpu.make_async_copy(grad_self, totals.at[pl.ds(0, node_rows)], sems.at[1])
-    agg_copy.start()
-    self_copy.start()
+    own_blocks = node_rows // block
+    copies = [
+        pltpu.make_async_copy(grad_agg, agg, sems.at[0]),
+        pltpu.make_async_copy(grad_self, totals.at[pl.ds(0, node_rows)], sems.at[1]),
+    ]
+    for copy in copies:
+        copy.start()
     live = count[0]
     chunks = (live + CHUNK - 1) // CHUNK
-    start_weights(chunks, weights, held, weight_sems)
-    rep = lax.axis_index("rep")
-    core = lax.axis_index("core")
-    totals[node_rows:] = jnp.zeros((totals.shape[0] - node_rows, width), F32)
-    spare = totals.shape[0] // block - 1
-    agg_copy.wait()
-    self_copy.wait()
-
-    def step(c, carry):
-        weight_copy(c, weights, held, weight_sems).wait()
-        products = [
-            lax.dot_general(
-                held[c * CHUNK + u],
-                agg[rows_at(targets[c * CHUNK + u], block)],
-                (((0,), (0,)), ((), ())),
-                preferred_element_type=F32,
-            )
-            for u in range(CHUNK)
-        ]
-        for u, value in enumerate(products):
-            t = c * CHUNK + u
-            source = jnp.where(t < live, sources[t], spare)
-            totals[rows_at(source, block)] += value
-        return carry
-
-    lax.fori_loop(0, chunks, step, 0)
-    own_copy = pltpu.make_async_copy(totals.at[pl.ds(0, node_rows)], grad_own, sems.at[0])
-    own_copy.start()
-    hub_base = node_rows
-    halo_base = hub_base + groups * CORES * REPS * hubs
-
-    def emit_halo(p, carry):
-        at = pl.multiple_of(halo_base + p * slots, slots)
-        halo[p] = totals[pl.ds(at, slots)].astype(BF16)
-        return carry
-
-    lax.fori_loop(0, peers, emit_halo, 0)
-
-    def emit_hub(p, carry):
-        for c, piece in enumerate((near, far)):
-            to_core = lax.rem(core + c, CORES)
-            for i in range(REPS):
-                to_rep = lax.rem(rep + i, REPS)
-                part = (p * CORES + to_core) * REPS + to_rep
-                at = pl.multiple_of(hub_base + part * hubs, hubs)
-                piece[i, p] = totals[pl.ds(at, hubs)].astype(BF16)
-        return carry
-
-    lax.fori_loop(0, groups, emit_hub, 0)
-    own_copy.wait()
-
-
-def backward(targets, sources, count, weights, grad_agg, grad_self, peers, slots, hubs):
+    start_weights(0, chunks, weights, held, weight_sems)
+    totals[node_rows:] = jnp.zeros((block, width), F32)
+    found = collect(live, lambda t: sources[t] < own_blocks, order)
+    for copy in copies:
+        copy.wait()
+    add_tiles(
+        found,
+        order,
+        chunks,
+        targets,
+        held,
+        agg,
+        totals,
+        lambda t: sources[t],
+        own_blocks,
+        lambda n: weight_copy(n, weights, held, weight_sems).wait(),
+    )
+    out = pltpu.make_async_copy(totals.at[pl.ds(0, node_rows)], grad_own, sems.at[0])
+    out.start()
+    out.wait()
+
+
+def backward_own(targets, sources, count, weights, grad_agg, grad_self, after):
     node_rows, width = grad_agg.shape
     tiles, block, _ = weights.shape
-    groups = peers // CORES
-    total_rows = node_rows + peers * REPS * hubs + peers * slots + block
-    piece = jax.ShapeDtypeStruct((REPS, groups, hubs, width), BF16)
-    return pl.pallas_call(
-        backward_kernel,
-        out_shape=(
-            jax.ShapeDtypeStruct((node_rows, width), F32),
-            jax.ShapeDtypeStruct((peers, slots, width), BF16),
-            piece,
-            piece,
-        ),
-        in_specs=[smem()] * 3 + [hbm()] * 3,
-        out_specs=(hbm(), vmem(), vmem(), vmem()),
+    return pl.pallas_call(
+        backward_own_kernel,
+        out_shape=jax.ShapeDtypeStruct((node_rows, width), F32),
+        in_specs=[smem()] * 3 + [hbm()] * 4,
+        out_specs=hbm(),
         scratch_shapes=[
+            pltpu.SMEM((tiles + CHUNK,), jnp.int32),
             pltpu.VMEM((tiles, block, block), BF16),
             pltpu.VMEM((node_rows, width), BF16),
-            pltpu.VMEM((total_rows, width), F32),
+            pltpu.VMEM((node_rows + block, width), F32),
             pltpu.SemaphoreType.DMA((tiles // CHUNK,)),
             pltpu.SemaphoreType.DMA((2,)),
         ],
-        compiler_params=params(WHOLE),
-        name="backward",
-    )(targets, sources, count, weights, grad_agg, grad_self)
+        compiler_params=params(40),
+        name="backward_own",
+    )(targets, sources, count, weights, grad_agg, grad_self, after)
 
 
 def split_pair(total):
@@ -423,7 +539,7 @@
 
 def fold_kernel(slices, out):
     def peer(p, total):
-        return total + slices[p]
+        return total + slices[p].astype(F32)
 
     total = lax.fori_loop(0, slices.shape[0], peer, jnp.zeros(slices.shape[1:], F32))
     out[0], out[1] = split_pair(total)
@@ -603,12 +719,15 @@
         out_grad, w_self, w_nbr,
     )
     w_slices = swap(grad_w.reshape(groups, -1, width), GROUP)
-    grad_own, grad_halo, near, far = backward(
-        tile_targets, tile_sources, tile_count, tile_weights, grad_agg, grad_self, peers, slots, hubs
+    grad_halo, near, far = backward_far(
+        tile_targets, tile_sources, tile_count, tile_weights, grad_agg, peers, slots, hubs
     )
     returned = swap(grad_halo, DOM)
     w_pair = fold(w_slices)
     pieces = join(near, core_swap(far), w_pair, core_swap(w_pair))
+    grad_own = backward_own(
+        tile_targets, tile_sources, tile_count, tile_weights, grad_agg, grad_self, pieces[0]
+    )
     pieces = [pieces[0]] + [rep_shift(pieces[i], i) for i in range(1, REPS)]
     merged = swap(merge(pieces), GROUP)
     slot_live = jnp.arange(slots, dtype=jnp.int32)[None, :] < send_counts[:, None]

time: 122 us -> 121 us (level)
  waiting for transfers between devices: 34.4 us -> 27.6 us
  starting transfers between devices: 46.3 us -> 50.5 us
  local copies, waits for them, and re-layouts: 3.57 us -> 5.78 us
    all_to_all x5, waiting for transfers between devices: 19.7 us -> 16.1 us  [swap(): return lax.all_to_all(value, axes, split_axis=0, concat_axis=0, tiled=True)]
    ppermute x6, waiting for transfers between devices: 12.8 us -> 9.81 us  [rep_shift(): lax.ppermute(value, 'rep', [(j, (j + shift) % REPS) for j in range(REPS)])]
    all_to_all x5, starting transfers between devices: 35.3 us -> 37.6 us  [swap(): return lax.all_to_all(value, axes, split_axis=0, concat_axis=0, tiled=True)]
    unnamed x28 -> x36, local copies, waits for them, and re-layouts: 3.4 us -> 5.62 us
    ppermute x6, starting transfers between devices: 10.2 us -> 11.7 us  [rep_shift(): lax.ppermute(value, 'rep', [(j, (j + shift) % REPS) for j in range(REPS)])]
    pallas_call x1 -> x2, Pallas kernels: 8.03 us -> 7.77 us  [the longest x1 4.83 us: backward_far(): pl.pallas_call(backward_far_kernel, out_shape=(halo, piece, piece), in_sp...]
  transfers between devices with their start and end apart: 17 -> 17, of which waited for: 13 -> 12; matrix products, arithmetic and copies ran while one was open for 0% -> 0% of each run, Pallas kernels for 16% -> 16%
where the time goes in v3:
time: 121 us; the launch traced here: 119 us
  starting transfers between devices  50.5 us (42%)
  Pallas kernels  33.6 us (28%)
  waiting for transfers between devices  27.6 us (23%)
  local copies, waits for them, and re-layouts  5.78 us (5%)
  between operations  1.61 us (1%)
    all_to_all x5, starting transfers between devices, swap(): return lax.all_to_all(value, axes, split_axis=0, concat_axis=0, tiled=True)  37.6 us
    all_to_all x5, waiting for transfers between devices, swap(): return lax.all_to_all(value, axes, split_axis=0, concat_axis=0, tiled=True)  16.1 us
    ppermute x6, starting transfers between devices, rep_shift(): lax.ppermute(value, 'rep', [(j, (j + shift) % REPS) for j in range(REPS)])  11.7 us
    ppermute x6, waiting for transfers between devices, rep_shift(): lax.ppermute(value, 'rep', [(j, (j + shift) % REPS) for j in range(REPS)])  9.81 us
    pallas_call x1, Pallas kernels, forward(): pl.pallas_call(forward_kernel, out_shape=shapes, in_specs=[smem()] * 3 +...  9.28 us
    unnamed x36, local copies, waits for them, and re-layouts  5.62 us
    pallas_call x1, Pallas kernels, scatter(): pl.pallas_call(scatter_kernel, out_shape=jax.ShapeDtypeStruct(grad_own.sh...  5.1 us
    pallas_call x1, Pallas kernels, halo_pack(): pl.pallas_call(halo_pack_kernel, out_shape=jax.ShapeDtypeStruct((peers, s...  5.1 us
  transfers between devices with their start and end apart: 17, of which 12 were waited for; matrix products, arithmetic and copies ran while one was open for 0% of the time, Pallas kernels for 16%

profile of v3, /device:TPU:32, one launch (start us, length us, event | category | flops | bytes accessed | tf_op | source)
XLA Modules:
  0.0 119.0 jit_solution(13077850163487472903)
XLA Ops:
  0.6 2.6 %hub_pack.1 = bf16[32,16,128]{2,1,0:T(8,128)(2,1)} custom-call(s32[16]{0:T(128)} %hub_rows.3, bf16[4096,128]{1,0:T(8,128)(2,1)} %features.3), custom_call_target="tpu_custom_call" | custom-call | tf_op jit(solution)/shard_map/hub_pack/pallas_call | solution.py:73
  3.2 11.4 %all-to-all-start.1 = ((bf16[32,16,128]{2,1,0:T(8,128)(2,1)}), bf16[32,16,128]{2,1,0:T(8,128)(2,1)S(1)}, u32[]{:S(2)}, u32[]{:S(2)}) async-start(bf16[32,16,128]{2,1,0:T(8,128)(2,1)} %hub_pack.1), calls=%async_computation.1 | async-start | bytes 262144 | tf_op jit(solution)/shard_map/all_to_all | solution.py:693
  14.6 5.1 %halo_pack.1 = bf16[64,32,128]{2,1,0:T(8,128)(2,1)} custom-call(s32[32,64]{1,0:T(8,128)} %bitcast.7, s32[64]{0:T(128)} %send_counts.1, bf16[4096,128]{1,0:T(8,128)(2,1)} %features.3), custom_call_target="tpu_custom_call" | custom-call | tf_op jit(solution)/shard_map/halo_pack/pallas_call | solution.py:111
  19.7 4.7 %all-to-all-done.1.refs_0_ = bf16[32,16,128]{2,1,0:T(8,128)(2,1)S(1)} async-done(((bf16[32,16,128]{2,1,0:T(8,128)(2,1)}), bf16[32,16,128]{2,1,0:T(8,128)(2,1)S(1)}, u32[]{:S(2)}, u32[]{:S(2)}) %all-to-all-start.1) | async-done | bytes 131104 | tf_op jit(solution)/shard_map/all_to_all | solution.py:693
  24.4 5.5 %all-to-all-start = ((bf16[64,32,128]{2,1,0:T(8,128)(2,1)}), bf16[64,32,128]{2,1,0:T(8,128)(2,1)S(1)}, u32[]{:S(2)}, u32[]{:S(2)}) async-start(bf16[64,32,128]{2,1,0:T(8,128)(2,1)} %halo_pack.1), calls=%async_computation | async-start | bytes 1048576 | tf_op jit(solution)/shard_map/all_to_all | solution.py:693
  29.9 1.6 %collective-permute-start = (bf16[32,16,128]{2,1,0:T(8,128)(2,1)S(1)}, bf16[32,16,128]{2,1,0:T(8,128)(2,1)S(1)}, u32[]{:S(2)}, u32[]{:S(2)}) collective-permute-start(bf16[32,16,128]{2,1,0:T(8,128)(2,1)S(1)} %all-to-all-done.1.refs_0_), channel_id=1, source_target_pairs={{0,1},{1,2},{2,3},{3,0},{4,5},{5,6},{6,7},{7,4},{8,9},{9,10},{10,1... | collective-permute-start | bytes 393224 | tf_op jit(solution)/shard_map/ppermute | solution.py:685
  31.5 2.7 %collective-permute-start.1 = (bf16[32,16,128]{2,1,0:T(8,128)(2,1)S(1)}, bf16[32,16,128]{2,1,0:T(8,128)(2,1)S(1)}, u32[]{:S(2)}, u32[]{:S(2)}) collective-permute-start(bf16[32,16,128]{2,1,0:T(8,128)(2,1)S(1)} %all-to-all-done.1.refs_0_), channel_id=1, source_target_pairs={{0,2},{1,3},{2,0},{3,1},{4,6},{5,7},{6,4},{7,5},{8,10},{9,11},{10,... | collective-permute-start | bytes 393224 | tf_op jit(solution)/shard_map/ppermute | solution.py:685
  34.2 1.4 %collective-permute-start.2 = (bf16[32,16,128]{2,1,0:T(8,128)(2,1)S(1)}, bf16[32,16,128]{2,1,0:T(8,128)(2,1)S(1)}, u32[]{:S(2)}, u32[]{:S(2)}) collective-permute-start(bf16[32,16,128]{2,1,0:T(8,128)(2,1)S(1)} %all-to-all-done.1.refs_0_), channel_id=1, source_target_pairs={{0,3},{1,0},{2,1},{3,2},{4,7},{5,4},{6,5},{7,6},{8,11},{9,8},{10,9... | collective-permute-start | bytes 393224 | tf_op jit(solution)/shard_map/ppermute | solution.py:685
  35.7 1.1 collective-permute-done.refs_1_
  36.8 3.8 %collective-permute-done.1.refs_2_ = bf16[32,16,128]{2,1,0:T(8,128)(2,1)S(1)} collective-permute-done((bf16[32,16,128]{2,1,0:T(8,128)(2,1)S(1)}, bf16[32,16,128]{2,1,0:T(8,128)(2,1)S(1)}, u32[]{:S(2)}, u32[]{:S(2)}) %collective-permute-start.1) | collective-permute-done | bytes 131104 | tf_op jit(solution)/shard_map/ppermute | solution.py:685
  40.6 0.5 collective-permute-start.6
  41.8 0.1 collective-permute-done.5.refs_6_
  41.9 0.2 collective-permute-done.6.refs_7_
  42.1 4.9 %all-to-all-done = bf16[64,32,128]{2,1,0:T(8,128)(2,1)S(1)} async-done(((bf16[64,32,128]{2,1,0:T(8,128)(2,1)}), bf16[64,32,128]{2,1,0:T(8,128)(2,1)S(1)}, u32[]{:S(2)}, u32[]{:S(2)}) %all-to-all-start) | async-done | bytes 524320 | tf_op jit(solution)/shard_map/all_to_all | solution.py:693
  47.1 0.7 copy-done.7
  47.8 9.3 %forward.1 = (bf16[4096,256]{1,0:T(8,128)(2,1)}, bf16[4096,128]{1,0:T(8,128)(2,1)}, f32[4096,128]{1,0:T(8,128)}, bf16[512,128]{1,0:T(8,128)(2,1)}) custom-call(s32[128]{0:T(128)} %targets.5, s32[128]{0:T(128)} %sources.5, s32[1]{0:T(128)S(6)} %copy.17.count, bf16[128,128,128]{2,1,0:T(8,128)(2,1)} %weights.5, bf16[32,8,16,128]{3,2,1,0:T(8,128)(2,1)} %bitcast.4, ...), custom_call_target="tpu_custom_call" | custom-call | tf_op jit(solution)/shard_map/forward/pallas_call | solution.py:289
  57.1 7.0 %all-to-all-start.2 = ((bf16[32,16,128]{2,1,0:T(8,128)(2,1)}), bf16[32,16,128]{2,1,0:T(8,128)(2,1)S(1)}, u32[]{:S(2)}, u32[]{:S(2)}) async-start(bf16[32,16,128]{2,1,0:T(8,128)(2,1)} %bitcast.6), calls=%async_computation.2 | async-start | bytes 262144 | tf_op jit(solution)/shard_map/all_to_all | solution.py:693
  64.1 4.8 %backward_far.1 = (bf16[64,32,128]{2,1,0:T(8,128)(2,1)}, bf16[4,32,16,128]{3,2,1,0:T(8,128)(2,1)}, bf16[4,32,16,128]{3,2,1,0:T(8,128)(2,1)}) custom-call(s32[128]{0:T(128)} %targets.5, s32[128]{0:T(128)} %sources.5, s32[1]{0:T(128)S(6)} %copy.17.count, bf16[128,128,128]{2,1,0:T(8,128)(2,1)} %weights.5, bf16[4096,128]{1,0:T(8,128)(2,1)} %get-tuple-element.19.grad_agg), custom_call_target="tpu_custom_call" | custom-call | tf_op jit(solution)/shard_map/backward_far/pallas_call | solution.py:444
  68.9 0.0 copy-start.16
  69.0 0.0 copy-start.17
  69.0 0.0 copy-start.4
  69.0 0.0 copy-start.5
  69.0 4.8 %all-to-all-done.2.slices = bf16[32,16,128]{2,1,0:T(8,128)(2,1)S(1)} async-done(((bf16[32,16,128]{2,1,0:T(8,128)(2,1)}), bf16[32,16,128]{2,1,0:T(8,128)(2,1)S(1)}, u32[]{:S(2)}, u32[]{:S(2)}) %all-to-all-start.2) | async-done | bytes 131104 | tf_op jit(solution)/shard_map/all_to_all | solution.py:693
  73.8 5.4 %all-to-all-start.4 = ((bf16[64,32,128]{2,1,0:T(8,128)(2,1)}), bf16[64,32,128]{2,1,0:T(8,128)(2,1)S(1)}, u32[]{:S(2)}, u32[]{:S(2)}) async-start(bf16[64,32,128]{2,1,0:T(8,128)(2,1)} %get-tuple-element.27), calls=%async_computation.4 | async-start | bytes 1048576 | tf_op jit(solution)/shard_map/all_to_all | solution.py:693
  79.2 0.2 collective-permute-start.7
  79.4 0.2 fold.1.w_near
  79.6 0.4 collective-permute-start.8
  80.0 1.2 collective-permute-done.8.w_far
  81.2 0.2 collective-permute-done.7.far
  81.4 1.0 copy-done.3
  82.4 0.3 join.1
  82.7 1.8 %collective-permute-start.9 = (bf16[34,16,128]{2,1,0:T(8,128)(2,1)S(1)}, bf16[34,16,128]{2,1,0:T(8,128)(2,1)S(1)}, u32[]{:S(2)}, u32[]{:S(2)}) collective-permute-start(bf16[34,16,128]{2,1,0:T(8,128)(2,1)S(1)} %get-tuple-element.24), channel_id=1, source_target_pairs={{0,1},{1,2},{2,3},{3,0},{4,5},{5,6},{6,7},{7,4},{8,9},{9,10},{10,1... | collective-permute-start | bytes 417800 | tf_op jit(solution)/shard_map/ppermute | solution.py:685
  84.6 2.4 %collective-permute-start.10 = (bf16[34,16,128]{2,1,0:T(8,128)(2,1)S(1)}, bf16[34,16,128]{2,1,0:T(8,128)(2,1)S(1)}, u32[]{:S(2)}, u32[]{:S(2)}) collective-permute-start(bf16[34,16,128]{2,1,0:T(8,128)(2,1)S(1)} %get-tuple-element.25), channel_id=1, source_target_pairs={{0,2},{1,3},{2,0},{3,1},{4,6},{5,7},{6,4},{7,5},{8,10},{9,11},{10,... | collective-permute-start | bytes 417800 | tf_op jit(solution)/shard_map/ppermute | solution.py:685
  86.9 1.8 %collective-permute-start.11 = (bf16[34,16,128]{2,1,0:T(8,128)(2,1)S(1)}, bf16[34,16,128]{2,1,0:T(8,128)(2,1)S(1)}, u32[]{:S(2)}, u32[]{:S(2)}) collective-permute-start(bf16[34,16,128]{2,1,0:T(8,128)(2,1)S(1)} %get-tuple-element.26), channel_id=1, source_target_pairs={{0,3},{1,0},{2,1},{3,2},{4,7},{5,4},{6,5},{7,6},{8,11},{9,8},{10,9... | collective-permute-start | bytes 417800 | tf_op jit(solution)/shard_map/ppermute | solution.py:685
  88.7 1.3 %collective-permute-done.9.hub1 = bf16[34,16,128]{2,1,0:T(8,128)(2,1)S(1)} collective-permute-done((bf16[34,16,128]{2,1,0:T(8,128)(2,1)S(1)}, bf16[34,16,128]{2,1,0:T(8,128)(2,1)S(1)}, u32[]{:S(2)}, u32[]{:S(2)}) %collective-permute-start.9) | collective-permute-done | bytes 139296 | tf_op jit(solution)/shard_map/ppermute | solution.py:685
  90.0 3.6 %collective-permute-done.10.hub2 = bf16[34,16,128]{2,1,0:T(8,128)(2,1)S(1)} collective-permute-done((bf16[34,16,128]{2,1,0:T(8,128)(2,1)S(1)}, bf16[34,16,128]{2,1,0:T(8,128)(2,1)S(1)}, u32[]{:S(2)}, u32[]{:S(2)}) %collective-permute-start.10) | collective-permute-done | bytes 139296 | tf_op jit(solution)/shard_map/ppermute | solution.py:685
  93.6 1.0 merge.1
  94.6 1.7 %all-to-all-done.4.received = bf16[64,32,128]{2,1,0:T(8,128)(2,1)S(1)} async-done(((bf16[64,32,128]{2,1,0:T(8,128)(2,1)}), bf16[64,32,128]{2,1,0:T(8,128)(2,1)S(1)}, u32[]{:S(2)}, u32[]{:S(2)}) %all-to-all-start.4) | async-done | bytes 524320 | tf_op jit(solution)/shard_map/all_to_all | solution.py:693
  96.3 8.3 %all-to-all-start.3 = ((bf16[32,32,128]{2,1,0:T(8,128)(2,1)}), bf16[32,32,128]{2,1,0:T(8,128)(2,1)S(1)}, u32[]{:S(2)}, u32[]{:S(2)}) async-start(bf16[32,32,128]{2,1,0:T(8,128)(2,1)} %merge.1), calls=%async_computation.3 | async-start | bytes 524288 | tf_op jit(solution)/shard_map/all_to_all | solution.py:693
  104.6 0.1 copy.16
  104.7 0.1 reshape.24.send_ids
  104.8 0.0 copy-start
  104.9 2.2 %copy-done = bf16[128,128,128]{2,1,0:T(8,128)(2,1)S(1)} copy-done((bf16[128,128,128]{2,1,0:T(8,128)(2,1)S(1)}, bf16[128,128,128]{2,1,0:T(8,128)(2,1)}, u32[]{:S(2)}) %copy-start) | copy-done | bytes 4194328
  107.0 1.6 %copy-done.2 = f32[4096,128]{1,0:T(8,128)S(1)} copy-done((f32[4096,128]{1,0:T(8,128)S(1)}, f32[4096,128]{1,0:T(8,128)}, u32[]{:S(2)}) %copy-start.2) | copy-done | bytes 2097176
  108.6 2.9 %backward_own.1.grad_own = f32[4096,128]{1,0:T(8,128)S(1)} custom-call(s32[128]{0:T(128)S(1)} %copy-done.4, s32[128]{0:T(128)S(1)} %copy-done.5, s32[1]{0:T(128)S(6)} %copy.17.count, bf16[128,128,128]{2,1,0:T(8,128)(2,1)S(1)} %copy-done, bf16[4096,128]{1,0:T(8,128)(2,1)S(1)} %copy-done.1, f32[4096,128]{1,0:T(8,128)S(1)} %copy-done.2, ...), custom_call_target="tpu_custom_call" | custom-call | tf_op jit(solution)/shard_map/backward_own/pallas_call | solution.py:517
  111.6 0.0 copy-start.6
  111.6 5.1 %scatter.1.grad_nodes = f32[4096,128]{1,0:T(8,128)S(1)} custom-call(s32[1,2048]{1,0:T(1,128)S(1)} %reshape.24.send_ids, bf16[64,32,128]{2,1,0:T(8,128)(2,1)S(1)} %all-to-all-done.4.received, f32[4096,128]{1,0:T(8,128)S(1)} %backward_own.1.grad_own), custom_call_target="tpu_custom_call" | custom-call | tf_op jit(solution)/shard_map/scatter/pallas_call | solution.py:639
  116.7 2.3 %finish.1 = (f32[4096,128]{1,0:T(8,128)}, f32[128,256]{1,0:T(8,128)}, f32[128,256]{1,0:T(8,128)}) custom-call(s32[16]{0:T(128)S(1)} %copy-done.6, bf16[32,32,128]{2,1,0:T(8,128)(2,1)S(1)} %all-to-all-done.3.received, f32[4096,128]{1,0:T(8,128)S(1)} %scatter.1.grad_nodes), custom_call_target="tpu_custom_call" | custom-call | tf_op jit(solution)/shard_map/finish/pallas_call | solution.py:669
  (35 shorter events, 0.1 us)
Async XLA Ops:
  3.2 21.2 %all-to-all-start.1 = ((bf16[32,16,128]{2,1,0:T(8,128)(2,1)}), bf16[32,16,128]{2,1,0:T(8,128)(2,1)S(1)}, u32[]{:S(2)}, u32[]{:S(2)}) async-start(bf16[32,16,128]{2,1,0:T(8,128)(2,1)} %hub_pack.1), calls=%async_computation.1 | async-start | bytes 262144 | tf_op jit(solution)/shard_map/all_to_all | solution.py:693
  24.4 22.6 %copy-start.8 = (bf16[32,16,128]{2,1,0:T(8,128)(2,1)}, bf16[32,16,128]{2,1,0:T(8,128)(2,1)S(1)}, u32[]{:S(2)}) copy-start(bf16[32,16,128]{2,1,0:T(8,128)(2,1)S(1)} %all-to-all-done.1.refs_0_) | copy-start | bytes 393220
  24.4 22.6 %all-to-all-start = ((bf16[64,32,128]{2,1,0:T(8,128)(2,1)}), bf16[64,32,128]{2,1,0:T(8,128)(2,1)S(1)}, u32[]{:S(2)}, u32[]{:S(2)}) async-start(bf16[64,32,128]{2,1,0:T(8,128)(2,1)} %halo_pack.1), calls=%async_computation | async-start | bytes 1048576 | tf_op jit(solution)/shard_map/all_to_all | solution.py:693
  29.9 6.8 %collective-permute-start = (bf16[32,16,128]{2,1,0:T(8,128)(2,1)S(1)}, bf16[32,16,128]{2,1,0:T(8,128)(2,1)S(1)}, u32[]{:S(2)}, u32[]{:S(2)}) collective-permute-start(bf16[32,16,128]{2,1,0:T(8,128)(2,1)S(1)} %all-to-all-done.1.refs_0_), channel_id=1, source_target_pairs={{0,1},{1,2},{2,3},{3,0},{4,5},{5,6},{6,7},{7,4},{8,9},{9,10},{10,1... | collective-permute-start | bytes 393224 | tf_op jit(solution)/shard_map/ppermute | solution.py:685
  31.5 9.1 %collective-permute-start.1 = (bf16[32,16,128]{2,1,0:T(8,128)(2,1)S(1)}, bf16[32,16,128]{2,1,0:T(8,128)(2,1)S(1)}, u32[]{:S(2)}, u32[]{:S(2)}) collective-permute-start(bf16[32,16,128]{2,1,0:T(8,128)(2,1)S(1)} %all-to-all-done.1.refs_0_), channel_id=1, source_target_pairs={{0,2},{1,3},{2,0},{3,1},{4,6},{5,7},{6,4},{7,5},{8,10},{9,11},{10,... | collective-permute-start | bytes 393224 | tf_op jit(solution)/shard_map/ppermute | solution.py:685
  34.2 6.3 %collective-permute-start.2 = (bf16[32,16,128]{2,1,0:T(8,128)(2,1)S(1)}, bf16[32,16,128]{2,1,0:T(8,128)(2,1)S(1)}, u32[]{:S(2)}, u32[]{:S(2)}) collective-permute-start(bf16[32,16,128]{2,1,0:T(8,128)(2,1)S(1)} %all-to-all-done.1.refs_0_), channel_id=1, source_target_pairs={{0,3},{1,0},{2,1},{3,2},{4,7},{5,4},{6,5},{7,6},{8,11},{9,8},{10,9... | collective-permute-start | bytes 393224 | tf_op jit(solution)/shard_map/ppermute | solution.py:685
  35.7 6.1 %collective-permute-start.3 = (bf16[32,16,128]{2,1,0:T(8,128)(2,1)S(1)}, bf16[32,16,128]{2,1,0:T(8,128)(2,1)S(1)}, u32[]{:S(2)}, u32[]{:S(2)}) collective-permute-start(bf16[32,16,128]{2,1,0:T(8,128)(2,1)S(1)} %all-to-all-done.1.refs_0_), channel_id=1, source_target_pairs={{0,4},{4,0},{1,5},{5,1},{2,6},{6,2},{3,7},{7,3},{8,12},{12,8},{9,1... | collective-permute-start | bytes 393224 | tf_op jit(solution)/shard_map/ppermute | solution.py:689
  36.8 10.3 %copy-start.9 = (bf16[32,16,128]{2,1,0:T(8,128)(2,1)}, bf16[32,16,128]{2,1,0:T(8,128)(2,1)S(1)}, u32[]{:S(2)}) copy-start(bf16[32,16,128]{2,1,0:T(8,128)(2,1)S(1)} %collective-permute-done.refs_1_) | copy-start | bytes 393220
  36.8 5.0 %collective-permute-start.4 = (bf16[32,16,128]{2,1,0:T(8,128)(2,1)S(1)}, bf16[32,16,128]{2,1,0:T(8,128)(2,1)S(1)}, u32[]{:S(2)}, u32[]{:S(2)}) collective-permute-start(bf16[32,16,128]{2,1,0:T(8,128)(2,1)S(1)} %collective-permute-done.refs_1_), channel_id=1, source_target_pairs={{0,4},{4,0},{1,5},{5,1},{2,6},{6,2},{3,7},{7,3},{8,12},{12,8},{9,1... | collective-permute-start | bytes 393224 | tf_op jit(solution)/shard_map/ppermute | solution.py:689
  40.6 6.5 %copy-start.10 = (bf16[32,16,128]{2,1,0:T(8,128)(2,1)}, bf16[32,16,128]{2,1,0:T(8,128)(2,1)S(1)}, u32[]{:S(2)}) copy-start(bf16[32,16,128]{2,1,0:T(8,128)(2,1)S(1)} %collective-permute-done.1.refs_2_) | copy-start | bytes 393220
  40.6 1.3 %collective-permute-start.5 = (bf16[32,16,128]{2,1,0:T(8,128)(2,1)S(1)}, bf16[32,16,128]{2,1,0:T(8,128)(2,1)S(1)}, u32[]{:S(2)}, u32[]{:S(2)}) collective-permute-start(bf16[32,16,128]{2,1,0:T(8,128)(2,1)S(1)} %collective-permute-done.1.refs_2_), channel_id=1, source_target_pairs={{0,4},{4,0},{1,5},{5,1},{2,6},{6,2},{3,7},{7,3},{8,12},{12,8},{9,1... | collective-permute-start | bytes 393224 | tf_op jit(solution)/shard_map/ppermute | solution.py:689
  40.6 6.5 %copy-start.11 = (bf16[32,16,128]{2,1,0:T(8,128)(2,1)}, bf16[32,16,128]{2,1,0:T(8,128)(2,1)S(1)}, u32[]{:S(2)}) copy-start(bf16[32,16,128]{2,1,0:T(8,128)(2,1)S(1)} %collective-permute-done.2.refs_3_) | copy-start | bytes 393220
  40.6 1.5 %collective-permute-start.6 = (bf16[32,16,128]{2,1,0:T(8,128)(2,1)S(1)}, bf16[32,16,128]{2,1,0:T(8,128)(2,1)S(1)}, u32[]{:S(2)}, u32[]{:S(2)}) collective-permute-start(bf16[32,16,128]{2,1,0:T(8,128)(2,1)S(1)} %collective-permute-done.2.refs_3_), channel_id=1, source_target_pairs={{0,4},{4,0},{1,5},{5,1},{2,6},{6,2},{3,7},{7,3},{8,12},{12,8},{9,1... | collective-permute-start | bytes 393224 | tf_op jit(solution)/shard_map/ppermute | solution.py:689
  41.7 5.3 %copy-start.12 = (bf16[32,16,128]{2,1,0:T(8,128)(2,1)}, bf16[32,16,128]{2,1,0:T(8,128)(2,1)S(1)}, u32[]{:S(2)}) copy-start(bf16[32,16,128]{2,1,0:T(8,128)(2,1)S(1)} %collective-permute-done.3.refs_4_) | copy-start | bytes 393220
  41.8 5.3 %copy-start.13 = (bf16[32,16,128]{2,1,0:T(8,128)(2,1)}, bf16[32,16,128]{2,1,0:T(8,128)(2,1)S(1)}, u32[]{:S(2)}) copy-start(bf16[32,16,128]{2,1,0:T(8,128)(2,1)S(1)} %collective-permute-done.4.refs_5_) | copy-start | bytes 393220
  41.9 5.2 %copy-start.14 = (bf16[32,16,128]{2,1,0:T(8,128)(2,1)}, bf16[32,16,128]{2,1,0:T(8,128)(2,1)S(1)}, u32[]{:S(2)}) copy-start(bf16[32,16,128]{2,1,0:T(8,128)(2,1)S(1)} %collective-permute-done.5.refs_6_) | copy-start | bytes 393220
  42.1 5.0 %copy-start.15 = (bf16[32,16,128]{2,1,0:T(8,128)(2,1)}, bf16[32,16,128]{2,1,0:T(8,128)(2,1)S(1)}, u32[]{:S(2)}) copy-start(bf16[32,16,128]{2,1,0:T(8,128)(2,1)S(1)} %collective-permute-done.6.refs_7_) | copy-start | bytes 393220
  47.0 0.8 copy-start.7
  57.1 16.7 %all-to-all-start.2 = ((bf16[32,16,128]{2,1,0:T(8,128)(2,1)}), bf16[32,16,128]{2,1,0:T(8,128)(2,1)S(1)}, u32[]{:S(2)}, u32[]{:S(2)}) async-start(bf16[32,16,128]{2,1,0:T(8,128)(2,1)} %bitcast.6), calls=%async_computation.2 | async-start | bytes 262144 | tf_op jit(solution)/shard_map/all_to_all | solution.py:693
  68.9 35.7 %copy-start.16 = (s32[64,32]{0,1:T(8,128)S(1)}, s32[64,32]{0,1:T(8,128)}, u32[]{:S(2)}) copy-start(s32[64,32]{0,1:T(8,128)} %param.16) | copy-start | bytes 24580
  69.0 35.7 %copy-start.17 = (s32[64]{0:T(128)S(1)}, s32[64]{0:T(128)}, u32[]{:S(2)}) copy-start(s32[64]{0:T(128)} %send_counts.1) | copy-start | bytes 772
  69.0 35.9 %copy-start.1 = (bf16[4096,128]{1,0:T(8,128)(2,1)S(1)}, bf16[4096,128]{1,0:T(8,128)(2,1)}, u32[]{:S(2)}) copy-start(bf16[4096,128]{1,0:T(8,128)(2,1)} %get-tuple-element.19.grad_agg) | copy-start | bytes 3145732
  69.0 35.9 %copy-start.4 = (s32[128]{0:T(128)S(1)}, s32[128]{0:T(128)}, u32[]{:S(2)}) copy-start(s32[128]{0:T(128)} %targets.5) | copy-start | bytes 1540
  69.0 35.9 %copy-start.5 = (s32[128]{0:T(128)S(1)}, s32[128]{0:T(128)}, u32[]{:S(2)}) copy-start(s32[128]{0:T(128)} %sources.5) | copy-start | bytes 1540
  73.8 22.5 %all-to-all-start.4 = ((bf16[64,32,128]{2,1,0:T(8,128)(2,1)}), bf16[64,32,128]{2,1,0:T(8,128)(2,1)S(1)}, u32[]{:S(2)}, u32[]{:S(2)}) async-start(bf16[64,32,128]{2,1,0:T(8,128)(2,1)} %get-tuple-element.27), calls=%async_computation.4 | async-start | bytes 1048576 | tf_op jit(solution)/shard_map/all_to_all | solution.py:693
  79.2 2.2 %collective-permute-start.7 = (bf16[4,32,16,128]{3,2,1,0:T(8,128)(2,1)}, bf16[4,32,16,128]{3,2,1,0:T(8,128)(2,1)S(1)}, u32[]{:S(2)}, u32[]{:S(2)}) collective-permute-start(bf16[4,32,16,128]{3,2,1,0:T(8,128)(2,1)} %get-tuple-element.21), channel_id=1, source_target_pairs={{0,4},{4,0},{1,5},{5,1},{2,6},{6,2},{3,7},{7,3},{8,12},{12,8},{9,1... | collective-permute-start | bytes 1572872 | tf_op jit(solution)/shard_map/ppermute | solution.py:689
  79.6 1.6 %collective-permute-start.8 = (bf16[2,16,128]{2,1,0:T(8,128)(2,1)S(1)}, bf16[2,16,128]{2,1,0:T(8,128)(2,1)S(1)}, u32[]{:S(2)}, u32[]{:S(2)}) collective-permute-start(bf16[2,16,128]{2,1,0:T(8,128)(2,1)S(1)} %fold.1.w_near), channel_id=1, source_target_pairs={{0,4},{4,0},{1,5},{5,1},{2,6},{6,2},{3,7},{7,3},{8,12},{12,8},{9,1... | collective-permute-start | bytes 24584 | tf_op jit(solution)/shard_map/ppermute | solution.py:689
  81.4 1.0 copy-start.3
  82.7 7.3 %collective-permute-start.9 = (bf16[34,16,128]{2,1,0:T(8,128)(2,1)S(1)}, bf16[34,16,128]{2,1,0:T(8,128)(2,1)S(1)}, u32[]{:S(2)}, u32[]{:S(2)}) collective-permute-start(bf16[34,16,128]{2,1,0:T(8,128)(2,1)S(1)} %get-tuple-element.24), channel_id=1, source_target_pairs={{0,1},{1,2},{2,3},{3,0},{4,5},{5,6},{6,7},{7,4},{8,9},{9,10},{10,1... | collective-permute-start | bytes 417800 | tf_op jit(solution)/shard_map/ppermute | solution.py:685
  84.6 9.0 %collective-permute-start.10 = (bf16[34,16,128]{2,1,0:T(8,128)(2,1)S(1)}, bf16[34,16,128]{2,1,0:T(8,128)(2,1)S(1)}, u32[]{:S(2)}, u32[]{:S(2)}) collective-permute-start(bf16[34,16,128]{2,1,0:T(8,128)(2,1)S(1)} %get-tuple-element.25), channel_id=1, source_target_pairs={{0,2},{1,3},{2,0},{3,1},{4,6},{5,7},{6,4},{7,5},{8,10},{9,11},{10,... | collective-permute-start | bytes 417800 | tf_op jit(solution)/shard_map/ppermute | solution.py:685
  86.9 6.7 %collective-permute-start.11 = (bf16[34,16,128]{2,1,0:T(8,128)(2,1)S(1)}, bf16[34,16,128]{2,1,0:T(8,128)(2,1)S(1)}, u32[]{:S(2)}, u32[]{:S(2)}) collective-permute-start(bf16[34,16,128]{2,1,0:T(8,128)(2,1)S(1)} %get-tuple-element.26), channel_id=1, source_target_pairs={{0,3},{1,0},{2,1},{3,2},{4,7},{5,4},{6,5},{7,6},{8,11},{9,8},{10,9... | collective-permute-start | bytes 417800 | tf_op jit(solution)/shard_map/ppermute | solution.py:685
  96.3 20.4 %all-to-all-start.3 = ((bf16[32,32,128]{2,1,0:T(8,128)(2,1)}), bf16[32,32,128]{2,1,0:T(8,128)(2,1)S(1)}, u32[]{:S(2)}, u32[]{:S(2)}) async-start(bf16[32,32,128]{2,1,0:T(8,128)(2,1)} %merge.1), calls=%async_computation.3 | async-start | bytes 524288 | tf_op jit(solution)/shard_map/all_to_all | solution.py:693
  104.8 2.2 %copy-start = (bf16[128,128,128]{2,1,0:T(8,128)(2,1)S(1)}, bf16[128,128,128]{2,1,0:T(8,128)(2,1)}, u32[]{:S(2)}) copy-start(bf16[128,128,128]{2,1,0:T(8,128)(2,1)} %weights.5) | copy-start | bytes 12582916
  107.0 1.6 %copy-start.2 = (f32[4096,128]{1,0:T(8,128)S(1)}, f32[4096,128]{1,0:T(8,128)}, u32[]{:S(2)}) copy-start(f32[4096,128]{1,0:T(8,128)} %get-tuple-element.28.grad_self) | copy-start | bytes 6291460
  111.6 5.1 %copy-start.6 = (s32[16]{0:T(128)S(1)}, s32[16]{0:T(128)}, u32[]{:S(2)}) copy-start(s32[16]{0:T(128)} %hub_rows.3) | copy-start | bytes 196

commit v4 on v3

--- a/solution.py
+++ b/solution.py
@@ -13,8 +13,13 @@
 CHUNK = 16
 ROWS = 1024
 NEAR = 16
+TILE = 8
 PARTS = 4
 WHOLE = 60
+FORWARD = 60
+SCATTER = 60
+FINISH = 16
+TOKEN = jax.ShapeDtypeStruct((8, 128), F32)
 REPS = 4
 CORES = 2
 GROUP = "group"
@@ -305,7 +310,7 @@
             pltpu.SemaphoreType.DMA((5 + parts,)),
             pltpu.SemaphoreType.DMA((3,)),
         ],
-        compiler_params=params(WHOLE),
+        compiler_params=params(FORWARD),
         name="forward",
     )(targets, sources, count, weights, features, halo, *hubs, out_grad, w_self, w_nbr)
 
@@ -471,6 +476,7 @@
     grad_self,
     after,
     grad_own,
+    token,
     order,
     held,
     agg,
@@ -508,6 +514,7 @@
     )
     out = pltpu.make_async_copy(totals.at[pl.ds(0, node_rows)], grad_own, sems.at[0])
     out.start()
+    token[...] = jnp.zeros_like(token)
     out.wait()
 
 
@@ -516,9 +523,9 @@
     tiles, block, _ = weights.shape
     return pl.pallas_call(
         backward_own_kernel,
-        out_shape=jax.ShapeDtypeStruct((node_rows, width), F32),
+        out_shape=(jax.ShapeDtypeStruct((node_rows, width), F32), TOKEN),
         in_specs=[smem()] * 3 + [hbm()] * 4,
-        out_specs=hbm(),
+        out_specs=(hbm(), vmem()),
         scratch_shapes=[
             pltpu.SMEM((tiles + CHUNK,), jnp.int32),
             pltpu.VMEM((tiles, block, block), BF16),
@@ -527,7 +534,7 @@
             pltpu.SemaphoreType.DMA((tiles // CHUNK,)),
             pltpu.SemaphoreType.DMA((2,)),
         ],
-        compiler_params=params(40),
+        compiler_params=params(WHOLE),
         name="backward_own",
     )(targets, sources, count, weights, grad_agg, grad_self, after)
 
@@ -557,6 +564,8 @@
 
 
 def join_kernel(near, far, w_near, w_far, *outs):
+    *outs, token = outs
+    token[...] = jnp.zeros_like(token)
     groups = near.shape[1]
     total = (w_near[0].astype(F32) + w_near[1].astype(F32)) + (
         w_far[0].astype(F32) + w_far[1].astype(F32)
@@ -579,15 +588,15 @@
     piece = jax.ShapeDtypeStruct((groups + 2, hubs, width), BF16)
     return pl.pallas_call(
         join_kernel,
-        out_shape=(piece,) * reps,
+        out_shape=(piece,) * reps + (TOKEN,),
         in_specs=[vmem()] * 4,
-        out_specs=(vmem(),) * reps,
+        out_specs=(vmem(),) * (reps + 1),
         compiler_params=params(8),
         name="join",
     )(near, far, w_near, w_far)
 
 
-def merge_kernel(hub0, hub1, hub2, hub3, out, w_parts):
+def merge_kernel(hub0, hub1, hub2, hub3, after, out, w_parts):
     groups, message, width = out.shape
     hubs = hub0.shape[1]
     rep = lax.axis_index("rep")
@@ -608,17 +617,17 @@
     lax.fori_loop(0, groups, group, 0)
 
 
-def merge(pieces):
+def merge(pieces, after):
     groups, hubs, width = pieces[0].shape
     return pl.pallas_call(
         merge_kernel,
         out_shape=jax.ShapeDtypeStruct((groups - 2, 2 * hubs, width), BF16),
-        in_specs=[vmem()] * 4,
+        in_specs=[vmem()] * 4 + [hbm()],
         out_specs=vmem(),
         scratch_shapes=[pltpu.VMEM((REPS, hubs, width), F32)],
         compiler_params=params(8),
         name="merge",
-    )(*pieces)
+    )(*pieces, after)
 
 
 def scatter_kernel(send_ids, received, grad_own, out):
@@ -641,30 +650,54 @@
         out_shape=jax.ShapeDtypeStruct(grad_own.shape, F32),
         in_specs=[vmem()] * 3,
         out_specs=vmem(),
-        compiler_params=params(32),
+        compiler_params=params(SCATTER),
         name="scatter",
     )(send_ids, received, grad_own)
 
 
 def finish(hub_rows, received, grad_nodes, hidden_width, grad_scale):
-    peers, message, width = received.shape
+    groups, message, width = received.shape
     hubs = hub_rows.shape[0]
-    half = message - hubs
-
-    def body(hub_rows, received, grad_nodes, out, grad_self, grad_nbr, held):
-        out[...] = grad_nodes[...]
+    w_rows = message - hubs
+
+    def body(hub_rows, received, grad_nodes, out, grad_self, grad_nbr, near, held, sems):
+        at = [hub_rows[h] // TILE for h in range(hubs)]
+        for h in range(hubs):
+            pltpu.make_async_copy(
+                grad_nodes.at[rows_at(at[h], TILE)], near.at[pl.ds(h * TILE, TILE)], sems.at[h]
+            ).start()
 
         def place(p, total):
-            held[rows_at(p, half)] = received[p, hubs:].astype(F32) * grad_scale
+            held[rows_at(p, w_rows)] = received[p, hubs:].astype(F32) * grad_scale
             return total + received[p, :hubs].astype(F32)
 
-        total = lax.fori_loop(0, peers, place, jnp.zeros((hubs, width), F32))
-        for h in range(hubs):
-            out[pl.ds(hub_rows[h], 1)] += total[h : h + 1]
+        total = lax.fori_loop(0, groups, place, jnp.zeros((hubs, width), F32), unroll=4)
         for k in range(hidden_width // width):
             columns = pl.ds(k * width, width)
             grad_self[:, columns] = held[2 * k * width : (2 * k + 1) * width]
             grad_nbr[:, columns] = held[(2 * k + 1) * width : (2 * k + 2) * width]
+        for h in range(hubs):
+            pltpu.make_async_copy(
+                grad_nodes.at[rows_at(at[h], TILE)], near.at[pl.ds(h * TILE, TILE)], sems.at[h]
+            ).wait()
+        first = []
+        for h in range(hubs):
+            slot = jnp.int32(h)
+            for j in reversed(range(h)):
+                slot = jnp.where(at[j] == at[h], j, slot)
+            first.append(slot)
+            row = slot * TILE + hub_rows[h] % TILE
+            near[pl.ds(row, 1)] += total[h : h + 1]
+
+        def back(h):
+            return pltpu.make_async_copy(
+                near.at[pl.ds(h * TILE, TILE)], out.at[rows_at(at[h], TILE)], sems.at[h]
+            )
+
+        for h in range(hubs):
+            pl.when(first[h] == h)(back(h).start)
+        for h in range(hubs):
+            pl.when(first[h] == h)(back(h).wait)
 
     return pl.pallas_call(
         body,
@@ -673,10 +706,15 @@
             jax.ShapeDtypeStruct((width, hidden_width), F32),
             jax.ShapeDtypeStruct((width, hidden_width), F32),
         ),
-        in_specs=[smem()] + [vmem()] * 2,
-        out_specs=(vmem(),) * 3,
-        scratch_shapes=[pltpu.VMEM((peers * half, width), F32)],
-        compiler_params=params(24),
+        in_specs=[smem(), vmem(), hbm()],
+        out_specs=(hbm(), vmem(), vmem()),
+        input_output_aliases={2: 0},
+        scratch_shapes=[
+            pltpu.VMEM((hubs * TILE, width), F32),
+            pltpu.VMEM((groups * w_rows, width), F32),
+            pltpu.SemaphoreType.DMA((hubs,)),
+        ],
+        compiler_params=params(FINISH),
         name="finish",
     )(hub_rows, received, grad_nodes)
 
@@ -724,12 +762,12 @@
     )
     returned = swap(grad_halo, DOM)
     w_pair = fold(w_slices)
-    pieces = join(near, core_swap(far), w_pair, core_swap(w_pair))
-    grad_own = backward_own(
-        tile_targets, tile_sources, tile_count, tile_weights, grad_agg, grad_self, pieces[0]
+    *pieces, joined = join(near, core_swap(far), w_pair, core_swap(w_pair))
+    grad_own, own_done = backward_own(
+        tile_targets, tile_sources, tile_count, tile_weights, grad_agg, grad_self, joined
     )
     pieces = [pieces[0]] + [rep_shift(pieces[i], i) for i in range(1, REPS)]
-    merged = swap(merge(pieces), GROUP)
+    merged = swap(merge(pieces, own_done), GROUP)
     slot_live = jnp.arange(slots, dtype=jnp.int32)[None, :] < send_counts[:, None]
     send_ids = jnp.where(slot_live, send_rows, node_rows).reshape(1, -1)
     grad_nodes = scatter(send_ids, returned, grad_own)

time: 121 us -> 122 us (level); the launches traced: 119 us -> 122 us
  Pallas kernels: 33.6 us -> 40.7 us
  waiting for transfers between devices: 27.6 us -> 24.1 us
  local copies, waits for them, and re-layouts: 5.78 us -> 3.84 us
    ppermute x6, waiting for transfers between devices: 9.81 us -> 4.9 us  [rep_shift(): lax.ppermute(value, 'rep', [(j, (j + shift) % REPS) for j in range(REPS)])]
    pallas_call x2, Pallas kernels: 3.25 us -> 6.57 us  [the longest x1 6.26 us: backward_own(): pl.pallas_call(backward_own_kernel, out_shape=(jax.ShapeDtypeStruct((node...]
    pallas_call x1, Pallas kernels: 5.1 us -> 8.23 us  [scatter(): pl.pallas_call(scatter_kernel, out_shape=jax.ShapeDtypeStruct(grad_own.sh...]
    unnamed x36 -> x32, local copies, waits for them, and re-layouts: 5.62 us -> 3.08 us
    all_to_all x5, waiting for transfers between devices: 16.1 us -> 17.5 us  [swap(): return lax.all_to_all(value, axes, split_axis=0, concat_axis=0, tiled=True)]
  transfers between devices with their start and end apart: 17 -> 17, of which waited for: 12 -> 10; matrix products, arithmetic and copies ran while one was open for 0% -> 1% of each run, Pallas kernels for 16% -> 21%
where the time goes in v4:
time: 122 us
  starting transfers between devices  51.2 us (42%)
  Pallas kernels  40.7 us (33%)
  waiting for transfers between devices  24.1 us (20%)
  local copies, waits for them, and re-layouts  3.84 us (3%)
  between operations  1.7 us (1%)
    all_to_all x5, starting transfers between devices, swap(): return lax.all_to_all(value, axes, split_axis=0, concat_axis=0, tiled=True)  38.4 us
    all_to_all x5, waiting for transfers between devices, swap(): return lax.all_to_all(value, axes, split_axis=0, concat_axis=0, tiled=True)  17.5 us
    ppermute x6, starting transfers between devices, rep_shift(): lax.ppermute(value, 'rep', [(j, (j + shift) % REPS) for j in range(REPS)])  11.7 us
    pallas_call x1, Pallas kernels, forward(): pl.pallas_call(forward_kernel, out_shape=shapes, in_specs=[smem()] * 3 +...  9.29 us
    pallas_call x1, Pallas kernels, scatter(): pl.pallas_call(scatter_kernel, out_shape=jax.ShapeDtypeStruct(grad_own.sh...  8.23 us
    pallas_call x1, Pallas kernels, backward_own(): pl.pallas_call(backward_own_kernel, out_shape=(jax.ShapeDtypeStruct((node...  6.26 us
    pallas_call x1, Pallas kernels, halo_pack(): pl.pallas_call(halo_pack_kernel, out_shape=jax.ShapeDtypeStruct((peers, s...  5.1 us
    ppermute x6, waiting for transfers between devices, rep_shift(): lax.ppermute(value, 'rep', [(j, (j + shift) % REPS) for j in range(REPS)])  4.9 us
  transfers between devices with their start and end apart: 17, of which 10 were waited for; matrix products, arithmetic and copies ran while one was open for 1% of the time, Pallas kernels for 21%

profile of v4, /device:TPU:32, one launch (start us, length us, event | category | flops | bytes accessed | tf_op | source)
XLA Modules:
  0.0 121.5 jit_solution(15927466116388102038)
XLA Ops:
  0.6 2.6 %hub_pack.1 = bf16[32,16,128]{2,1,0:T(8,128)(2,1)} custom-call(s32[16]{0:T(128)} %hub_rows.3, bf16[4096,128]{1,0:T(8,128)(2,1)} %features.3), custom_call_target="tpu_custom_call" | custom-call | tf_op jit(solution)/shard_map/hub_pack/pallas_call | solution.py:78
  3.2 11.4 %all-to-all-start.1 = ((bf16[32,16,128]{2,1,0:T(8,128)(2,1)}), bf16[32,16,128]{2,1,0:T(8,128)(2,1)S(1)}, u32[]{:S(2)}, u32[]{:S(2)}) async-start(bf16[32,16,128]{2,1,0:T(8,128)(2,1)} %hub_pack.1), calls=%async_computation.1 | async-start | bytes 262144 | tf_op jit(solution)/shard_map/all_to_all | solution.py:731
  14.6 5.1 %halo_pack.1 = bf16[64,32,128]{2,1,0:T(8,128)(2,1)} custom-call(s32[32,64]{1,0:T(8,128)} %bitcast.7, s32[64]{0:T(128)} %send_counts.1, bf16[4096,128]{1,0:T(8,128)(2,1)} %features.3), custom_call_target="tpu_custom_call" | custom-call | tf_op jit(solution)/shard_map/halo_pack/pallas_call | solution.py:116
  19.7 4.7 %all-to-all-done.1.refs_0_ = bf16[32,16,128]{2,1,0:T(8,128)(2,1)S(1)} async-done(((bf16[32,16,128]{2,1,0:T(8,128)(2,1)}), bf16[32,16,128]{2,1,0:T(8,128)(2,1)S(1)}, u32[]{:S(2)}, u32[]{:S(2)}) %all-to-all-start.1) | async-done | bytes 131104 | tf_op jit(solution)/shard_map/all_to_all | solution.py:731
  24.4 5.5 %all-to-all-start = ((bf16[64,32,128]{2,1,0:T(8,128)(2,1)}), bf16[64,32,128]{2,1,0:T(8,128)(2,1)S(1)}, u32[]{:S(2)}, u32[]{:S(2)}) async-start(bf16[64,32,128]{2,1,0:T(8,128)(2,1)} %halo_pack.1), calls=%async_computation | async-start | bytes 1048576 | tf_op jit(solution)/shard_map/all_to_all | solution.py:731
  29.9 1.6 %collective-permute-start = (bf16[32,16,128]{2,1,0:T(8,128)(2,1)S(1)}, bf16[32,16,128]{2,1,0:T(8,128)(2,1)S(1)}, u32[]{:S(2)}, u32[]{:S(2)}) collective-permute-start(bf16[32,16,128]{2,1,0:T(8,128)(2,1)S(1)} %all-to-all-done.1.refs_0_), channel_id=1, source_target_pairs={{0,1},{1,2},{2,3},{3,0},{4,5},{5,6},{6,7},{7,4},{8,9},{9,10},{10,1... | collective-permute-start | bytes 393224 | tf_op jit(solution)/shard_map/ppermute | solution.py:723
  31.5 2.7 %collective-permute-start.1 = (bf16[32,16,128]{2,1,0:T(8,128)(2,1)S(1)}, bf16[32,16,128]{2,1,0:T(8,128)(2,1)S(1)}, u32[]{:S(2)}, u32[]{:S(2)}) collective-permute-start(bf16[32,16,128]{2,1,0:T(8,128)(2,1)S(1)} %all-to-all-done.1.refs_0_), channel_id=1, source_target_pairs={{0,2},{1,3},{2,0},{3,1},{4,6},{5,7},{6,4},{7,5},{8,10},{9,11},{10,... | collective-permute-start | bytes 393224 | tf_op jit(solution)/shard_map/ppermute | solution.py:723
  34.2 1.4 %collective-permute-start.2 = (bf16[32,16,128]{2,1,0:T(8,128)(2,1)S(1)}, bf16[32,16,128]{2,1,0:T(8,128)(2,1)S(1)}, u32[]{:S(2)}, u32[]{:S(2)}) collective-permute-start(bf16[32,16,128]{2,1,0:T(8,128)(2,1)S(1)} %all-to-all-done.1.refs_0_), channel_id=1, source_target_pairs={{0,3},{1,0},{2,1},{3,2},{4,7},{5,4},{6,5},{7,6},{8,11},{9,8},{10,9... | collective-permute-start | bytes 393224 | tf_op jit(solution)/shard_map/ppermute | solution.py:723
  35.7 0.0 collective-permute-start.3
  35.7 1.1 collective-permute-done.refs_1_
  36.8 0.0 collective-permute-start.4
  36.8 3.8 %collective-permute-done.1.refs_2_ = bf16[32,16,128]{2,1,0:T(8,128)(2,1)S(1)} collective-permute-done((bf16[32,16,128]{2,1,0:T(8,128)(2,1)S(1)}, bf16[32,16,128]{2,1,0:T(8,128)(2,1)S(1)}, u32[]{:S(2)}, u32[]{:S(2)}) %collective-permute-start.1) | collective-permute-done | bytes 131104 | tf_op jit(solution)/shard_map/ppermute | solution.py:723
  40.6 0.5 collective-permute-start.6
  41.7 0.0 collective-permute-done.4.refs_5_
  41.8 0.1 collective-permute-done.5.refs_6_
  41.9 0.2 collective-permute-done.6.refs_7_
  42.1 4.9 %all-to-all-done = bf16[64,32,128]{2,1,0:T(8,128)(2,1)S(1)} async-done(((bf16[64,32,128]{2,1,0:T(8,128)(2,1)}), bf16[64,32,128]{2,1,0:T(8,128)(2,1)S(1)}, u32[]{:S(2)}, u32[]{:S(2)}) %all-to-all-start) | async-done | bytes 524320 | tf_op jit(solution)/shard_map/all_to_all | solution.py:731
  47.1 0.7 copy-done.5
  47.8 9.3 %forward.1 = (bf16[4096,256]{1,0:T(8,128)(2,1)}, bf16[4096,128]{1,0:T(8,128)(2,1)}, f32[4096,128]{1,0:T(8,128)}, bf16[512,128]{1,0:T(8,128)(2,1)}) custom-call(s32[128]{0:T(128)} %targets.5, s32[128]{0:T(128)} %sources.5, s32[1]{0:T(128)S(6)} %copy.19.count, bf16[128,128,128]{2,1,0:T(8,128)(2,1)} %weights.5, bf16[32,8,16,128]{3,2,1,0:T(8,128)(2,1)} %bitcast.4, ...), custom_call_target="tpu_custom_call" | custom-call | tf_op jit(solution)/shard_map/forward/pallas_call | solution.py:294
  57.1 7.0 %all-to-all-start.2 = ((bf16[32,16,128]{2,1,0:T(8,128)(2,1)}), bf16[32,16,128]{2,1,0:T(8,128)(2,1)S(1)}, u32[]{:S(2)}, u32[]{:S(2)}) async-start(bf16[32,16,128]{2,1,0:T(8,128)(2,1)} %bitcast.6), calls=%async_computation.2 | async-start | bytes 262144 | tf_op jit(solution)/shard_map/all_to_all | solution.py:731
  64.1 4.7 %backward_far.1 = (bf16[64,32,128]{2,1,0:T(8,128)(2,1)}, bf16[4,32,16,128]{3,2,1,0:T(8,128)(2,1)}, bf16[4,32,16,128]{3,2,1,0:T(8,128)(2,1)}) custom-call(s32[128]{0:T(128)} %targets.5, s32[128]{0:T(128)} %sources.5, s32[1]{0:T(128)S(6)} %copy.19.count, bf16[128,128,128]{2,1,0:T(8,128)(2,1)} %weights.5, bf16[4096,128]{1,0:T(8,128)(2,1)} %get-tuple-element.22.grad_agg), custom_call_target="tpu_custom_call" | custom-call | tf_op jit(solution)/shard_map/backward_far/pallas_call | solution.py:449
  68.8 4.9 %all-to-all-done.2.slices = bf16[32,16,128]{2,1,0:T(8,128)(2,1)S(1)} async-done(((bf16[32,16,128]{2,1,0:T(8,128)(2,1)}), bf16[32,16,128]{2,1,0:T(8,128)(2,1)S(1)}, u32[]{:S(2)}, u32[]{:S(2)}) %all-to-all-start.2) | async-done | bytes 131104 | tf_op jit(solution)/shard_map/all_to_all | solution.py:731
  73.8 5.0 %all-to-all-start.4 = ((bf16[64,32,128]{2,1,0:T(8,128)(2,1)}), bf16[64,32,128]{2,1,0:T(8,128)(2,1)S(1)}, u32[]{:S(2)}, u32[]{:S(2)}) async-start(bf16[64,32,128]{2,1,0:T(8,128)(2,1)} %get-tuple-element.33), calls=%async_computation.4 | async-start | bytes 1048576 | tf_op jit(solution)/shard_map/all_to_all | solution.py:731
  78.8 0.2 collective-permute-start.7
  79.0 0.2 fold.1.w_near
  79.2 0.4 collective-permute-start.8
  79.6 1.2 collective-permute-done.8.w_far
  80.8 0.2 collective-permute-done.7.far
  81.0 1.0 copy-done
  82.0 0.3 join.1
  82.4 0.0 copy-start.1
  82.4 0.6 copy-done.1
  83.0 2.5 %collective-permute-start.9 = (bf16[34,16,128]{2,1,0:T(8,128)(2,1)S(1)}, bf16[34,16,128]{2,1,0:T(8,128)(2,1)S(1)}, u32[]{:S(2)}, u32[]{:S(2)}) collective-permute-start(bf16[34,16,128]{2,1,0:T(8,128)(2,1)S(1)} %get-tuple-element.27), channel_id=1, source_target_pairs={{0,1},{1,2},{2,3},{3,0},{4,5},{5,6},{6,7},{7,4},{8,9},{9,10},{10,1... | collective-permute-start | bytes 417800 | tf_op jit(solution)/shard_map/ppermute | solution.py:723
  85.5 2.6 %collective-permute-start.10 = (bf16[34,16,128]{2,1,0:T(8,128)(2,1)S(1)}, bf16[34,16,128]{2,1,0:T(8,128)(2,1)S(1)}, u32[]{:S(2)}, u32[]{:S(2)}) collective-permute-start(bf16[34,16,128]{2,1,0:T(8,128)(2,1)S(1)} %get-tuple-element.28), channel_id=1, source_target_pairs={{0,2},{1,3},{2,0},{3,1},{4,6},{5,7},{6,4},{7,5},{8,10},{9,11},{10,... | collective-permute-start | bytes 417800 | tf_op jit(solution)/shard_map/ppermute | solution.py:723
  88.1 0.8 collective-permute-start.11
  88.9 6.3 %backward_own.1 = (f32[4096,128]{1,0:T(8,128)}, f32[8,128]{1,0:T(8,128)}) custom-call(s32[128]{0:T(128)} %targets.5, s32[128]{0:T(128)} %sources.5, s32[1]{0:T(128)S(6)} %copy.19.count, bf16[128,128,128]{2,1,0:T(8,128)(2,1)} %weights.5, bf16[4096,128]{1,0:T(8,128)(2,1)} %get-tuple-element.22.grad_agg, f32[4096,128]{1,0:T(8,128)} %get-tuple-element.30.grad_self, ...), custom_call_target="tpu_custom_call" | custom-call | tf_op jit(solution)/shard_map/backward_own/pallas_call | solution.py:524
  95.2 0.0 collective-permute-done.10.hub2
  95.2 0.0 collective-permute-done.11.hub3
  95.2 0.0 copy-start.2
  95.2 0.7 copy-done.2
  95.9 1.0 merge.1
  96.9 0.0 all-to-all-done.4.received
  96.9 9.5 %all-to-all-start.3 = ((bf16[32,32,128]{2,1,0:T(8,128)(2,1)}), bf16[32,32,128]{2,1,0:T(8,128)(2,1)S(1)}, u32[]{:S(2)}, u32[]{:S(2)}) async-start(bf16[32,32,128]{2,1,0:T(8,128)(2,1)} %merge.1), calls=%async_computation.3 | async-start | bytes 524288 | tf_op jit(solution)/shard_map/all_to_all | solution.py:731
  106.4 0.1 copy.17
  106.5 0.7 reshape.24.send_ids
  107.2 8.2 %scatter.1.grad_nodes = f32[4096,128]{1,0:T(8,128)} custom-call(s32[1,2048]{1,0:T(1,128)} %reshape.24.send_ids, bf16[64,32,128]{2,1,0:T(8,128)(2,1)} %copy-done.4, f32[4096,128]{1,0:T(8,128)} %get-tuple-element.34.grad_own), custom_call_target="tpu_custom_call" | custom-call | tf_op jit(solution)/shard_map/scatter/pallas_call | solution.py:648
  115.4 2.9 %all-to-all-done.3.received = bf16[32,32,128]{2,1,0:T(8,128)(2,1)S(1)} async-done(((bf16[32,32,128]{2,1,0:T(8,128)(2,1)}), bf16[32,32,128]{2,1,0:T(8,128)(2,1)S(1)}, u32[]{:S(2)}, u32[]{:S(2)}) %all-to-all-start.3) | async-done | bytes 262176 | tf_op jit(solution)/shard_map/all_to_all | solution.py:731
  118.3 3.0 %finish.1 = (f32[4096,128]{1,0:T(8,128)}, f32[128,256]{1,0:T(8,128)}, f32[128,256]{1,0:T(8,128)}) custom-call(s32[16]{0:T(128)S(1)} %copy-done.3, bf16[32,32,128]{2,1,0:T(8,128)(2,1)S(1)} %all-to-all-done.3.received, f32[4096,128]{1,0:T(8,128)} %scatter.1.grad_nodes), custom_call_target="tpu_custom_call", output_to_operand_aliasing={{0}: (2, {})} | custom-call | tf_op jit(solution)/shard_map/finish/pallas_call | solution.py:702
  (31 shorter events, 0.1 us)
Async XLA Ops:
  3.2 21.2 %all-to-all-start.1 = ((bf16[32,16,128]{2,1,0:T(8,128)(2,1)}), bf16[32,16,128]{2,1,0:T(8,128)(2,1)S(1)}, u32[]{:S(2)}, u32[]{:S(2)}) async-start(bf16[32,16,128]{2,1,0:T(8,128)(2,1)} %hub_pack.1), calls=%async_computation.1 | async-start | bytes 262144 | tf_op jit(solution)/shard_map/all_to_all | solution.py:731
  24.4 22.6 %copy-start.6 = (bf16[32,16,128]{2,1,0:T(8,128)(2,1)}, bf16[32,16,128]{2,1,0:T(8,128)(2,1)S(1)}, u32[]{:S(2)}) copy-start(bf16[32,16,128]{2,1,0:T(8,128)(2,1)S(1)} %all-to-all-done.1.refs_0_) | copy-start | bytes 393220
  24.4 22.6 %all-to-all-start = ((bf16[64,32,128]{2,1,0:T(8,128)(2,1)}), bf16[64,32,128]{2,1,0:T(8,128)(2,1)S(1)}, u32[]{:S(2)}, u32[]{:S(2)}) async-start(bf16[64,32,128]{2,1,0:T(8,128)(2,1)} %halo_pack.1), calls=%async_computation | async-start | bytes 1048576 | tf_op jit(solution)/shard_map/all_to_all | solution.py:731
  29.9 6.8 %collective-permute-start = (bf16[32,16,128]{2,1,0:T(8,128)(2,1)S(1)}, bf16[32,16,128]{2,1,0:T(8,128)(2,1)S(1)}, u32[]{:S(2)}, u32[]{:S(2)}) collective-permute-start(bf16[32,16,128]{2,1,0:T(8,128)(2,1)S(1)} %all-to-all-done.1.refs_0_), channel_id=1, source_target_pairs={{0,1},{1,2},{2,3},{3,0},{4,5},{5,6},{6,7},{7,4},{8,9},{9,10},{10,1... | collective-permute-start | bytes 393224 | tf_op jit(solution)/shard_map/ppermute | solution.py:723
  31.5 9.1 %collective-permute-start.1 = (bf16[32,16,128]{2,1,0:T(8,128)(2,1)S(1)}, bf16[32,16,128]{2,1,0:T(8,128)(2,1)S(1)}, u32[]{:S(2)}, u32[]{:S(2)}) collective-permute-start(bf16[32,16,128]{2,1,0:T(8,128)(2,1)S(1)} %all-to-all-done.1.refs_0_), channel_id=1, source_target_pairs={{0,2},{1,3},{2,0},{3,1},{4,6},{5,7},{6,4},{7,5},{8,10},{9,11},{10,... | collective-permute-start | bytes 393224 | tf_op jit(solution)/shard_map/ppermute | solution.py:723
  34.2 6.3 %collective-permute-start.2 = (bf16[32,16,128]{2,1,0:T(8,128)(2,1)S(1)}, bf16[32,16,128]{2,1,0:T(8,128)(2,1)S(1)}, u32[]{:S(2)}, u32[]{:S(2)}) collective-permute-start(bf16[32,16,128]{2,1,0:T(8,128)(2,1)S(1)} %all-to-all-done.1.refs_0_), channel_id=1, source_target_pairs={{0,3},{1,0},{2,1},{3,2},{4,7},{5,4},{6,5},{7,6},{8,11},{9,8},{10,9... | collective-permute-start | bytes 393224 | tf_op jit(solution)/shard_map/ppermute | solution.py:723
  35.7 6.1 %collective-permute-start.3 = (bf16[32,16,128]{2,1,0:T(8,128)(2,1)S(1)}, bf16[32,16,128]{2,1,0:T(8,128)(2,1)S(1)}, u32[]{:S(2)}, u32[]{:S(2)}) collective-permute-start(bf16[32,16,128]{2,1,0:T(8,128)(2,1)S(1)} %all-to-all-done.1.refs_0_), channel_id=1, source_target_pairs={{0,4},{4,0},{1,5},{5,1},{2,6},{6,2},{3,7},{7,3},{8,12},{12,8},{9,1... | collective-permute-start | bytes 393224 | tf_op jit(solution)/shard_map/ppermute | solution.py:727
  36.8 10.3 %copy-start.7 = (bf16[32,16,128]{2,1,0:T(8,128)(2,1)}, bf16[32,16,128]{2,1,0:T(8,128)(2,1)S(1)}, u32[]{:S(2)}) copy-start(bf16[32,16,128]{2,1,0:T(8,128)(2,1)S(1)} %collective-permute-done.refs_1_) | copy-start | bytes 393220
  36.8 5.0 %collective-permute-start.4 = (bf16[32,16,128]{2,1,0:T(8,128)(2,1)S(1)}, bf16[32,16,128]{2,1,0:T(8,128)(2,1)S(1)}, u32[]{:S(2)}, u32[]{:S(2)}) collective-permute-start(bf16[32,16,128]{2,1,0:T(8,128)(2,1)S(1)} %collective-permute-done.refs_1_), channel_id=1, source_target_pairs={{0,4},{4,0},{1,5},{5,1},{2,6},{6,2},{3,7},{7,3},{8,12},{12,8},{9,1... | collective-permute-start | bytes 393224 | tf_op jit(solution)/shard_map/ppermute | solution.py:727
  40.6 6.5 %copy-start.8 = (bf16[32,16,128]{2,1,0:T(8,128)(2,1)}, bf16[32,16,128]{2,1,0:T(8,128)(2,1)S(1)}, u32[]{:S(2)}) copy-start(bf16[32,16,128]{2,1,0:T(8,128)(2,1)S(1)} %collective-permute-done.1.refs_2_) | copy-start | bytes 393220
  40.6 1.3 %collective-permute-start.5 = (bf16[32,16,128]{2,1,0:T(8,128)(2,1)S(1)}, bf16[32,16,128]{2,1,0:T(8,128)(2,1)S(1)}, u32[]{:S(2)}, u32[]{:S(2)}) collective-permute-start(bf16[32,16,128]{2,1,0:T(8,128)(2,1)S(1)} %collective-permute-done.1.refs_2_), channel_id=1, source_target_pairs={{0,4},{4,0},{1,5},{5,1},{2,6},{6,2},{3,7},{7,3},{8,12},{12,8},{9,1... | collective-permute-start | bytes 393224 | tf_op jit(solution)/shard_map/ppermute | solution.py:727
  40.6 6.5 %copy-start.9 = (bf16[32,16,128]{2,1,0:T(8,128)(2,1)}, bf16[32,16,128]{2,1,0:T(8,128)(2,1)S(1)}, u32[]{:S(2)}) copy-start(bf16[32,16,128]{2,1,0:T(8,128)(2,1)S(1)} %collective-permute-done.2.refs_3_) | copy-start | bytes 393220
  40.6 1.5 %collective-permute-start.6 = (bf16[32,16,128]{2,1,0:T(8,128)(2,1)S(1)}, bf16[32,16,128]{2,1,0:T(8,128)(2,1)S(1)}, u32[]{:S(2)}, u32[]{:S(2)}) collective-permute-start(bf16[32,16,128]{2,1,0:T(8,128)(2,1)S(1)} %collective-permute-done.2.refs_3_), channel_id=1, source_target_pairs={{0,4},{4,0},{1,5},{5,1},{2,6},{6,2},{3,7},{7,3},{8,12},{12,8},{9,1... | collective-permute-start | bytes 393224 | tf_op jit(solution)/shard_map/ppermute | solution.py:727
  41.7 5.3 %copy-start.10 = (bf16[32,16,128]{2,1,0:T(8,128)(2,1)}, bf16[32,16,128]{2,1,0:T(8,128)(2,1)S(1)}, u32[]{:S(2)}) copy-start(bf16[32,16,128]{2,1,0:T(8,128)(2,1)S(1)} %collective-permute-done.3.refs_4_) | copy-start | bytes 393220
  41.8 5.3 %copy-start.11 = (bf16[32,16,128]{2,1,0:T(8,128)(2,1)}, bf16[32,16,128]{2,1,0:T(8,128)(2,1)S(1)}, u32[]{:S(2)}) copy-start(bf16[32,16,128]{2,1,0:T(8,128)(2,1)S(1)} %collective-permute-done.4.refs_5_) | copy-start | bytes 393220
  41.9 5.2 %copy-start.12 = (bf16[32,16,128]{2,1,0:T(8,128)(2,1)}, bf16[32,16,128]{2,1,0:T(8,128)(2,1)S(1)}, u32[]{:S(2)}) copy-start(bf16[32,16,128]{2,1,0:T(8,128)(2,1)S(1)} %collective-permute-done.5.refs_6_) | copy-start | bytes 393220
  42.1 5.0 %copy-start.13 = (bf16[32,16,128]{2,1,0:T(8,128)(2,1)}, bf16[32,16,128]{2,1,0:T(8,128)(2,1)S(1)}, u32[]{:S(2)}) copy-start(bf16[32,16,128]{2,1,0:T(8,128)(2,1)S(1)} %collective-permute-done.6.refs_7_) | copy-start | bytes 393220
  47.0 0.8 copy-start.5
  57.1 16.7 %all-to-all-start.2 = ((bf16[32,16,128]{2,1,0:T(8,128)(2,1)}), bf16[32,16,128]{2,1,0:T(8,128)(2,1)S(1)}, u32[]{:S(2)}, u32[]{:S(2)}) async-start(bf16[32,16,128]{2,1,0:T(8,128)(2,1)} %bitcast.6), calls=%async_computation.2 | async-start | bytes 262144 | tf_op jit(solution)/shard_map/all_to_all | solution.py:731
  73.8 23.1 %all-to-all-start.4 = ((bf16[64,32,128]{2,1,0:T(8,128)(2,1)}), bf16[64,32,128]{2,1,0:T(8,128)(2,1)S(1)}, u32[]{:S(2)}, u32[]{:S(2)}) async-start(bf16[64,32,128]{2,1,0:T(8,128)(2,1)} %get-tuple-element.33), calls=%async_computation.4 | async-start | bytes 1048576 | tf_op jit(solution)/shard_map/all_to_all | solution.py:731
  78.8 2.2 %collective-permute-start.7 = (bf16[4,32,16,128]{3,2,1,0:T(8,128)(2,1)}, bf16[4,32,16,128]{3,2,1,0:T(8,128)(2,1)S(1)}, u32[]{:S(2)}, u32[]{:S(2)}) collective-permute-start(bf16[4,32,16,128]{3,2,1,0:T(8,128)(2,1)} %get-tuple-element.24), channel_id=1, source_target_pairs={{0,4},{4,0},{1,5},{5,1},{2,6},{6,2},{3,7},{7,3},{8,12},{12,8},{9,1... | collective-permute-start | bytes 1572872 | tf_op jit(solution)/shard_map/ppermute | solution.py:727
  79.2 1.6 %collective-permute-start.8 = (bf16[2,16,128]{2,1,0:T(8,128)(2,1)S(1)}, bf16[2,16,128]{2,1,0:T(8,128)(2,1)S(1)}, u32[]{:S(2)}, u32[]{:S(2)}) collective-permute-start(bf16[2,16,128]{2,1,0:T(8,128)(2,1)S(1)} %fold.1.w_near), channel_id=1, source_target_pairs={{0,4},{4,0},{1,5},{5,1},{2,6},{6,2},{3,7},{7,3},{8,12},{12,8},{9,1... | collective-permute-start | bytes 24584 | tf_op jit(solution)/shard_map/ppermute | solution.py:727
  81.0 1.0 copy-start
  82.4 0.6 copy-start.1
  83.0 12.2 %collective-permute-start.9 = (bf16[34,16,128]{2,1,0:T(8,128)(2,1)S(1)}, bf16[34,16,128]{2,1,0:T(8,128)(2,1)S(1)}, u32[]{:S(2)}, u32[]{:S(2)}) collective-permute-start(bf16[34,16,128]{2,1,0:T(8,128)(2,1)S(1)} %get-tuple-element.27), channel_id=1, source_target_pairs={{0,1},{1,2},{2,3},{3,0},{4,5},{5,6},{6,7},{7,4},{8,9},{9,10},{10,1... | collective-permute-start | bytes 417800 | tf_op jit(solution)/shard_map/ppermute | solution.py:723
  85.5 9.7 %collective-permute-start.10 = (bf16[34,16,128]{2,1,0:T(8,128)(2,1)S(1)}, bf16[34,16,128]{2,1,0:T(8,128)(2,1)S(1)}, u32[]{:S(2)}, u32[]{:S(2)}) collective-permute-start(bf16[34,16,128]{2,1,0:T(8,128)(2,1)S(1)} %get-tuple-element.28), channel_id=1, source_target_pairs={{0,2},{1,3},{2,0},{3,1},{4,6},{5,7},{6,4},{7,5},{8,10},{9,11},{10,... | collective-permute-start | bytes 417800 | tf_op jit(solution)/shard_map/ppermute | solution.py:723
  88.1 7.1 %collective-permute-start.11 = (bf16[34,16,128]{2,1,0:T(8,128)(2,1)S(1)}, bf16[34,16,128]{2,1,0:T(8,128)(2,1)S(1)}, u32[]{:S(2)}, u32[]{:S(2)}) collective-permute-start(bf16[34,16,128]{2,1,0:T(8,128)(2,1)S(1)} %get-tuple-element.29), channel_id=1, source_target_pairs={{0,3},{1,0},{2,1},{3,2},{4,7},{5,4},{6,5},{7,6},{8,11},{9,8},{10,9... | collective-permute-start | bytes 417800 | tf_op jit(solution)/shard_map/ppermute | solution.py:723
  88.9 17.5 %copy-start.14 = (s32[64,32]{0,1:T(8,128)S(1)}, s32[64,32]{0,1:T(8,128)}, u32[]{:S(2)}) copy-start(s32[64,32]{0,1:T(8,128)} %param.16) | copy-start | bytes 24580
  88.9 17.5 %copy-start.15 = (s32[64]{0:T(128)S(1)}, s32[64]{0:T(128)}, u32[]{:S(2)}) copy-start(s32[64]{0:T(128)} %send_counts.1) | copy-start | bytes 772
  95.2 0.7 copy-start.2
  96.9 10.3 %copy-start.4 = (bf16[64,32,128]{2,1,0:T(8,128)(2,1)}, bf16[64,32,128]{2,1,0:T(8,128)(2,1)S(1)}, u32[]{:S(2)}) copy-start(bf16[64,32,128]{2,1,0:T(8,128)(2,1)S(1)} %all-to-all-done.4.received) | copy-start | bytes 1572868
  96.9 21.5 %all-to-all-start.3 = ((bf16[32,32,128]{2,1,0:T(8,128)(2,1)}), bf16[32,32,128]{2,1,0:T(8,128)(2,1)S(1)}, u32[]{:S(2)}, u32[]{:S(2)}) async-start(bf16[32,32,128]{2,1,0:T(8,128)(2,1)} %merge.1), calls=%async_computation.3 | async-start | bytes 524288 | tf_op jit(solution)/shard_map/all_to_all | solution.py:731
  107.2 11.2 %copy-start.3 = (s32[16]{0:T(128)S(1)}, s32[16]{0:T(128)}, u32[]{:S(2)}) copy-start(s32[16]{0:T(128)} %hub_rows.3) | copy-start | bytes 196

commit v5 on v4

--- a/solution.py
+++ b/solution.py
@@ -16,10 +16,9 @@
 TILE = 8
 PARTS = 4
 WHOLE = 60
-FORWARD = 60
-SCATTER = 60
 FINISH = 16
-TOKEN = jax.ShapeDtypeStruct((8, 128), F32)
+FOLDS = 4
+FOLD_ROWS = 512
 REPS = 4
 CORES = 2
 GROUP = "group"
@@ -310,7 +309,7 @@
             pltpu.SemaphoreType.DMA((5 + parts,)),
             pltpu.SemaphoreType.DMA((3,)),
         ],
-        compiler_params=params(FORWARD),
+        compiler_params=params(WHOLE),
         name="forward",
     )(targets, sources, count, weights, features, halo, *hubs, out_grad, w_self, w_nbr)
 
@@ -467,29 +466,44 @@
     )(targets, sources, count, weights, grad_agg)
 
 
-def backward_own_kernel(
+def own_rows_kernel(
     targets,
     sources,
     count,
+    hub_rows,
     weights,
     grad_agg,
     grad_self,
-    after,
-    grad_own,
-    token,
+    returned,
+    ids_across,
+    ids_down,
+    out,
+    near,
     order,
     held,
     agg,
     totals,
+    scattered,
+    rows,
+    spread,
     weight_sems,
     sems,
+    out_sems,
 ):
     block = weights.shape[1]
     node_rows, width = grad_agg.shape
     own_blocks = node_rows // block
+    slots = returned.shape[0]
+    folded = node_rows // FOLDS
     copies = [
-        pltpu.make_async_copy(grad_agg, agg, sems.at[0]),
-        pltpu.make_async_copy(grad_self, totals.at[pl.ds(0, node_rows)], sems.at[1]),
+        pltpu.make_async_copy(x, y, sems.at[n])
+        for n, (x, y) in enumerate(
+            (
+                (returned, rows),
+                (grad_agg, agg),
+                (grad_self, totals.at[pl.ds(0, node_rows)]),
+            )
+        )
     ]
     for copy in copies:
         copy.start()
@@ -498,7 +512,30 @@
     start_weights(0, chunks, weights, held, weight_sems)
     totals[node_rows:] = jnp.zeros((block, width), F32)
     found = collect(live, lambda t: sources[t] < own_blocks, order)
-    for copy in copies:
+    down = jnp.concatenate(
+        [ids_down[...], jnp.zeros((block - ids_down.shape[0], block), F32)], 0
+    ).T
+    copies[0].wait()
+    for j in range(slots // block):
+        part = pl.ds(j * block, block)
+        fold = jnp.broadcast_to(down[:, j : j + 1], (block, width))
+        value = rows[part].astype(F32)
+        for q in range(FOLDS):
+            inside = (fold >= q * folded) & (fold < (q + 1) * folded)
+            spread[part, pl.ds(q * width, width)] = jnp.where(inside, value, 0.0).astype(BF16)
+    across = ids_across[...] % folded
+    steps = folded // FOLD_ROWS
+
+    def spots(c):
+        return [pl.ds(q * folded + c * FOLD_ROWS, FOLD_ROWS) for q in range(FOLDS)]
+
+    for c in range(steps):
+        ids = lax.broadcasted_iota(jnp.int32, (FOLD_ROWS, slots), 0) + c * FOLD_ROWS
+        hot = (ids == across).astype(F32).astype(BF16)
+        added = jnp.dot(hot, spread[...], preferred_element_type=F32)
+        for q, at in enumerate(spots(c)):
+            scattered[at] = added[:, q * width : (q + 1) * width]
+    for copy in copies[1:]:
         copy.wait()
     add_tiles(
         found,
@@ -512,31 +549,60 @@
         own_blocks,
         lambda n: weight_copy(n, weights, held, weight_sems).wait(),
     )
-    out = pltpu.make_async_copy(totals.at[pl.ds(0, node_rows)], grad_own, sems.at[0])
-    out.start()
-    token[...] = jnp.zeros_like(token)
-    out.wait()
-
-
-def backward_own(targets, sources, count, weights, grad_agg, grad_self, after):
+    outs = []
+    for c in range(steps):
+        for q, at in enumerate(spots(c)):
+            totals[at] += scattered[at]
+            outs.append(pltpu.make_async_copy(totals.at[at], out.at[at], out_sems.at[c, q]))
+            outs[-1].start()
+    for h in range(hub_rows.shape[0]):
+        near[pl.ds(h * TILE, TILE)] = totals[rows_at(hub_rows[h] // TILE, TILE)]
+
+    for copy in outs:
+        copy.wait()
+
+
+def own_rows(
+    targets, sources, count, hub_rows, weights, grad_agg, grad_self, returned, send_ids
+):
     node_rows, width = grad_agg.shape
     tiles, block, _ = weights.shape
+    hubs = hub_rows.shape[0]
+    slots = returned.shape[0] * returned.shape[1]
     return pl.pallas_call(
-        backward_own_kernel,
-        out_shape=(jax.ShapeDtypeStruct((node_rows, width), F32), TOKEN),
-        in_specs=[smem()] * 3 + [hbm()] * 4,
+        own_rows_kernel,
+        out_shape=(
+            jax.ShapeDtypeStruct((node_rows, width), F32),
+            jax.ShapeDtypeStruct((hubs * TILE, width), F32),
+        ),
+        in_specs=[smem()] * 4 + [hbm()] * 4 + [vmem()] * 2,
         out_specs=(hbm(), vmem()),
         scratch_shapes=[
             pltpu.SMEM((tiles + CHUNK,), jnp.int32),
             pltpu.VMEM((tiles, block, block), BF16),
             pltpu.VMEM((node_rows, width), BF16),
             pltpu.VMEM((node_rows + block, width), F32),
+            pltpu.VMEM((node_rows, width), F32),
+            pltpu.VMEM((slots, width), BF16),
+            pltpu.VMEM((slots, FOLDS * width), BF16),
             pltpu.SemaphoreType.DMA((tiles // CHUNK,)),
-            pltpu.SemaphoreType.DMA((2,)),
+            pltpu.SemaphoreType.DMA((3,)),
+            pltpu.SemaphoreType.DMA((node_rows // FOLDS // FOLD_ROWS, FOLDS)),
         ],
         compiler_params=params(WHOLE),
-        name="backward_own",
-    )(targets, sources, count, weights, grad_agg, grad_self, after)
+        name="own_rows",
+    )(
+        targets,
+        sources,
+        count,
+        hub_rows,
+        weights,
+        grad_agg,
+        grad_self,
+        returned.reshape(slots, width),
+        send_ids.reshape(1, slots),
+        send_ids.reshape(slots // block, block).astype(F32),
+    )
 
 
 def split_pair(total):
@@ -564,8 +630,6 @@
 
 
 def join_kernel(near, far, w_near, w_far, *outs):
-    *outs, token = outs
-    token[...] = jnp.zeros_like(token)
     groups = near.shape[1]
     total = (w_near[0].astype(F32) + w_near[1].astype(F32)) + (
         w_far[0].astype(F32) + w_far[1].astype(F32)
@@ -588,15 +652,15 @@
     piece = jax.ShapeDtypeStruct((groups + 2, hubs, width), BF16)
     return pl.pallas_call(
         join_kernel,
-        out_shape=(piece,) * reps + (TOKEN,),
+        out_shape=(piece,) * reps,
         in_specs=[vmem()] * 4,
-        out_specs=(vmem(),) * (reps + 1),
+        out_specs=(vmem(),) * reps,
         compiler_params=params(8),
         name="join",
     )(near, far, w_near, w_far)
 
 
-def merge_kernel(hub0, hub1, hub2, hub3, after, out, w_parts):
+def merge_kernel(hub0, hub1, hub2, hub3, out, w_parts):
     groups, message, width = out.shape
     hubs = hub0.shape[1]
     rep = lax.axis_index("rep")
@@ -617,69 +681,35 @@
     lax.fori_loop(0, groups, group, 0)
 
 
-def merge(pieces, after):
+def merge(pieces):
     groups, hubs, width = pieces[0].shape
     return pl.pallas_call(
         merge_kernel,
         out_shape=jax.ShapeDtypeStruct((groups - 2, 2 * hubs, width), BF16),
-        in_specs=[vmem()] * 4 + [hbm()],
+        in_specs=[vmem()] * 4,
         out_specs=vmem(),
         scratch_shapes=[pltpu.VMEM((REPS, hubs, width), F32)],
         compiler_params=params(8),
         name="merge",
-    )(*pieces, after)
-
-
-def scatter_kernel(send_ids, received, grad_own, out):
-    peers, slots, width = received.shape
-    rows = received[...].reshape(peers * slots, width)
-
-    def scatter(c, carry):
-        at = rows_at(c, ROWS)
-        ids = lax.broadcasted_iota(jnp.int32, (ROWS, peers * slots), 0) + c * ROWS
-        hot = (ids == send_ids[...]).astype(F32).astype(BF16)
-        out[at] = grad_own[at] + jnp.dot(hot, rows, preferred_element_type=F32)
-        return carry
-
-    lax.fori_loop(0, out.shape[0] // ROWS, scatter, 0)
-
-
-def scatter(send_ids, received, grad_own):
-    return pl.pallas_call(
-        scatter_kernel,
-        out_shape=jax.ShapeDtypeStruct(grad_own.shape, F32),
-        in_specs=[vmem()] * 3,
-        out_specs=vmem(),
-        compiler_params=params(SCATTER),
-        name="scatter",
-    )(send_ids, received, grad_own)
-
-
-def finish(hub_rows, received, grad_nodes, hidden_width, grad_scale):
+    )(*pieces)
+
+
+def finish(hub_rows, received, around, grad_nodes, hidden_width, grad_scale):
     groups, message, width = received.shape
     hubs = hub_rows.shape[0]
     w_rows = message - hubs
 
-    def body(hub_rows, received, grad_nodes, out, grad_self, grad_nbr, near, held, sems):
+    def body(
+        hub_rows, received, around, grad_nodes, out, grad_self, grad_nbr, near, held, sems
+    ):
         at = [hub_rows[h] // TILE for h in range(hubs)]
-        for h in range(hubs):
-            pltpu.make_async_copy(
-                grad_nodes.at[rows_at(at[h], TILE)], near.at[pl.ds(h * TILE, TILE)], sems.at[h]
-            ).start()
+        near[...] = around[...]
 
         def place(p, total):
             held[rows_at(p, w_rows)] = received[p, hubs:].astype(F32) * grad_scale
             return total + received[p, :hubs].astype(F32)
 
         total = lax.fori_loop(0, groups, place, jnp.zeros((hubs, width), F32), unroll=4)
-        for k in range(hidden_width // width):
-            columns = pl.ds(k * width, width)
-            grad_self[:, columns] = held[2 * k * width : (2 * k + 1) * width]
-            grad_nbr[:, columns] = held[(2 * k + 1) * width : (2 * k + 2) * width]
-        for h in range(hubs):
-            pltpu.make_async_copy(
-                grad_nodes.at[rows_at(at[h], TILE)], near.at[pl.ds(h * TILE, TILE)], sems.at[h]
-            ).wait()
         first = []
         for h in range(hubs):
             slot = jnp.int32(h)
@@ -696,6 +726,10 @@
 
         for h in range(hubs):
             pl.when(first[h] == h)(back(h).start)
+        for k in range(hidden_width // width):
+            columns = pl.ds(k * width, width)
+            grad_self[:, columns] = held[2 * k * width : (2 * k + 1) * width]
+            grad_nbr[:, columns] = held[(2 * k + 1) * width : (2 * k + 2) * width]
         for h in range(hubs):
             pl.when(first[h] == h)(back(h).wait)
 
@@ -706,9 +740,9 @@
             jax.ShapeDtypeStruct((width, hidden_width), F32),
             jax.ShapeDtypeStruct((width, hidden_width), F32),
         ),
-        in_specs=[smem(), vmem(), hbm()],
+        in_specs=[smem(), vmem(), vmem(), hbm()],
         out_specs=(hbm(), vmem(), vmem()),
-        input_output_aliases={2: 0},
+        input_output_aliases={3: 0},
         scratch_shapes=[
             pltpu.VMEM((hubs * TILE, width), F32),
             pltpu.VMEM((groups * w_rows, width), F32),
@@ -716,7 +750,7 @@
         ],
         compiler_params=params(FINISH),
         name="finish",
-    )(hub_rows, received, grad_nodes)
+    )(hub_rows, received, around, grad_nodes)
 
 
 def rep_shift(value, shift):
@@ -762,18 +796,18 @@
     )
     returned = swap(grad_halo, DOM)
     w_pair = fold(w_slices)
-    *pieces, joined = join(near, core_swap(far), w_pair, core_swap(w_pair))
-    grad_own, own_done = backward_own(
-        tile_targets, tile_sources, tile_count, tile_weights, grad_agg, grad_self, joined
-    )
+    pieces = join(near, core_swap(far), w_pair, core_swap(w_pair))
     pieces = [pieces[0]] + [rep_shift(pieces[i], i) for i in range(1, REPS)]
-    merged = swap(merge(pieces, own_done), GROUP)
+    merged = swap(merge(pieces), GROUP)
     slot_live = jnp.arange(slots, dtype=jnp.int32)[None, :] < send_counts[:, None]
-    send_ids = jnp.where(slot_live, send_rows, node_rows).reshape(1, -1)
-    grad_nodes = scatter(send_ids, returned, grad_own)
+    send_ids = jnp.where(slot_live, send_rows, node_rows)
+    grad_nodes, around = own_rows(
+        tile_targets, tile_sources, tile_count, hub_rows, tile_weights, grad_agg, grad_self,
+        returned, send_ids,
+    )
     grad_scale = 1.0 / math.sqrt(node_rows * peers * REPS)
     grad_features, grad_w_self, grad_w_nbr = finish(
-        hub_rows, merged, grad_nodes, w_self.shape[1], grad_scale
+        hub_rows, merged, around, grad_nodes, w_self.shape[1], grad_scale
     )
     return (hidden, grad_features, grad_w_self, grad_w_nbr)
 

time: 122 us -> 121 us (level)
  Pallas kernels: 40.7 us -> 33.1 us
  waiting for transfers between devices: 24.1 us -> 30.3 us
    pallas_call x3 -> x2, Pallas kernels: 14.8 us -> 7.67 us  [the longest x1 7.36 us: own_rows(): pl.pallas_call(own_rows_kernel, out_shape=(jax.ShapeDtypeStruct((node_row...]
    ppermute x6, waiting for transfers between devices: 4.9 us -> 9.23 us  [rep_shift(): lax.ppermute(value, 'rep', [(j, (j + shift) % REPS) for j in range(REPS)])]
    all_to_all x5, waiting for transfers between devices: 17.5 us -> 19.4 us  [swap(): return lax.all_to_all(value, axes, split_axis=0, concat_axis=0, tiled=True)]
    all_to_all x5, starting transfers between devices: 38.4 us -> 37 us  [swap(): return lax.all_to_all(value, axes, split_axis=0, concat_axis=0, tiled=True)]
    unnamed x32 -> x30, local copies, waits for them, and re-layouts: 3.08 us -> 2.66 us
  transfers between devices with their start and end apart: 17 -> 17, of which waited for: 10 -> 13; matrix products, arithmetic and copies ran while one was open for 1% -> 1% of each run, Pallas kernels for 21% -> 16%
where the time goes in v5:
time: 121 us; the launch traced here: 119 us
  starting transfers between devices  50.1 us (41%)
  Pallas kernels  33.1 us (27%)
  waiting for transfers between devices  30.3 us (25%)
  local copies, waits for them, and re-layouts  4.19 us (3%)
  between operations  1.68 us (1%)
    all_to_all x5, starting transfers between devices, swap(): return lax.all_to_all(value, axes, split_axis=0, concat_axis=0, tiled=True)  37 us
    all_to_all x5, waiting for transfers between devices, swap(): return lax.all_to_all(value, axes, split_axis=0, concat_axis=0, tiled=True)  19.4 us
    ppermute x6, starting transfers between devices, rep_shift(): lax.ppermute(value, 'rep', [(j, (j + shift) % REPS) for j in range(REPS)])  12 us
    pallas_call x1, Pallas kernels, forward(): pl.pallas_call(forward_kernel, out_shape=shapes, in_specs=[smem()] * 3 +...  9.29 us
    ppermute x6, waiting for transfers between devices, rep_shift(): lax.ppermute(value, 'rep', [(j, (j + shift) % REPS) for j in range(REPS)])  9.23 us
    pallas_call x1, Pallas kernels, own_rows(): pl.pallas_call(own_rows_kernel, out_shape=(jax.ShapeDtypeStruct((node_row...  7.36 us
    pallas_call x1, Pallas kernels, halo_pack(): pl.pallas_call(halo_pack_kernel, out_shape=jax.ShapeDtypeStruct((peers, s...  5.1 us
    pallas_call x1, Pallas kernels, backward_far(): pl.pallas_call(backward_far_kernel, out_shape=(halo, piece, piece), in_sp...  5.01 us
  transfers between devices with their start and end apart: 17, of which 13 were waited for; matrix products, arithmetic and copies ran while one was open for 1% of the time, Pallas kernels for 16%

profile of v5, /device:TPU:32, one launch (start us, length us, event | category | flops | bytes accessed | tf_op | source)
XLA Modules:
  0.0 119.4 jit_solution(2202155908225955132)
XLA Ops:
  0.6 2.6 %hub_pack.1 = bf16[32,16,128]{2,1,0:T(8,128)(2,1)} custom-call(s32[16]{0:T(128)} %hub_rows.5, bf16[4096,128]{1,0:T(8,128)(2,1)} %features.3), custom_call_target="tpu_custom_call" | custom-call | tf_op jit(solution)/shard_map/hub_pack/pallas_call | solution.py:77
  3.2 11.4 %all-to-all-start.1 = ((bf16[32,16,128]{2,1,0:T(8,128)(2,1)}), bf16[32,16,128]{2,1,0:T(8,128)(2,1)S(1)}, u32[]{:S(2)}, u32[]{:S(2)}) async-start(bf16[32,16,128]{2,1,0:T(8,128)(2,1)} %hub_pack.1), calls=%async_computation.1 | async-start | bytes 262144 | tf_op jit(solution)/shard_map/all_to_all | solution.py:765
  14.6 5.1 %halo_pack.1 = bf16[64,32,128]{2,1,0:T(8,128)(2,1)} custom-call(s32[32,64]{1,0:T(8,128)} %bitcast.9, s32[64]{0:T(128)} %send_counts.1, bf16[4096,128]{1,0:T(8,128)(2,1)} %features.3), custom_call_target="tpu_custom_call" | custom-call | tf_op jit(solution)/shard_map/halo_pack/pallas_call | solution.py:115
  19.7 4.7 %all-to-all-done.1.refs_0_ = bf16[32,16,128]{2,1,0:T(8,128)(2,1)S(1)} async-done(((bf16[32,16,128]{2,1,0:T(8,128)(2,1)}), bf16[32,16,128]{2,1,0:T(8,128)(2,1)S(1)}, u32[]{:S(2)}, u32[]{:S(2)}) %all-to-all-start.1) | async-done | bytes 131104 | tf_op jit(solution)/shard_map/all_to_all | solution.py:765
  24.4 5.5 %all-to-all-start = ((bf16[64,32,128]{2,1,0:T(8,128)(2,1)}), bf16[64,32,128]{2,1,0:T(8,128)(2,1)S(1)}, u32[]{:S(2)}, u32[]{:S(2)}) async-start(bf16[64,32,128]{2,1,0:T(8,128)(2,1)} %halo_pack.1), calls=%async_computation | async-start | bytes 1048576 | tf_op jit(solution)/shard_map/all_to_all | solution.py:765
  29.9 1.6 %collective-permute-start = (bf16[32,16,128]{2,1,0:T(8,128)(2,1)S(1)}, bf16[32,16,128]{2,1,0:T(8,128)(2,1)S(1)}, u32[]{:S(2)}, u32[]{:S(2)}) collective-permute-start(bf16[32,16,128]{2,1,0:T(8,128)(2,1)S(1)} %all-to-all-done.1.refs_0_), channel_id=1, source_target_pairs={{0,1},{1,2},{2,3},{3,0},{4,5},{5,6},{6,7},{7,4},{8,9},{9,10},{10,1... | collective-permute-start | bytes 393224 | tf_op jit(solution)/shard_map/ppermute | solution.py:757
  31.5 2.7 %collective-permute-start.1 = (bf16[32,16,128]{2,1,0:T(8,128)(2,1)S(1)}, bf16[32,16,128]{2,1,0:T(8,128)(2,1)S(1)}, u32[]{:S(2)}, u32[]{:S(2)}) collective-permute-start(bf16[32,16,128]{2,1,0:T(8,128)(2,1)S(1)} %all-to-all-done.1.refs_0_), channel_id=1, source_target_pairs={{0,2},{1,3},{2,0},{3,1},{4,6},{5,7},{6,4},{7,5},{8,10},{9,11},{10,... | collective-permute-start | bytes 393224 | tf_op jit(solution)/shard_map/ppermute | solution.py:757
  34.2 1.4 %collective-permute-start.2 = (bf16[32,16,128]{2,1,0:T(8,128)(2,1)S(1)}, bf16[32,16,128]{2,1,0:T(8,128)(2,1)S(1)}, u32[]{:S(2)}, u32[]{:S(2)}) collective-permute-start(bf16[32,16,128]{2,1,0:T(8,128)(2,1)S(1)} %all-to-all-done.1.refs_0_), channel_id=1, source_target_pairs={{0,3},{1,0},{2,1},{3,2},{4,7},{5,4},{6,5},{7,6},{8,11},{9,8},{10,9... | collective-permute-start | bytes 393224 | tf_op jit(solution)/shard_map/ppermute | solution.py:757
  35.7 0.0 collective-permute-start.3
  35.7 1.1 collective-permute-done.refs_1_
  36.8 3.8 %collective-permute-done.1.refs_2_ = bf16[32,16,128]{2,1,0:T(8,128)(2,1)S(1)} collective-permute-done((bf16[32,16,128]{2,1,0:T(8,128)(2,1)S(1)}, bf16[32,16,128]{2,1,0:T(8,128)(2,1)S(1)}, u32[]{:S(2)}, u32[]{:S(2)}) %collective-permute-start.1) | collective-permute-done | bytes 131104 | tf_op jit(solution)/shard_map/ppermute | solution.py:757
  40.6 0.0 collective-permute-start.5
  40.6 0.0 collective-permute-done.2.refs_3_
  40.6 0.5 collective-permute-start.6
  41.8 0.1 collective-permute-done.5.refs_6_
  41.9 0.2 collective-permute-done.6.refs_7_
  42.1 4.9 %all-to-all-done = bf16[64,32,128]{2,1,0:T(8,128)(2,1)S(1)} async-done(((bf16[64,32,128]{2,1,0:T(8,128)(2,1)}), bf16[64,32,128]{2,1,0:T(8,128)(2,1)S(1)}, u32[]{:S(2)}, u32[]{:S(2)}) %all-to-all-start) | async-done | bytes 524320 | tf_op jit(solution)/shard_map/all_to_all | solution.py:765
  47.1 0.7 copy-done.4
  47.8 9.3 %forward.1 = (bf16[4096,256]{1,0:T(8,128)(2,1)}, bf16[4096,128]{1,0:T(8,128)(2,1)}, f32[4096,128]{1,0:T(8,128)}, bf16[512,128]{1,0:T(8,128)(2,1)}) custom-call(s32[128]{0:T(128)} %targets.5, s32[128]{0:T(128)} %sources.5, s32[1]{0:T(128)S(6)} %copy.21.count, bf16[128,128,128]{2,1,0:T(8,128)(2,1)} %weights.5, bf16[32,8,16,128]{3,2,1,0:T(8,128)(2,1)} %bitcast.5, ...), custom_call_target="tpu_custom_call" | custom-call | tf_op jit(solution)/shard_map/forward/pallas_call | solution.py:293
  57.1 6.5 %all-to-all-start.2 = ((bf16[32,16,128]{2,1,0:T(8,128)(2,1)}), bf16[32,16,128]{2,1,0:T(8,128)(2,1)S(1)}, u32[]{:S(2)}, u32[]{:S(2)}) async-start(bf16[32,16,128]{2,1,0:T(8,128)(2,1)} %bitcast.8), calls=%async_computation.2 | async-start | bytes 262144 | tf_op jit(solution)/shard_map/all_to_all | solution.py:765
  63.7 5.0 %backward_far.1 = (bf16[64,32,128]{2,1,0:T(8,128)(2,1)}, bf16[4,32,16,128]{3,2,1,0:T(8,128)(2,1)}, bf16[4,32,16,128]{3,2,1,0:T(8,128)(2,1)}) custom-call(s32[128]{0:T(128)} %targets.5, s32[128]{0:T(128)} %sources.5, s32[1]{0:T(128)S(6)} %copy.21.count, bf16[128,128,128]{2,1,0:T(8,128)(2,1)} %weights.5, bf16[4096,128]{1,0:T(8,128)(2,1)} %get-tuple-element.21.grad_agg), custom_call_target="tpu_custom_call" | custom-call | tf_op jit(solution)/shard_map/backward_far/pallas_call | solution.py:448
  68.7 0.0 copy-start.13
  68.7 0.0 copy-start.14
  68.7 4.6 %all-to-all-done.2.slices = bf16[32,16,128]{2,1,0:T(8,128)(2,1)S(1)} async-done(((bf16[32,16,128]{2,1,0:T(8,128)(2,1)}), bf16[32,16,128]{2,1,0:T(8,128)(2,1)S(1)}, u32[]{:S(2)}, u32[]{:S(2)}) %all-to-all-start.2) | async-done | bytes 131104 | tf_op jit(solution)/shard_map/all_to_all | solution.py:765
  73.3 5.6 %all-to-all-start.4 = ((bf16[64,32,128]{2,1,0:T(8,128)(2,1)}), bf16[64,32,128]{2,1,0:T(8,128)(2,1)S(1)}, u32[]{:S(2)}, u32[]{:S(2)}) async-start(bf16[64,32,128]{2,1,0:T(8,128)(2,1)} %get-tuple-element.30), calls=%async_computation.4 | async-start | bytes 1048576 | tf_op jit(solution)/shard_map/all_to_all | solution.py:765
  79.0 0.2 collective-permute-start.7
  79.2 0.2 fold.1.w_near
  79.4 0.4 collective-permute-start.8
  79.8 1.2 collective-permute-done.8.w_far
  81.0 0.2 collective-permute-done.7.far
  81.2 1.0 copy-done
  82.2 0.3 join.1
  82.5 2.4 %collective-permute-start.9 = (bf16[34,16,128]{2,1,0:T(8,128)(2,1)S(1)}, bf16[34,16,128]{2,1,0:T(8,128)(2,1)S(1)}, u32[]{:S(2)}, u32[]{:S(2)}) collective-permute-start(bf16[34,16,128]{2,1,0:T(8,128)(2,1)S(1)} %get-tuple-element.26), channel_id=1, source_target_pairs={{0,1},{1,2},{2,3},{3,0},{4,5},{5,6},{6,7},{7,4},{8,9},{9,10},{10,1... | collective-permute-start | bytes 417800 | tf_op jit(solution)/shard_map/ppermute | solution.py:757
  84.9 1.5 %collective-permute-start.10 = (bf16[34,16,128]{2,1,0:T(8,128)(2,1)S(1)}, bf16[34,16,128]{2,1,0:T(8,128)(2,1)S(1)}, u32[]{:S(2)}, u32[]{:S(2)}) collective-permute-start(bf16[34,16,128]{2,1,0:T(8,128)(2,1)S(1)} %get-tuple-element.27), channel_id=1, source_target_pairs={{0,2},{1,3},{2,0},{3,1},{4,6},{5,7},{6,4},{7,5},{8,10},{9,11},{10,... | collective-permute-start | bytes 417800 | tf_op jit(solution)/shard_map/ppermute | solution.py:757
  86.4 2.4 %collective-permute-start.11 = (bf16[34,16,128]{2,1,0:T(8,128)(2,1)S(1)}, bf16[34,16,128]{2,1,0:T(8,128)(2,1)S(1)}, u32[]{:S(2)}, u32[]{:S(2)}) collective-permute-start(bf16[34,16,128]{2,1,0:T(8,128)(2,1)S(1)} %get-tuple-element.28), channel_id=1, source_target_pairs={{0,3},{1,0},{2,1},{3,2},{4,7},{5,4},{6,5},{7,6},{8,11},{9,8},{10,9... | collective-permute-start | bytes 417800 | tf_op jit(solution)/shard_map/ppermute | solution.py:757
  88.8 0.8 collective-permute-done.9.hub1
  89.5 3.6 %collective-permute-done.10.hub2 = bf16[34,16,128]{2,1,0:T(8,128)(2,1)S(1)} collective-permute-done((bf16[34,16,128]{2,1,0:T(8,128)(2,1)S(1)}, bf16[34,16,128]{2,1,0:T(8,128)(2,1)S(1)}, u32[]{:S(2)}, u32[]{:S(2)}) %collective-permute-start.10) | collective-permute-done | bytes 139296 | tf_op jit(solution)/shard_map/ppermute | solution.py:757
  93.1 1.0 merge.1
  94.1 2.0 %all-to-all-done.4 = bf16[64,32,128]{2,1,0:T(8,128)(2,1)S(1)} async-done(((bf16[64,32,128]{2,1,0:T(8,128)(2,1)}), bf16[64,32,128]{2,1,0:T(8,128)(2,1)S(1)}, u32[]{:S(2)}, u32[]{:S(2)}) %all-to-all-start.4) | async-done | bytes 524320 | tf_op jit(solution)/shard_map/all_to_all | solution.py:765
  96.1 7.9 %all-to-all-start.3 = ((bf16[32,32,128]{2,1,0:T(8,128)(2,1)}), bf16[32,32,128]{2,1,0:T(8,128)(2,1)S(1)}, u32[]{:S(2)}, u32[]{:S(2)}) async-start(bf16[32,32,128]{2,1,0:T(8,128)(2,1)} %merge.1), calls=%async_computation.3 | async-start | bytes 524288 | tf_op jit(solution)/shard_map/all_to_all | solution.py:765
  104.1 0.1 copy.18
  104.1 0.7 reshape.30.ids_across
  104.8 0.1 copy.19
  104.9 0.7 convert_element_type.6.ids_down
  105.6 7.4 %own_rows.1 = (f32[4096,128]{1,0:T(8,128)}, f32[128,128]{1,0:T(8,128)}) custom-call(s32[128]{0:T(128)} %targets.5, s32[128]{0:T(128)} %sources.5, s32[1]{0:T(128)S(6)} %copy.21.count, s32[16]{0:T(128)} %hub_rows.5, bf16[128,128,128]{2,1,0:T(8,128)(2,1)} %weights.5, bf16[4096,128]{1,0:T(8,128)(2,1)} %get-tuple-element.21.grad_agg, ...), custom_call_target="tpu_custom_call" | custom-call | tf_op jit(solution)/shard_map/own_rows/pallas_call | solution.py:572
  113.0 3.2 %all-to-all-done.3.received = bf16[32,32,128]{2,1,0:T(8,128)(2,1)S(1)} async-done(((bf16[32,32,128]{2,1,0:T(8,128)(2,1)}), bf16[32,32,128]{2,1,0:T(8,128)(2,1)S(1)}, u32[]{:S(2)}, u32[]{:S(2)}) %all-to-all-start.3) | async-done | bytes 262176 | tf_op jit(solution)/shard_map/all_to_all | solution.py:765
  116.1 0.8 copy-done.1
  117.0 2.3 %finish.1 = (f32[4096,128]{1,0:T(8,128)}, f32[128,256]{1,0:T(8,128)}, f32[128,256]{1,0:T(8,128)}) custom-call(s32[16]{0:T(128)S(1)} %copy-done.2, bf16[32,32,128]{2,1,0:T(8,128)(2,1)S(1)} %all-to-all-done.3.received, f32[128,128]{1,0:T(8,128)S(1)} %copy-done.1, f32[4096,128]{1,0:T(8,128)} %get-tuple-element.32.grad_nodes), custom_call_target="tpu_custom_call", output_to_operand_aliasing={{0}: (3, {})} | custom-call | tf_op jit(solution)/shard_map/finish/pallas_call | solution.py:736
  (30 shorter events, 0.1 us)
Async XLA Ops:
  3.2 21.2 %all-to-all-start.1 = ((bf16[32,16,128]{2,1,0:T(8,128)(2,1)}), bf16[32,16,128]{2,1,0:T(8,128)(2,1)S(1)}, u32[]{:S(2)}, u32[]{:S(2)}) async-start(bf16[32,16,128]{2,1,0:T(8,128)(2,1)} %hub_pack.1), calls=%async_computation.1 | async-start | bytes 262144 | tf_op jit(solution)/shard_map/all_to_all | solution.py:765
  24.4 22.6 %copy-start.5 = (bf16[32,16,128]{2,1,0:T(8,128)(2,1)}, bf16[32,16,128]{2,1,0:T(8,128)(2,1)S(1)}, u32[]{:S(2)}) copy-start(bf16[32,16,128]{2,1,0:T(8,128)(2,1)S(1)} %all-to-all-done.1.refs_0_) | copy-start | bytes 393220
  24.4 22.6 %all-to-all-start = ((bf16[64,32,128]{2,1,0:T(8,128)(2,1)}), bf16[64,32,128]{2,1,0:T(8,128)(2,1)S(1)}, u32[]{:S(2)}, u32[]{:S(2)}) async-start(bf16[64,32,128]{2,1,0:T(8,128)(2,1)} %halo_pack.1), calls=%async_computation | async-start | bytes 1048576 | tf_op jit(solution)/shard_map/all_to_all | solution.py:765
  29.9 6.8 %collective-permute-start = (bf16[32,16,128]{2,1,0:T(8,128)(2,1)S(1)}, bf16[32,16,128]{2,1,0:T(8,128)(2,1)S(1)}, u32[]{:S(2)}, u32[]{:S(2)}) collective-permute-start(bf16[32,16,128]{2,1,0:T(8,128)(2,1)S(1)} %all-to-all-done.1.refs_0_), channel_id=1, source_target_pairs={{0,1},{1,2},{2,3},{3,0},{4,5},{5,6},{6,7},{7,4},{8,9},{9,10},{10,1... | collective-permute-start | bytes 393224 | tf_op jit(solution)/shard_map/ppermute | solution.py:757
  31.5 9.1 %collective-permute-start.1 = (bf16[32,16,128]{2,1,0:T(8,128)(2,1)S(1)}, bf16[32,16,128]{2,1,0:T(8,128)(2,1)S(1)}, u32[]{:S(2)}, u32[]{:S(2)}) collective-permute-start(bf16[32,16,128]{2,1,0:T(8,128)(2,1)S(1)} %all-to-all-done.1.refs_0_), channel_id=1, source_target_pairs={{0,2},{1,3},{2,0},{3,1},{4,6},{5,7},{6,4},{7,5},{8,10},{9,11},{10,... | collective-permute-start | bytes 393224 | tf_op jit(solution)/shard_map/ppermute | solution.py:757
  34.2 6.3 %collective-permute-start.2 = (bf16[32,16,128]{2,1,0:T(8,128)(2,1)S(1)}, bf16[32,16,128]{2,1,0:T(8,128)(2,1)S(1)}, u32[]{:S(2)}, u32[]{:S(2)}) collective-permute-start(bf16[32,16,128]{2,1,0:T(8,128)(2,1)S(1)} %all-to-all-done.1.refs_0_), channel_id=1, source_target_pairs={{0,3},{1,0},{2,1},{3,2},{4,7},{5,4},{6,5},{7,6},{8,11},{9,8},{10,9... | collective-permute-start | bytes 393224 | tf_op jit(solution)/shard_map/ppermute | solution.py:757
  35.7 6.1 %collective-permute-start.3 = (bf16[32,16,128]{2,1,0:T(8,128)(2,1)S(1)}, bf16[32,16,128]{2,1,0:T(8,128)(2,1)S(1)}, u32[]{:S(2)}, u32[]{:S(2)}) collective-permute-start(bf16[32,16,128]{2,1,0:T(8,128)(2,1)S(1)} %all-to-all-done.1.refs_0_), channel_id=1, source_target_pairs={{0,4},{4,0},{1,5},{5,1},{2,6},{6,2},{3,7},{7,3},{8,12},{12,8},{9,1... | collective-permute-start | bytes 393224 | tf_op jit(solution)/shard_map/ppermute | solution.py:761
  36.8 10.3 %copy-start.6 = (bf16[32,16,128]{2,1,0:T(8,128)(2,1)}, bf16[32,16,128]{2,1,0:T(8,128)(2,1)S(1)}, u32[]{:S(2)}) copy-start(bf16[32,16,128]{2,1,0:T(8,128)(2,1)S(1)} %collective-permute-done.refs_1_) | copy-start | bytes 393220
  36.8 5.0 %collective-permute-start.4 = (bf16[32,16,128]{2,1,0:T(8,128)(2,1)S(1)}, bf16[32,16,128]{2,1,0:T(8,128)(2,1)S(1)}, u32[]{:S(2)}, u32[]{:S(2)}) collective-permute-start(bf16[32,16,128]{2,1,0:T(8,128)(2,1)S(1)} %collective-permute-done.refs_1_), channel_id=1, source_target_pairs={{0,4},{4,0},{1,5},{5,1},{2,6},{6,2},{3,7},{7,3},{8,12},{12,8},{9,1... | collective-permute-start | bytes 393224 | tf_op jit(solution)/shard_map/ppermute | solution.py:761
  40.6 6.5 %copy-start.7 = (bf16[32,16,128]{2,1,0:T(8,128)(2,1)}, bf16[32,16,128]{2,1,0:T(8,128)(2,1)S(1)}, u32[]{:S(2)}) copy-start(bf16[32,16,128]{2,1,0:T(8,128)(2,1)S(1)} %collective-permute-done.1.refs_2_) | copy-start | bytes 393220
  40.6 1.3 %collective-permute-start.5 = (bf16[32,16,128]{2,1,0:T(8,128)(2,1)S(1)}, bf16[32,16,128]{2,1,0:T(8,128)(2,1)S(1)}, u32[]{:S(2)}, u32[]{:S(2)}) collective-permute-start(bf16[32,16,128]{2,1,0:T(8,128)(2,1)S(1)} %collective-permute-done.1.refs_2_), channel_id=1, source_target_pairs={{0,4},{4,0},{1,5},{5,1},{2,6},{6,2},{3,7},{7,3},{8,12},{12,8},{9,1... | collective-permute-start | bytes 393224 | tf_op jit(solution)/shard_map/ppermute | solution.py:761
  40.6 6.5 %copy-start.8 = (bf16[32,16,128]{2,1,0:T(8,128)(2,1)}, bf16[32,16,128]{2,1,0:T(8,128)(2,1)S(1)}, u32[]{:S(2)}) copy-start(bf16[32,16,128]{2,1,0:T(8,128)(2,1)S(1)} %collective-permute-done.2.refs_3_) | copy-start | bytes 393220
  40.6 1.5 %collective-permute-start.6 = (bf16[32,16,128]{2,1,0:T(8,128)(2,1)S(1)}, bf16[32,16,128]{2,1,0:T(8,128)(2,1)S(1)}, u32[]{:S(2)}, u32[]{:S(2)}) collective-permute-start(bf16[32,16,128]{2,1,0:T(8,128)(2,1)S(1)} %collective-permute-done.2.refs_3_), channel_id=1, source_target_pairs={{0,4},{4,0},{1,5},{5,1},{2,6},{6,2},{3,7},{7,3},{8,12},{12,8},{9,1... | collective-permute-start | bytes 393224 | tf_op jit(solution)/shard_map/ppermute | solution.py:761
  41.7 5.3 %copy-start.9 = (bf16[32,16,128]{2,1,0:T(8,128)(2,1)}, bf16[32,16,128]{2,1,0:T(8,128)(2,1)S(1)}, u32[]{:S(2)}) copy-start(bf16[32,16,128]{2,1,0:T(8,128)(2,1)S(1)} %collective-permute-done.3.refs_4_) | copy-start | bytes 393220
  41.8 5.3 %copy-start.10 = (bf16[32,16,128]{2,1,0:T(8,128)(2,1)}, bf16[32,16,128]{2,1,0:T(8,128)(2,1)S(1)}, u32[]{:S(2)}) copy-start(bf16[32,16,128]{2,1,0:T(8,128)(2,1)S(1)} %collective-permute-done.4.refs_5_) | copy-start | bytes 393220
  41.9 5.2 %copy-start.11 = (bf16[32,16,128]{2,1,0:T(8,128)(2,1)}, bf16[32,16,128]{2,1,0:T(8,128)(2,1)S(1)}, u32[]{:S(2)}) copy-start(bf16[32,16,128]{2,1,0:T(8,128)(2,1)S(1)} %collective-permute-done.5.refs_6_) | copy-start | bytes 393220
  42.1 5.0 %copy-start.12 = (bf16[32,16,128]{2,1,0:T(8,128)(2,1)}, bf16[32,16,128]{2,1,0:T(8,128)(2,1)S(1)}, u32[]{:S(2)}) copy-start(bf16[32,16,128]{2,1,0:T(8,128)(2,1)S(1)} %collective-permute-done.6.refs_7_) | copy-start | bytes 393220
  47.0 0.8 copy-start.4
  57.1 16.2 %all-to-all-start.2 = ((bf16[32,16,128]{2,1,0:T(8,128)(2,1)}), bf16[32,16,128]{2,1,0:T(8,128)(2,1)S(1)}, u32[]{:S(2)}, u32[]{:S(2)}) async-start(bf16[32,16,128]{2,1,0:T(8,128)(2,1)} %bitcast.8), calls=%async_computation.2 | async-start | bytes 262144 | tf_op jit(solution)/shard_map/all_to_all | solution.py:765
  68.7 35.3 %copy-start.13 = (s32[64,32]{0,1:T(8,128)S(1)}, s32[64,32]{0,1:T(8,128)}, u32[]{:S(2)}) copy-start(s32[64,32]{0,1:T(8,128)} %param.16) | copy-start | bytes 24580
  68.7 35.3 %copy-start.14 = (s32[64]{0:T(128)S(1)}, s32[64]{0:T(128)}, u32[]{:S(2)}) copy-start(s32[64]{0:T(128)} %send_counts.1) | copy-start | bytes 772
  73.3 22.7 %all-to-all-start.4 = ((bf16[64,32,128]{2,1,0:T(8,128)(2,1)}), bf16[64,32,128]{2,1,0:T(8,128)(2,1)S(1)}, u32[]{:S(2)}, u32[]{:S(2)}) async-start(bf16[64,32,128]{2,1,0:T(8,128)(2,1)} %get-tuple-element.30), calls=%async_computation.4 | async-start | bytes 1048576 | tf_op jit(solution)/shard_map/all_to_all | solution.py:765
  79.0 2.2 %collective-permute-start.7 = (bf16[4,32,16,128]{3,2,1,0:T(8,128)(2,1)}, bf16[4,32,16,128]{3,2,1,0:T(8,128)(2,1)S(1)}, u32[]{:S(2)}, u32[]{:S(2)}) collective-permute-start(bf16[4,32,16,128]{3,2,1,0:T(8,128)(2,1)} %get-tuple-element.23), channel_id=1, source_target_pairs={{0,4},{4,0},{1,5},{5,1},{2,6},{6,2},{3,7},{7,3},{8,12},{12,8},{9,1... | collective-permute-start | bytes 1572872 | tf_op jit(solution)/shard_map/ppermute | solution.py:761
  79.4 1.6 %collective-permute-start.8 = (bf16[2,16,128]{2,1,0:T(8,128)(2,1)S(1)}, bf16[2,16,128]{2,1,0:T(8,128)(2,1)S(1)}, u32[]{:S(2)}, u32[]{:S(2)}) collective-permute-start(bf16[2,16,128]{2,1,0:T(8,128)(2,1)S(1)} %fold.1.w_near), channel_id=1, source_target_pairs={{0,4},{4,0},{1,5},{5,1},{2,6},{6,2},{3,7},{7,3},{8,12},{12,8},{9,1... | collective-permute-start | bytes 24584 | tf_op jit(solution)/shard_map/ppermute | solution.py:761
  81.2 1.0 copy-start
  82.5 7.0 %collective-permute-start.9 = (bf16[34,16,128]{2,1,0:T(8,128)(2,1)S(1)}, bf16[34,16,128]{2,1,0:T(8,128)(2,1)S(1)}, u32[]{:S(2)}, u32[]{:S(2)}) collective-permute-start(bf16[34,16,128]{2,1,0:T(8,128)(2,1)S(1)} %get-tuple-element.26), channel_id=1, source_target_pairs={{0,1},{1,2},{2,3},{3,0},{4,5},{5,6},{6,7},{7,4},{8,9},{9,10},{10,1... | collective-permute-start | bytes 417800 | tf_op jit(solution)/shard_map/ppermute | solution.py:757
  84.9 8.2 %collective-permute-start.10 = (bf16[34,16,128]{2,1,0:T(8,128)(2,1)S(1)}, bf16[34,16,128]{2,1,0:T(8,128)(2,1)S(1)}, u32[]{:S(2)}, u32[]{:S(2)}) collective-permute-start(bf16[34,16,128]{2,1,0:T(8,128)(2,1)S(1)} %get-tuple-element.27), channel_id=1, source_target_pairs={{0,2},{1,3},{2,0},{3,1},{4,6},{5,7},{6,4},{7,5},{8,10},{9,11},{10,... | collective-permute-start | bytes 417800 | tf_op jit(solution)/shard_map/ppermute | solution.py:757
  86.4 6.7 %collective-permute-start.11 = (bf16[34,16,128]{2,1,0:T(8,128)(2,1)S(1)}, bf16[34,16,128]{2,1,0:T(8,128)(2,1)S(1)}, u32[]{:S(2)}, u32[]{:S(2)}) collective-permute-start(bf16[34,16,128]{2,1,0:T(8,128)(2,1)S(1)} %get-tuple-element.28), channel_id=1, source_target_pairs={{0,3},{1,0},{2,1},{3,2},{4,7},{5,4},{6,5},{7,6},{8,11},{9,8},{10,9... | collective-permute-start | bytes 417800 | tf_op jit(solution)/shard_map/ppermute | solution.py:757
  96.1 9.5 %copy-start.3 = (bf16[64,32,128]{2,1,0:T(8,128)(2,1)}, bf16[64,32,128]{2,1,0:T(8,128)(2,1)S(1)}, u32[]{:S(2)}) copy-start(bf16[64,32,128]{2,1,0:T(8,128)(2,1)S(1)} %all-to-all-done.4) | copy-start | bytes 1572868
  96.1 20.0 %all-to-all-start.3 = ((bf16[32,32,128]{2,1,0:T(8,128)(2,1)}), bf16[32,32,128]{2,1,0:T(8,128)(2,1)S(1)}, u32[]{:S(2)}, u32[]{:S(2)}) async-start(bf16[32,32,128]{2,1,0:T(8,128)(2,1)} %merge.1), calls=%async_computation.3 | async-start | bytes 524288 | tf_op jit(solution)/shard_map/all_to_all | solution.py:765
  105.6 10.5 %copy-start.2 = (s32[16]{0:T(128)S(1)}, s32[16]{0:T(128)}, u32[]{:S(2)}) copy-start(s32[16]{0:T(128)} %hub_rows.5) | copy-start | bytes 196
  116.1 0.8 copy-start.1

commit v6 on v5

--- a/solution.py
+++ b/solution.py
@@ -16,6 +16,9 @@
 TILE = 8
 PARTS = 4
 WHOLE = 60
+FORWARD = 52
+FAR = 52
+OWN = 52
 FINISH = 16
 FOLDS = 4
 FOLD_ROWS = 512
@@ -309,7 +312,7 @@
             pltpu.SemaphoreType.DMA((5 + parts,)),
             pltpu.SemaphoreType.DMA((3,)),
         ],
-        compiler_params=params(WHOLE),
+        compiler_params=params(FORWARD),
         name="forward",
     )(targets, sources, count, weights, features, halo, *hubs, out_grad, w_self, w_nbr)
 
@@ -461,7 +464,7 @@
             pltpu.SemaphoreType.DMA((tiles // CHUNK,)),
             pltpu.SemaphoreType.DMA((3,)),
         ],
-        compiler_params=params(WHOLE),
+        compiler_params=params(FAR),
         name="backward_far",
     )(targets, sources, count, weights, grad_agg)
 
@@ -589,7 +592,7 @@
             pltpu.SemaphoreType.DMA((3,)),
             pltpu.SemaphoreType.DMA((node_rows // FOLDS // FOLD_ROWS, FOLDS)),
         ],
-        compiler_params=params(WHOLE),
+        compiler_params=params(OWN),
         name="own_rows",
     )(
         targets,

time: 121 us -> 118 us (0.975)
  waiting for transfers between devices: 30.3 us -> 34.6 us
  local copies, waits for them, and re-layouts: 4.19 us -> 0.36 us
  Pallas kernels: 33.1 us -> 30.5 us
    all_to_all x5, waiting for transfers between devices: 19.4 us -> 22.5 us  [swap(): return lax.all_to_all(value, axes, split_axis=0, concat_axis=0, tiled=True)]
    unnamed x30 -> x16, local copies, waits for them, and re-layouts: 2.66 us -> 0.04 us
    ppermute x6, waiting for transfers between devices: 9.23 us -> 10.5 us  [rep_shift(): lax.ppermute(value, 'rep', [(j, (j + shift) % REPS) for j in range(REPS)])]
  transfers between devices with their start and end apart: 17 -> 17, of which waited for: 13 -> 12; matrix products, arithmetic and copies ran while one was open for 1% -> 0% of each run, Pallas kernels for 16% -> 15%
where the time goes in v6:
time: 118 us; the launch traced here: 117 us
  starting transfers between devices  50 us (42%)
  waiting for transfers between devices  34.6 us (29%)
  Pallas kernels  30.5 us (26%)
  between operations  1.67 us (1%)
    all_to_all x5, starting transfers between devices, swap(): return lax.all_to_all(value, axes, split_axis=0, concat_axis=0, tiled=True)  37.2 us
    all_to_all x5, waiting for transfers between devices, swap(): return lax.all_to_all(value, axes, split_axis=0, concat_axis=0, tiled=True)  22.5 us
    ppermute x6, starting transfers between devices, rep_shift(): lax.ppermute(value, 'rep', [(j, (j + shift) % REPS) for j in range(REPS)])  11.6 us
    ppermute x6, waiting for transfers between devices, rep_shift(): lax.ppermute(value, 'rep', [(j, (j + shift) % REPS) for j in range(REPS)])  10.5 us
    pallas_call x1, Pallas kernels, forward(): pl.pallas_call(forward_kernel, out_shape=shapes, in_specs=[smem()] * 3 +...  8.43 us
    pallas_call x1, Pallas kernels, own_rows(): pl.pallas_call(own_rows_kernel, out_shape=(jax.ShapeDtypeStruct((node_row...  6.16 us
    pallas_call x1, Pallas kernels, halo_pack(): pl.pallas_call(halo_pack_kernel, out_shape=jax.ShapeDtypeStruct((peers, s...  5.1 us
    pallas_call x1, Pallas kernels, backward_far(): pl.pallas_call(backward_far_kernel, out_shape=(halo, piece, piece), in_sp...  4.32 us
  transfers between devices with their start and end apart: 17, of which 12 were waited for; matrix products, arithmetic and copies ran while one was open for 0% of the time, Pallas kernels for 15%

profile of v6, /device:TPU:32, one launch (start us, length us, event | category | flops | bytes accessed | tf_op | source)
XLA Modules:
  0.0 117.1 jit_solution(7065943608035906601)
XLA Ops:
  0.7 2.7 %hub_pack.1 = bf16[32,16,128]{2,1,0:T(8,128)(2,1)} custom-call(s32[16]{0:T(128)} %hub_rows.5, bf16[4096,128]{1,0:T(8,128)(2,1)} %features.3), custom_call_target="tpu_custom_call" | custom-call | tf_op jit(solution)/shard_map/hub_pack/pallas_call | solution.py:80
  3.4 11.4 %all-to-all-start.1 = ((bf16[32,16,128]{2,1,0:T(8,128)(2,1)}), bf16[32,16,128]{2,1,0:T(8,128)(2,1)S(1)}, u32[]{:S(2)}, u32[]{:S(2)}) async-start(bf16[32,16,128]{2,1,0:T(8,128)(2,1)} %hub_pack.1), calls=%async_computation.1 | async-start | bytes 262144 | tf_op jit(solution)/shard_map/all_to_all | solution.py:768
  14.8 5.1 %halo_pack.1 = bf16[64,32,128]{2,1,0:T(8,128)(2,1)} custom-call(s32[32,64]{1,0:T(8,128)} %bitcast.8, s32[64]{0:T(128)} %send_counts.1, bf16[4096,128]{1,0:T(8,128)(2,1)} %features.3), custom_call_target="tpu_custom_call" | custom-call | tf_op jit(solution)/shard_map/halo_pack/pallas_call | solution.py:118
  19.9 4.7 %all-to-all-done.1.refs_0_ = bf16[32,16,128]{2,1,0:T(8,128)(2,1)S(1)} async-done(((bf16[32,16,128]{2,1,0:T(8,128)(2,1)}), bf16[32,16,128]{2,1,0:T(8,128)(2,1)S(1)}, u32[]{:S(2)}, u32[]{:S(2)}) %all-to-all-start.1) | async-done | bytes 131104 | tf_op jit(solution)/shard_map/all_to_all | solution.py:768
  24.6 5.5 %all-to-all-start = ((bf16[64,32,128]{2,1,0:T(8,128)(2,1)}), bf16[64,32,128]{2,1,0:T(8,128)(2,1)S(1)}, u32[]{:S(2)}, u32[]{:S(2)}) async-start(bf16[64,32,128]{2,1,0:T(8,128)(2,1)} %halo_pack.1), calls=%async_computation | async-start | bytes 1048576 | tf_op jit(solution)/shard_map/all_to_all | solution.py:768
  30.1 1.6 %collective-permute-start = (bf16[32,16,128]{2,1,0:T(8,128)(2,1)S(1)}, bf16[32,16,128]{2,1,0:T(8,128)(2,1)S(1)}, u32[]{:S(2)}, u32[]{:S(2)}) collective-permute-start(bf16[32,16,128]{2,1,0:T(8,128)(2,1)S(1)} %all-to-all-done.1.refs_0_), channel_id=1, source_target_pairs={{0,1},{1,2},{2,3},{3,0},{4,5},{5,6},{6,7},{7,4},{8,9},{9,10},{10,1... | collective-permute-start | bytes 393224 | tf_op jit(solution)/shard_map/ppermute | solution.py:760
  31.7 2.7 %collective-permute-start.1 = (bf16[32,16,128]{2,1,0:T(8,128)(2,1)S(1)}, bf16[32,16,128]{2,1,0:T(8,128)(2,1)S(1)}, u32[]{:S(2)}, u32[]{:S(2)}) collective-permute-start(bf16[32,16,128]{2,1,0:T(8,128)(2,1)S(1)} %all-to-all-done.1.refs_0_), channel_id=1, source_target_pairs={{0,2},{1,3},{2,0},{3,1},{4,6},{5,7},{6,4},{7,5},{8,10},{9,11},{10,... | collective-permute-start | bytes 393224 | tf_op jit(solution)/shard_map/ppermute | solution.py:760
  34.4 1.4 %collective-permute-start.2 = (bf16[32,16,128]{2,1,0:T(8,128)(2,1)S(1)}, bf16[32,16,128]{2,1,0:T(8,128)(2,1)S(1)}, u32[]{:S(2)}, u32[]{:S(2)}) collective-permute-start(bf16[32,16,128]{2,1,0:T(8,128)(2,1)S(1)} %all-to-all-done.1.refs_0_), channel_id=1, source_target_pairs={{0,3},{1,0},{2,1},{3,2},{4,7},{5,4},{6,5},{7,6},{8,11},{9,8},{10,9... | collective-permute-start | bytes 393224 | tf_op jit(solution)/shard_map/ppermute | solution.py:760
  35.8 1.1 collective-permute-done.refs_1_
  36.9 0.0 collective-permute-start.4
  36.9 3.8 %collective-permute-done.1.refs_2_ = bf16[32,16,128]{2,1,0:T(8,128)(2,1)S(1)} collective-permute-done((bf16[32,16,128]{2,1,0:T(8,128)(2,1)S(1)}, bf16[32,16,128]{2,1,0:T(8,128)(2,1)S(1)}, u32[]{:S(2)}, u32[]{:S(2)}) %collective-permute-start.1) | collective-permute-done | bytes 131104 | tf_op jit(solution)/shard_map/ppermute | solution.py:760
  40.7 0.0 collective-permute-start.5
  40.7 0.0 collective-permute-done.2.refs_3_
  40.7 0.5 collective-permute-start.6
  41.9 0.0 collective-permute-done.3.refs_4_
  41.9 0.2 collective-permute-done.5.refs_6_
  42.1 0.2 collective-permute-done.6.refs_7_
  42.3 4.9 %all-to-all-done = bf16[64,32,128]{2,1,0:T(8,128)(2,1)S(1)} async-done(((bf16[64,32,128]{2,1,0:T(8,128)(2,1)}), bf16[64,32,128]{2,1,0:T(8,128)(2,1)S(1)}, u32[]{:S(2)}, u32[]{:S(2)}) %all-to-all-start) | async-done | bytes 524320 | tf_op jit(solution)/shard_map/all_to_all | solution.py:768
  47.2 8.4 %forward.1 = (bf16[4096,256]{1,0:T(8,128)(2,1)}, bf16[4096,128]{1,0:T(8,128)(2,1)}, f32[4096,128]{1,0:T(8,128)}, bf16[512,128]{1,0:T(8,128)(2,1)}) custom-call(s32[128]{0:T(128)S(1)} %copy-done.3, s32[128]{0:T(128)S(1)} %copy-done.4, s32[1]{0:T(128)S(6)} %copy.21.count, bf16[128,128,128]{2,1,0:T(8,128)(2,1)} %weights.5, bf16[32,8,16,128]{3,2,1,0:T(8,128)(2,1)} %bitcast.7, ...), custom_call_target="tpu_custom_call" | custom-call | tf_op jit(solution)/shard_map/forward/pallas_call | solution.py:296
  55.7 7.4 %all-to-all-start.2 = ((bf16[32,16,128]{2,1,0:T(8,128)(2,1)}), bf16[32,16,128]{2,1,0:T(8,128)(2,1)S(1)}, u32[]{:S(2)}, u32[]{:S(2)}) async-start(bf16[32,16,128]{2,1,0:T(8,128)(2,1)} %bitcast.3), calls=%async_computation.2 | async-start | bytes 262144 | tf_op jit(solution)/shard_map/all_to_all | solution.py:768
  63.0 4.3 %backward_far.1 = (bf16[64,32,128]{2,1,0:T(8,128)(2,1)}, bf16[4,32,16,128]{3,2,1,0:T(8,128)(2,1)S(1)}, bf16[4,32,16,128]{3,2,1,0:T(8,128)(2,1)S(1)}) custom-call(s32[128]{0:T(128)S(1)} %copy-done.3, s32[128]{0:T(128)S(1)} %copy-done.4, s32[1]{0:T(128)S(6)} %copy.21.count, bf16[128,128,128]{2,1,0:T(8,128)(2,1)} %weights.5, ...), custom_call_target="tpu_custom_call" | custom-call | tf_op jit(solution)/shard_map/backward_far/pallas_call | solution.py:451
  67.4 0.0 copy-start.6
  67.4 0.0 copy-start.7
  67.4 0.0 copy-start
  67.4 0.0 copy-start.5
  67.4 5.4 %all-to-all-done.2.slices = bf16[32,16,128]{2,1,0:T(8,128)(2,1)S(1)} async-done(((bf16[32,16,128]{2,1,0:T(8,128)(2,1)}), bf16[32,16,128]{2,1,0:T(8,128)(2,1)S(1)}, u32[]{:S(2)}, u32[]{:S(2)}) %all-to-all-start.2) | async-done | bytes 131104 | tf_op jit(solution)/shard_map/all_to_all | solution.py:768
  72.8 5.3 %all-to-all-start.4 = ((bf16[64,32,128]{2,1,0:T(8,128)(2,1)}), bf16[64,32,128]{2,1,0:T(8,128)(2,1)S(1)}, u32[]{:S(2)}, u32[]{:S(2)}) async-start(bf16[64,32,128]{2,1,0:T(8,128)(2,1)} %get-tuple-element.30), calls=%async_computation.4 | async-start | bytes 1048576 | tf_op jit(solution)/shard_map/all_to_all | solution.py:768
  78.1 0.2 collective-permute-start.7
  78.4 0.2 fold.1.w_near
  78.5 0.4 collective-permute-start.8
  79.0 1.2 collective-permute-done.8.w_far
  80.1 0.3 join.1
  80.5 1.9 %collective-permute-start.9 = (bf16[34,16,128]{2,1,0:T(8,128)(2,1)S(1)}, bf16[34,16,128]{2,1,0:T(8,128)(2,1)S(1)}, u32[]{:S(2)}, u32[]{:S(2)}) collective-permute-start(bf16[34,16,128]{2,1,0:T(8,128)(2,1)S(1)} %get-tuple-element.26), channel_id=1, source_target_pairs={{0,1},{1,2},{2,3},{3,0},{4,5},{5,6},{6,7},{7,4},{8,9},{9,10},{10,1... | collective-permute-start | bytes 417800 | tf_op jit(solution)/shard_map/ppermute | solution.py:760
  82.4 2.9 %collective-permute-start.10 = (bf16[34,16,128]{2,1,0:T(8,128)(2,1)S(1)}, bf16[34,16,128]{2,1,0:T(8,128)(2,1)S(1)}, u32[]{:S(2)}, u32[]{:S(2)}) collective-permute-start(bf16[34,16,128]{2,1,0:T(8,128)(2,1)S(1)} %get-tuple-element.27), channel_id=1, source_target_pairs={{0,2},{1,3},{2,0},{3,1},{4,6},{5,7},{6,4},{7,5},{8,10},{9,11},{10,... | collective-permute-start | bytes 417800 | tf_op jit(solution)/shard_map/ppermute | solution.py:760
  85.3 1.0 collective-permute-start.11
  86.4 1.5 %collective-permute-done.9.hub1 = bf16[34,16,128]{2,1,0:T(8,128)(2,1)S(1)} collective-permute-done((bf16[34,16,128]{2,1,0:T(8,128)(2,1)S(1)}, bf16[34,16,128]{2,1,0:T(8,128)(2,1)S(1)}, u32[]{:S(2)}, u32[]{:S(2)}) %collective-permute-start.9) | collective-permute-done | bytes 139296 | tf_op jit(solution)/shard_map/ppermute | solution.py:760
  87.8 4.2 %collective-permute-done.10.hub2 = bf16[34,16,128]{2,1,0:T(8,128)(2,1)S(1)} collective-permute-done((bf16[34,16,128]{2,1,0:T(8,128)(2,1)S(1)}, bf16[34,16,128]{2,1,0:T(8,128)(2,1)S(1)}, u32[]{:S(2)}, u32[]{:S(2)}) %collective-permute-start.10) | collective-permute-done | bytes 139296 | tf_op jit(solution)/shard_map/ppermute | solution.py:760
  92.0 0.0 collective-permute-done.11.hub3
  92.0 1.0 merge.1
  93.0 2.3 %all-to-all-done.4 = bf16[64,32,128]{2,1,0:T(8,128)(2,1)S(1)} async-done(((bf16[64,32,128]{2,1,0:T(8,128)(2,1)}), bf16[64,32,128]{2,1,0:T(8,128)(2,1)S(1)}, u32[]{:S(2)}, u32[]{:S(2)}) %all-to-all-start.4) | async-done | bytes 524320 | tf_op jit(solution)/shard_map/all_to_all | solution.py:768
  95.2 7.7 %all-to-all-start.3 = ((bf16[32,32,128]{2,1,0:T(8,128)(2,1)}), bf16[32,32,128]{2,1,0:T(8,128)(2,1)S(1)}, u32[]{:S(2)}, u32[]{:S(2)}) async-start(bf16[32,32,128]{2,1,0:T(8,128)(2,1)} %merge.1), calls=%async_computation.3 | async-start | bytes 524288 | tf_op jit(solution)/shard_map/all_to_all | solution.py:768
  102.9 0.1 copy.18
  103.0 0.1 reshape.30.ids_across
  103.1 0.1 copy.19
  103.2 0.1 convert_element_type.6.ids_down
  103.3 6.2 %own_rows.1 = (f32[4096,128]{1,0:T(8,128)}, f32[128,128]{1,0:T(8,128)S(1)}) custom-call(s32[128]{0:T(128)S(1)} %copy-done.3, s32[128]{0:T(128)S(1)} %copy-done.4, s32[1]{0:T(128)S(6)} %copy.21.count, s32[16]{0:T(128)S(1)} %copy-done.5, bf16[128,128,128]{2,1,0:T(8,128)(2,1)} %weights.5, bf16[4096,128]{1,0:T(8,128)(2,1)S(1)} %copy-done, ...), custom_call_target="tpu_custom_call" | custom-call | tf_op jit(solution)/shard_map/own_rows/pallas_call | solution.py:575
  109.4 5.3 %all-to-all-done.3.received = bf16[32,32,128]{2,1,0:T(8,128)(2,1)S(1)} async-done(((bf16[32,32,128]{2,1,0:T(8,128)(2,1)}), bf16[32,32,128]{2,1,0:T(8,128)(2,1)S(1)}, u32[]{:S(2)}, u32[]{:S(2)}) %all-to-all-start.3) | async-done | bytes 262176 | tf_op jit(solution)/shard_map/all_to_all | solution.py:768
  114.7 2.3 %finish.1 = (f32[4096,128]{1,0:T(8,128)}, f32[128,256]{1,0:T(8,128)}, f32[128,256]{1,0:T(8,128)}) custom-call(s32[16]{0:T(128)S(1)} %copy-done.5, bf16[32,32,128]{2,1,0:T(8,128)(2,1)S(1)} %all-to-all-done.3.received, f32[128,128]{1,0:T(8,128)S(1)} %get-tuple-element.31.around, f32[4096,128]{1,0:T(8,128)} %get-tuple-element.32.grad_nodes), custom_call_target="tpu_custom_call", output_to_operand_aliasing={{0}: (3, {})} | custom-call | tf_op jit(solution)/shard_map/finish/pallas_call | solution.py:739
  (16 shorter events, 0.0 us)
Async XLA Ops:
  0.6 46.6 %copy-start.3 = (s32[128]{0:T(128)S(1)}, s32[128]{0:T(128)}, u32[]{:S(2)}) copy-start(s32[128]{0:T(128)} %targets.5) | copy-start | bytes 1540
  0.6 46.6 %copy-start.4 = (s32[128]{0:T(128)S(1)}, s32[128]{0:T(128)}, u32[]{:S(2)}) copy-start(s32[128]{0:T(128)} %sources.5) | copy-start | bytes 1540
  0.7 46.6 %copy-start.1 = (bf16[128,256]{1,0:T(8,128)(2,1)S(1)}, bf16[128,256]{1,0:T(8,128)(2,1)}, u32[]{:S(2)}) copy-start(bf16[128,256]{1,0:T(8,128)(2,1)} %refs_9_.1) | copy-start | bytes 196612
  0.7 46.6 %copy-start.2 = (bf16[128,256]{1,0:T(8,128)(2,1)S(1)}, bf16[128,256]{1,0:T(8,128)(2,1)}, u32[]{:S(2)}) copy-start(bf16[128,256]{1,0:T(8,128)(2,1)} %refs_10_.1) | copy-start | bytes 196612
  3.4 21.2 %all-to-all-start.1 = ((bf16[32,16,128]{2,1,0:T(8,128)(2,1)}), bf16[32,16,128]{2,1,0:T(8,128)(2,1)S(1)}, u32[]{:S(2)}, u32[]{:S(2)}) async-start(bf16[32,16,128]{2,1,0:T(8,128)(2,1)} %hub_pack.1), calls=%async_computation.1 | async-start | bytes 262144 | tf_op jit(solution)/shard_map/all_to_all | solution.py:768
  24.6 22.6 %all-to-all-start = ((bf16[64,32,128]{2,1,0:T(8,128)(2,1)}), bf16[64,32,128]{2,1,0:T(8,128)(2,1)S(1)}, u32[]{:S(2)}, u32[]{:S(2)}) async-start(bf16[64,32,128]{2,1,0:T(8,128)(2,1)} %halo_pack.1), calls=%async_computation | async-start | bytes 1048576 | tf_op jit(solution)/shard_map/all_to_all | solution.py:768
  30.1 6.8 %collective-permute-start = (bf16[32,16,128]{2,1,0:T(8,128)(2,1)S(1)}, bf16[32,16,128]{2,1,0:T(8,128)(2,1)S(1)}, u32[]{:S(2)}, u32[]{:S(2)}) collective-permute-start(bf16[32,16,128]{2,1,0:T(8,128)(2,1)S(1)} %all-to-all-done.1.refs_0_), channel_id=1, source_target_pairs={{0,1},{1,2},{2,3},{3,0},{4,5},{5,6},{6,7},{7,4},{8,9},{9,10},{10,1... | collective-permute-start | bytes 393224 | tf_op jit(solution)/shard_map/ppermute | solution.py:760
  31.7 9.1 %collective-permute-start.1 = (bf16[32,16,128]{2,1,0:T(8,128)(2,1)S(1)}, bf16[32,16,128]{2,1,0:T(8,128)(2,1)S(1)}, u32[]{:S(2)}, u32[]{:S(2)}) collective-permute-start(bf16[32,16,128]{2,1,0:T(8,128)(2,1)S(1)} %all-to-all-done.1.refs_0_), channel_id=1, source_target_pairs={{0,2},{1,3},{2,0},{3,1},{4,6},{5,7},{6,4},{7,5},{8,10},{9,11},{10,... | collective-permute-start | bytes 393224 | tf_op jit(solution)/shard_map/ppermute | solution.py:760
  34.4 6.3 %collective-permute-start.2 = (bf16[32,16,128]{2,1,0:T(8,128)(2,1)S(1)}, bf16[32,16,128]{2,1,0:T(8,128)(2,1)S(1)}, u32[]{:S(2)}, u32[]{:S(2)}) collective-permute-start(bf16[32,16,128]{2,1,0:T(8,128)(2,1)S(1)} %all-to-all-done.1.refs_0_), channel_id=1, source_target_pairs={{0,3},{1,0},{2,1},{3,2},{4,7},{5,4},{6,5},{7,6},{8,11},{9,8},{10,9... | collective-permute-start | bytes 393224 | tf_op jit(solution)/shard_map/ppermute | solution.py:760
  35.8 6.1 %collective-permute-start.3 = (bf16[32,16,128]{2,1,0:T(8,128)(2,1)S(1)}, bf16[32,16,128]{2,1,0:T(8,128)(2,1)S(1)}, u32[]{:S(2)}, u32[]{:S(2)}) collective-permute-start(bf16[32,16,128]{2,1,0:T(8,128)(2,1)S(1)} %all-to-all-done.1.refs_0_), channel_id=1, source_target_pairs={{0,4},{4,0},{1,5},{5,1},{2,6},{6,2},{3,7},{7,3},{8,12},{12,8},{9,1... | collective-permute-start | bytes 393224 | tf_op jit(solution)/shard_map/ppermute | solution.py:764
  36.9 5.0 %collective-permute-start.4 = (bf16[32,16,128]{2,1,0:T(8,128)(2,1)S(1)}, bf16[32,16,128]{2,1,0:T(8,128)(2,1)S(1)}, u32[]{:S(2)}, u32[]{:S(2)}) collective-permute-start(bf16[32,16,128]{2,1,0:T(8,128)(2,1)S(1)} %collective-permute-done.refs_1_), channel_id=1, source_target_pairs={{0,4},{4,0},{1,5},{5,1},{2,6},{6,2},{3,7},{7,3},{8,12},{12,8},{9,1... | collective-permute-start | bytes 393224 | tf_op jit(solution)/shard_map/ppermute | solution.py:764
  40.7 1.3 %collective-permute-start.5 = (bf16[32,16,128]{2,1,0:T(8,128)(2,1)S(1)}, bf16[32,16,128]{2,1,0:T(8,128)(2,1)S(1)}, u32[]{:S(2)}, u32[]{:S(2)}) collective-permute-start(bf16[32,16,128]{2,1,0:T(8,128)(2,1)S(1)} %collective-permute-done.1.refs_2_), channel_id=1, source_target_pairs={{0,4},{4,0},{1,5},{5,1},{2,6},{6,2},{3,7},{7,3},{8,12},{12,8},{9,1... | collective-permute-start | bytes 393224 | tf_op jit(solution)/shard_map/ppermute | solution.py:764
  40.7 1.5 %collective-permute-start.6 = (bf16[32,16,128]{2,1,0:T(8,128)(2,1)S(1)}, bf16[32,16,128]{2,1,0:T(8,128)(2,1)S(1)}, u32[]{:S(2)}, u32[]{:S(2)}) collective-permute-start(bf16[32,16,128]{2,1,0:T(8,128)(2,1)S(1)} %collective-permute-done.2.refs_3_), channel_id=1, source_target_pairs={{0,4},{4,0},{1,5},{5,1},{2,6},{6,2},{3,7},{7,3},{8,12},{12,8},{9,1... | collective-permute-start | bytes 393224 | tf_op jit(solution)/shard_map/ppermute | solution.py:764
  55.7 17.1 %all-to-all-start.2 = ((bf16[32,16,128]{2,1,0:T(8,128)(2,1)}), bf16[32,16,128]{2,1,0:T(8,128)(2,1)S(1)}, u32[]{:S(2)}, u32[]{:S(2)}) async-start(bf16[32,16,128]{2,1,0:T(8,128)(2,1)} %bitcast.3), calls=%async_computation.2 | async-start | bytes 262144 | tf_op jit(solution)/shard_map/all_to_all | solution.py:768
  67.4 35.5 %copy-start.6 = (s32[64,32]{0,1:T(8,128)S(1)}, s32[64,32]{0,1:T(8,128)}, u32[]{:S(2)}) copy-start(s32[64,32]{0,1:T(8,128)} %param.16) | copy-start | bytes 24580
  67.4 35.5 %copy-start.7 = (s32[64]{0:T(128)S(1)}, s32[64]{0:T(128)}, u32[]{:S(2)}) copy-start(s32[64]{0:T(128)} %send_counts.1) | copy-start | bytes 772
  67.4 35.9 %copy-start = (bf16[4096,128]{1,0:T(8,128)(2,1)S(1)}, bf16[4096,128]{1,0:T(8,128)(2,1)}, u32[]{:S(2)}) copy-start(bf16[4096,128]{1,0:T(8,128)(2,1)} %get-tuple-element.21.grad_agg) | copy-start | bytes 3145732
  67.4 35.9 %copy-start.5 = (s32[16]{0:T(128)S(1)}, s32[16]{0:T(128)}, u32[]{:S(2)}) copy-start(s32[16]{0:T(128)} %hub_rows.5) | copy-start | bytes 196
  72.8 22.4 %all-to-all-start.4 = ((bf16[64,32,128]{2,1,0:T(8,128)(2,1)}), bf16[64,32,128]{2,1,0:T(8,128)(2,1)S(1)}, u32[]{:S(2)}, u32[]{:S(2)}) async-start(bf16[64,32,128]{2,1,0:T(8,128)(2,1)} %get-tuple-element.30), calls=%async_computation.4 | async-start | bytes 1048576 | tf_op jit(solution)/shard_map/all_to_all | solution.py:768
  78.1 2.0 %collective-permute-start.7 = (bf16[4,32,16,128]{3,2,1,0:T(8,128)(2,1)S(1)}, bf16[4,32,16,128]{3,2,1,0:T(8,128)(2,1)S(1)}, u32[]{:S(2)}, u32[]{:S(2)}) collective-permute-start(bf16[4,32,16,128]{3,2,1,0:T(8,128)(2,1)S(1)} %get-tuple-element.23), channel_id=1, source_target_pairs={{0,4},{4,0},{1,5},{5,1},{2,6},{6,2},{3,7},{7,3},{8,12},{12,8},{9,1... | collective-permute-start | bytes 1572872 | tf_op jit(solution)/shard_map/ppermute | solution.py:764
  78.5 1.6 %collective-permute-start.8 = (bf16[2,16,128]{2,1,0:T(8,128)(2,1)S(1)}, bf16[2,16,128]{2,1,0:T(8,128)(2,1)S(1)}, u32[]{:S(2)}, u32[]{:S(2)}) collective-permute-start(bf16[2,16,128]{2,1,0:T(8,128)(2,1)S(1)} %fold.1.w_near), channel_id=1, source_target_pairs={{0,4},{4,0},{1,5},{5,1},{2,6},{6,2},{3,7},{7,3},{8,12},{12,8},{9,1... | collective-permute-start | bytes 24584 | tf_op jit(solution)/shard_map/ppermute | solution.py:764
  80.5 7.4 %collective-permute-start.9 = (bf16[34,16,128]{2,1,0:T(8,128)(2,1)S(1)}, bf16[34,16,128]{2,1,0:T(8,128)(2,1)S(1)}, u32[]{:S(2)}, u32[]{:S(2)}) collective-permute-start(bf16[34,16,128]{2,1,0:T(8,128)(2,1)S(1)} %get-tuple-element.26), channel_id=1, source_target_pairs={{0,1},{1,2},{2,3},{3,0},{4,5},{5,6},{6,7},{7,4},{8,9},{9,10},{10,1... | collective-permute-start | bytes 417800 | tf_op jit(solution)/shard_map/ppermute | solution.py:760
  82.4 9.6 %collective-permute-start.10 = (bf16[34,16,128]{2,1,0:T(8,128)(2,1)S(1)}, bf16[34,16,128]{2,1,0:T(8,128)(2,1)S(1)}, u32[]{:S(2)}, u32[]{:S(2)}) collective-permute-start(bf16[34,16,128]{2,1,0:T(8,128)(2,1)S(1)} %get-tuple-element.27), channel_id=1, source_target_pairs={{0,2},{1,3},{2,0},{3,1},{4,6},{5,7},{6,4},{7,5},{8,10},{9,11},{10,... | collective-permute-start | bytes 417800 | tf_op jit(solution)/shard_map/ppermute | solution.py:760
  85.3 6.7 %collective-permute-start.11 = (bf16[34,16,128]{2,1,0:T(8,128)(2,1)S(1)}, bf16[34,16,128]{2,1,0:T(8,128)(2,1)S(1)}, u32[]{:S(2)}, u32[]{:S(2)}) collective-permute-start(bf16[34,16,128]{2,1,0:T(8,128)(2,1)S(1)} %get-tuple-element.28), channel_id=1, source_target_pairs={{0,3},{1,0},{2,1},{3,2},{4,7},{5,4},{6,5},{7,6},{8,11},{9,8},{10,9... | collective-permute-start | bytes 417800 | tf_op jit(solution)/shard_map/ppermute | solution.py:760
  95.2 19.4 %all-to-all-start.3 = ((bf16[32,32,128]{2,1,0:T(8,128)(2,1)}), bf16[32,32,128]{2,1,0:T(8,128)(2,1)S(1)}, u32[]{:S(2)}, u32[]{:S(2)}) async-start(bf16[32,32,128]{2,1,0:T(8,128)(2,1)} %merge.1), calls=%async_computation.3 | async-start | bytes 524288 | tf_op jit(solution)/shard_map/all_to_all | solution.py:768

commit v7 on v6

--- a/solution.py
+++ b/solution.py
@@ -10,7 +10,7 @@
 
 BF16 = jnp.bfloat16
 F32 = jnp.float32
-CHUNK = 16
+CHUNK = 32
 ROWS = 1024
 NEAR = 16
 TILE = 8
@@ -261,7 +261,8 @@
         return carry
 
     steps = node_rows // ROWS
-    lax.fori_loop(0, steps, dense, 0)
+    for c in range(steps):
+        dense(c, 0)
     half = grad_total.shape[1] // 2
     w_all[: grad_total.shape[0]] = grad_total[:, :half].astype(BF16)
     w_all[grad_total.shape[0] :] = grad_total[:, half:].astype(BF16)
@@ -703,7 +704,7 @@
     w_rows = message - hubs
 
     def body(
-        hub_rows, received, around, grad_nodes, out, grad_self, grad_nbr, near, held, sems
+        hub_rows, received, around, grad_nodes, out, grad_self, grad_nbr, near, held, wide, sems
     ):
         at = [hub_rows[h] // TILE for h in range(hubs)]
         near[...] = around[...]
@@ -713,6 +714,16 @@
             return total + received[p, :hubs].astype(F32)
 
         total = lax.fori_loop(0, groups, place, jnp.zeros((hubs, width), F32), unroll=4)
+        for k in range(hidden_width // width):
+            columns = pl.ds(k * width, width)
+            for n in range(2):
+                wide[n, :, columns] = held[pl.ds((2 * k + n) * width, width)]
+        w_outs = [
+            pltpu.make_async_copy(wide.at[n], grad, sems.at[hubs + n])
+            for n, grad in enumerate((grad_self, grad_nbr))
+        ]
+        for copy in w_outs:
+            copy.start()
         first = []
         for h in range(hubs):
             slot = jnp.int32(h)
@@ -729,12 +740,10 @@
 
         for h in range(hubs):
             pl.when(first[h] == h)(back(h).start)
-        for k in range(hidden_width // width):
-            columns = pl.ds(k * width, width)
-            grad_self[:, columns] = held[2 * k * width : (2 * k + 1) * width]
-            grad_nbr[:, columns] = held[(2 * k + 1) * width : (2 * k + 2) * width]
         for h in range(hubs):
             pl.when(first[h] == h)(back(h).wait)
+        for copy in w_outs:
+            copy.wait()
 
     return pl.pallas_call(
         body,
@@ -744,12 +753,13 @@
             jax.ShapeDtypeStruct((width, hidden_width), F32),
         ),
         in_specs=[smem(), vmem(), vmem(), hbm()],
-        out_specs=(hbm(), vmem(), vmem()),
+        out_specs=(hbm(),) * 3,
         input_output_aliases={3: 0},
         scratch_shapes=[
             pltpu.VMEM((hubs * TILE, width), F32),
             pltpu.VMEM((groups * w_rows, width), F32),
-            pltpu.SemaphoreType.DMA((hubs,)),
+            pltpu.VMEM((2, width, hidden_width), F32),
+            pltpu.SemaphoreType.DMA((hubs + 2,)),
         ],
         compiler_params=params(FINISH),
         name="finish",

time: 118 us -> 116 us (0.983)
  starting transfers between devices: 50 us -> 47.3 us
    all_to_all x5, starting transfers between devices: 37.2 us -> 35.1 us  [swap(): return lax.all_to_all(value, axes, split_axis=0, concat_axis=0, tiled=True)]
  transfers between devices with their start and end apart: 17 -> 17, of which waited for: 12 -> 13; matrix products, arithmetic and copies ran while one was open for 0% -> 0% of each run, Pallas kernels for 15% -> 16%
where the time goes in v7:
time: 116 us; the launch traced here: 114 us
  starting transfers between devices  47.3 us (41%)
  waiting for transfers between devices  34.3 us (30%)
  Pallas kernels  30.8 us (27%)
  between operations  1.67 us (1%)
    all_to_all x5, starting transfers between devices, swap(): return lax.all_to_all(value, axes, split_axis=0, concat_axis=0, tiled=True)  35.1 us
    all_to_all x5, waiting for transfers between devices, swap(): return lax.all_to_all(value, axes, split_axis=0, concat_axis=0, tiled=True)  22.6 us
    ppermute x6, starting transfers between devices, rep_shift(): lax.ppermute(value, 'rep', [(j, (j + shift) % REPS) for j in range(REPS)])  11.1 us
    ppermute x6, waiting for transfers between devices, rep_shift(): lax.ppermute(value, 'rep', [(j, (j + shift) % REPS) for j in range(REPS)])  10.1 us
    pallas_call x1, Pallas kernels, forward(): pl.pallas_call(forward_kernel, out_shape=shapes, in_specs=[smem()] * 3 +...  8.58 us
    pallas_call x1, Pallas kernels, own_rows(): pl.pallas_call(own_rows_kernel, out_shape=(jax.ShapeDtypeStruct((node_row...  6.61 us
    pallas_call x1, Pallas kernels, halo_pack(): pl.pallas_call(halo_pack_kernel, out_shape=jax.ShapeDtypeStruct((peers, s...  5.1 us
    pallas_call x1, Pallas kernels, backward_far(): pl.pallas_call(backward_far_kernel, out_shape=(halo, piece, piece), in_sp...  4.69 us
  transfers between devices with their start and end apart: 17, of which 13 were waited for; matrix products, arithmetic and copies ran while one was open for 0% of the time, Pallas kernels for 16%

profile of v7, /device:TPU:32, one launch (start us, length us, event | category | flops | bytes accessed | tf_op | source)
XLA Modules:
  0.0 114.4 jit_solution(17742014899053642282)
XLA Ops:
  0.7 2.7 %hub_pack.1 = bf16[32,16,128]{2,1,0:T(8,128)(2,1)} custom-call(s32[16]{0:T(128)} %hub_rows.5, bf16[4096,128]{1,0:T(8,128)(2,1)} %features.3), custom_call_target="tpu_custom_call" | custom-call | tf_op jit(solution)/shard_map/hub_pack/pallas_call | solution.py:80
  3.4 11.4 %all-to-all-start.1 = ((bf16[32,16,128]{2,1,0:T(8,128)(2,1)}), bf16[32,16,128]{2,1,0:T(8,128)(2,1)S(1)}, u32[]{:S(2)}, u32[]{:S(2)}) async-start(bf16[32,16,128]{2,1,0:T(8,128)(2,1)} %hub_pack.1), calls=%async_computation.1 | async-start | bytes 262144 | tf_op jit(solution)/shard_map/all_to_all | solution.py:778
  14.8 5.1 %halo_pack.1 = bf16[64,32,128]{2,1,0:T(8,128)(2,1)} custom-call(s32[32,64]{1,0:T(8,128)} %bitcast.8, s32[64]{0:T(128)} %send_counts.1, bf16[4096,128]{1,0:T(8,128)(2,1)} %features.3), custom_call_target="tpu_custom_call" | custom-call | tf_op jit(solution)/shard_map/halo_pack/pallas_call | solution.py:118
  19.9 4.7 %all-to-all-done.1.refs_0_ = bf16[32,16,128]{2,1,0:T(8,128)(2,1)S(1)} async-done(((bf16[32,16,128]{2,1,0:T(8,128)(2,1)}), bf16[32,16,128]{2,1,0:T(8,128)(2,1)S(1)}, u32[]{:S(2)}, u32[]{:S(2)}) %all-to-all-start.1) | async-done | bytes 131104 | tf_op jit(solution)/shard_map/all_to_all | solution.py:778
  24.6 5.5 %all-to-all-start = ((bf16[64,32,128]{2,1,0:T(8,128)(2,1)}), bf16[64,32,128]{2,1,0:T(8,128)(2,1)S(1)}, u32[]{:S(2)}, u32[]{:S(2)}) async-start(bf16[64,32,128]{2,1,0:T(8,128)(2,1)} %halo_pack.1), calls=%async_computation | async-start | bytes 1048576 | tf_op jit(solution)/shard_map/all_to_all | solution.py:778
  30.1 1.6 %collective-permute-start = (bf16[32,16,128]{2,1,0:T(8,128)(2,1)S(1)}, bf16[32,16,128]{2,1,0:T(8,128)(2,1)S(1)}, u32[]{:S(2)}, u32[]{:S(2)}) collective-permute-start(bf16[32,16,128]{2,1,0:T(8,128)(2,1)S(1)} %all-to-all-done.1.refs_0_), channel_id=1, source_target_pairs={{0,1},{1,2},{2,3},{3,0},{4,5},{5,6},{6,7},{7,4},{8,9},{9,10},{10,1... | collective-permute-start | bytes 393224 | tf_op jit(solution)/shard_map/ppermute | solution.py:770
  31.7 2.7 %collective-permute-start.1 = (bf16[32,16,128]{2,1,0:T(8,128)(2,1)S(1)}, bf16[32,16,128]{2,1,0:T(8,128)(2,1)S(1)}, u32[]{:S(2)}, u32[]{:S(2)}) collective-permute-start(bf16[32,16,128]{2,1,0:T(8,128)(2,1)S(1)} %all-to-all-done.1.refs_0_), channel_id=1, source_target_pairs={{0,2},{1,3},{2,0},{3,1},{4,6},{5,7},{6,4},{7,5},{8,10},{9,11},{10,... | collective-permute-start | bytes 393224 | tf_op jit(solution)/shard_map/ppermute | solution.py:770
  34.4 1.4 %collective-permute-start.2 = (bf16[32,16,128]{2,1,0:T(8,128)(2,1)S(1)}, bf16[32,16,128]{2,1,0:T(8,128)(2,1)S(1)}, u32[]{:S(2)}, u32[]{:S(2)}) collective-permute-start(bf16[32,16,128]{2,1,0:T(8,128)(2,1)S(1)} %all-to-all-done.1.refs_0_), channel_id=1, source_target_pairs={{0,3},{1,0},{2,1},{3,2},{4,7},{5,4},{6,5},{7,6},{8,11},{9,8},{10,9... | collective-permute-start | bytes 393224 | tf_op jit(solution)/shard_map/ppermute | solution.py:770
  35.8 1.1 collective-permute-done.refs_1_
  36.9 0.0 collective-permute-start.4
  36.9 3.8 %collective-permute-done.1.refs_2_ = bf16[32,16,128]{2,1,0:T(8,128)(2,1)S(1)} collective-permute-done((bf16[32,16,128]{2,1,0:T(8,128)(2,1)S(1)}, bf16[32,16,128]{2,1,0:T(8,128)(2,1)S(1)}, u32[]{:S(2)}, u32[]{:S(2)}) %collective-permute-start.1) | collective-permute-done | bytes 131104 | tf_op jit(solution)/shard_map/ppermute | solution.py:770
  40.7 0.0 collective-permute-done.2.refs_3_
  40.7 0.5 collective-permute-start.6
  41.9 0.0 collective-permute-done.3.refs_4_
  41.9 0.2 collective-permute-done.5.refs_6_
  42.1 0.2 collective-permute-done.6.refs_7_
  42.3 4.9 %all-to-all-done = bf16[64,32,128]{2,1,0:T(8,128)(2,1)S(1)} async-done(((bf16[64,32,128]{2,1,0:T(8,128)(2,1)}), bf16[64,32,128]{2,1,0:T(8,128)(2,1)S(1)}, u32[]{:S(2)}, u32[]{:S(2)}) %all-to-all-start) | async-done | bytes 524320 | tf_op jit(solution)/shard_map/all_to_all | solution.py:778
  47.2 8.6 %forward.1 = (bf16[4096,256]{1,0:T(8,128)(2,1)}, bf16[4096,128]{1,0:T(8,128)(2,1)}, f32[4096,128]{1,0:T(8,128)}, bf16[512,128]{1,0:T(8,128)(2,1)}) custom-call(s32[128]{0:T(128)S(1)} %copy-done.3, s32[128]{0:T(128)S(1)} %copy-done.4, s32[1]{0:T(128)S(6)} %copy.21.count, bf16[128,128,128]{2,1,0:T(8,128)(2,1)} %weights.5, bf16[32,8,16,128]{3,2,1,0:T(8,128)(2,1)} %bitcast.7, ...), custom_call_target="tpu_custom_call" | custom-call | tf_op jit(solution)/shard_map/forward/pallas_call | solution.py:297
  55.8 6.1 %all-to-all-start.2 = ((bf16[32,16,128]{2,1,0:T(8,128)(2,1)}), bf16[32,16,128]{2,1,0:T(8,128)(2,1)S(1)}, u32[]{:S(2)}, u32[]{:S(2)}) async-start(bf16[32,16,128]{2,1,0:T(8,128)(2,1)} %bitcast.3), calls=%async_computation.2 | async-start | bytes 262144 | tf_op jit(solution)/shard_map/all_to_all | solution.py:778
  61.9 4.7 %backward_far.1 = (bf16[64,32,128]{2,1,0:T(8,128)(2,1)}, bf16[4,32,16,128]{3,2,1,0:T(8,128)(2,1)S(1)}, bf16[4,32,16,128]{3,2,1,0:T(8,128)(2,1)S(1)}) custom-call(s32[128]{0:T(128)S(1)} %copy-done.3, s32[128]{0:T(128)S(1)} %copy-done.4, s32[1]{0:T(128)S(6)} %copy.21.count, bf16[128,128,128]{2,1,0:T(8,128)(2,1)} %weights.5, ...), custom_call_target="tpu_custom_call" | custom-call | tf_op jit(solution)/shard_map/backward_far/pallas_call | solution.py:452
  66.6 0.0 copy-start.6
  66.6 0.0 copy-start.7
  66.7 0.0 copy-start
  66.7 0.0 copy-start.5
  66.7 5.0 %all-to-all-done.2.slices = bf16[32,16,128]{2,1,0:T(8,128)(2,1)S(1)} async-done(((bf16[32,16,128]{2,1,0:T(8,128)(2,1)}), bf16[32,16,128]{2,1,0:T(8,128)(2,1)S(1)}, u32[]{:S(2)}, u32[]{:S(2)}) %all-to-all-start.2) | async-done | bytes 131104 | tf_op jit(solution)/shard_map/all_to_all | solution.py:778
  71.7 5.4 %all-to-all-start.4 = ((bf16[64,32,128]{2,1,0:T(8,128)(2,1)}), bf16[64,32,128]{2,1,0:T(8,128)(2,1)S(1)}, u32[]{:S(2)}, u32[]{:S(2)}) async-start(bf16[64,32,128]{2,1,0:T(8,128)(2,1)} %get-tuple-element.30), calls=%async_computation.4 | async-start | bytes 1048576 | tf_op jit(solution)/shard_map/all_to_all | solution.py:778
  77.1 0.2 collective-permute-start.7
  77.3 0.2 fold.1.w_near
  77.5 0.4 collective-permute-start.8
  78.0 1.2 %collective-permute-done.8.w_far = bf16[2,16,128]{2,1,0:T(8,128)(2,1)S(1)} collective-permute-done((bf16[2,16,128]{2,1,0:T(8,128)(2,1)S(1)}, bf16[2,16,128]{2,1,0:T(8,128)(2,1)S(1)}, u32[]{:S(2)}, u32[]{:S(2)}) %collective-permute-start.8) | collective-permute-done | bytes 8224 | tf_op jit(solution)/shard_map/ppermute | solution.py:774
  79.1 0.0 collective-permute-done.7.far
  79.1 0.3 join.1
  79.4 1.3 %collective-permute-start.9 = (bf16[34,16,128]{2,1,0:T(8,128)(2,1)S(1)}, bf16[34,16,128]{2,1,0:T(8,128)(2,1)S(1)}, u32[]{:S(2)}, u32[]{:S(2)}) collective-permute-start(bf16[34,16,128]{2,1,0:T(8,128)(2,1)S(1)} %get-tuple-element.26), channel_id=1, source_target_pairs={{0,1},{1,2},{2,3},{3,0},{4,5},{5,6},{6,7},{7,4},{8,9},{9,10},{10,1... | collective-permute-start | bytes 417800 | tf_op jit(solution)/shard_map/ppermute | solution.py:770
  80.8 2.2 %collective-permute-start.10 = (bf16[34,16,128]{2,1,0:T(8,128)(2,1)S(1)}, bf16[34,16,128]{2,1,0:T(8,128)(2,1)S(1)}, u32[]{:S(2)}, u32[]{:S(2)}) collective-permute-start(bf16[34,16,128]{2,1,0:T(8,128)(2,1)S(1)} %get-tuple-element.27), channel_id=1, source_target_pairs={{0,2},{1,3},{2,0},{3,1},{4,6},{5,7},{6,4},{7,5},{8,10},{9,11},{10,... | collective-permute-start | bytes 417800 | tf_op jit(solution)/shard_map/ppermute | solution.py:770
  83.0 1.8 %collective-permute-start.11 = (bf16[34,16,128]{2,1,0:T(8,128)(2,1)S(1)}, bf16[34,16,128]{2,1,0:T(8,128)(2,1)S(1)}, u32[]{:S(2)}, u32[]{:S(2)}) collective-permute-start(bf16[34,16,128]{2,1,0:T(8,128)(2,1)S(1)} %get-tuple-element.28), channel_id=1, source_target_pairs={{0,3},{1,0},{2,1},{3,2},{4,7},{5,4},{6,5},{7,6},{8,11},{9,8},{10,9... | collective-permute-start | bytes 417800 | tf_op jit(solution)/shard_map/ppermute | solution.py:770
  84.8 2.2 %collective-permute-done.9.hub1 = bf16[34,16,128]{2,1,0:T(8,128)(2,1)S(1)} collective-permute-done((bf16[34,16,128]{2,1,0:T(8,128)(2,1)S(1)}, bf16[34,16,128]{2,1,0:T(8,128)(2,1)S(1)}, u32[]{:S(2)}, u32[]{:S(2)}) %collective-permute-start.9) | collective-permute-done | bytes 139296 | tf_op jit(solution)/shard_map/ppermute | solution.py:770
  87.0 2.7 %collective-permute-done.10.hub2 = bf16[34,16,128]{2,1,0:T(8,128)(2,1)S(1)} collective-permute-done((bf16[34,16,128]{2,1,0:T(8,128)(2,1)S(1)}, bf16[34,16,128]{2,1,0:T(8,128)(2,1)S(1)}, u32[]{:S(2)}, u32[]{:S(2)}) %collective-permute-start.10) | collective-permute-done | bytes 139296 | tf_op jit(solution)/shard_map/ppermute | solution.py:770
  89.7 0.3 collective-permute-done.11.hub3
  90.0 1.0 merge.1
  91.0 3.2 %all-to-all-done.4 = bf16[64,32,128]{2,1,0:T(8,128)(2,1)S(1)} async-done(((bf16[64,32,128]{2,1,0:T(8,128)(2,1)}), bf16[64,32,128]{2,1,0:T(8,128)(2,1)S(1)}, u32[]{:S(2)}, u32[]{:S(2)}) %all-to-all-start.4) | async-done | bytes 524320 | tf_op jit(solution)/shard_map/all_to_all | solution.py:778
  94.2 6.7 %all-to-all-start.3 = ((bf16[32,32,128]{2,1,0:T(8,128)(2,1)}), bf16[32,32,128]{2,1,0:T(8,128)(2,1)S(1)}, u32[]{:S(2)}, u32[]{:S(2)}) async-start(bf16[32,32,128]{2,1,0:T(8,128)(2,1)} %merge.1), calls=%async_computation.3 | async-start | bytes 524288 | tf_op jit(solution)/shard_map/all_to_all | solution.py:778
  100.9 0.1 copy.18
  101.0 0.1 reshape.30.ids_across
  101.1 0.1 copy.19
  101.2 0.1 convert_element_type.6.ids_down
  101.3 6.6 %own_rows.1 = (f32[4096,128]{1,0:T(8,128)}, f32[128,128]{1,0:T(8,128)S(1)}) custom-call(s32[128]{0:T(128)S(1)} %copy-done.3, s32[128]{0:T(128)S(1)} %copy-done.4, s32[1]{0:T(128)S(6)} %copy.21.count, s32[16]{0:T(128)S(1)} %copy-done.5, bf16[128,128,128]{2,1,0:T(8,128)(2,1)} %weights.5, bf16[4096,128]{1,0:T(8,128)(2,1)S(1)} %copy-done, ...), custom_call_target="tpu_custom_call" | custom-call | tf_op jit(solution)/shard_map/own_rows/pallas_call | solution.py:576
  107.9 4.7 %all-to-all-done.3.received = bf16[32,32,128]{2,1,0:T(8,128)(2,1)S(1)} async-done(((bf16[32,32,128]{2,1,0:T(8,128)(2,1)}), bf16[32,32,128]{2,1,0:T(8,128)(2,1)S(1)}, u32[]{:S(2)}, u32[]{:S(2)}) %all-to-all-start.3) | async-done | bytes 262176 | tf_op jit(solution)/shard_map/all_to_all | solution.py:778
  112.6 1.6 %finish.1 = (f32[4096,128]{1,0:T(8,128)}, f32[128,256]{1,0:T(8,128)}, f32[128,256]{1,0:T(8,128)}) custom-call(s32[16]{0:T(128)S(1)} %copy-done.5, bf16[32,32,128]{2,1,0:T(8,128)(2,1)S(1)} %all-to-all-done.3.received, f32[128,128]{1,0:T(8,128)S(1)} %get-tuple-element.31.around, f32[4096,128]{1,0:T(8,128)} %get-tuple-element.32.grad_nodes), custom_call_target="tpu_custom_call", output_to_operand_aliasing={{0}: (3, {})} | custom-call | tf_op jit(solution)/shard_map/finish/pallas_call | solution.py:748
  (16 shorter events, 0.0 us)
Async XLA Ops:
  0.6 46.6 %copy-start.3 = (s32[128]{0:T(128)S(1)}, s32[128]{0:T(128)}, u32[]{:S(2)}) copy-start(s32[128]{0:T(128)} %targets.5) | copy-start | bytes 1540
  0.6 46.6 %copy-start.4 = (s32[128]{0:T(128)S(1)}, s32[128]{0:T(128)}, u32[]{:S(2)}) copy-start(s32[128]{0:T(128)} %sources.5) | copy-start | bytes 1540
  0.7 46.6 %copy-start.1 = (bf16[128,256]{1,0:T(8,128)(2,1)S(1)}, bf16[128,256]{1,0:T(8,128)(2,1)}, u32[]{:S(2)}) copy-start(bf16[128,256]{1,0:T(8,128)(2,1)} %refs_9_.1) | copy-start | bytes 196612
  0.7 46.6 %copy-start.2 = (bf16[128,256]{1,0:T(8,128)(2,1)S(1)}, bf16[128,256]{1,0:T(8,128)(2,1)}, u32[]{:S(2)}) copy-start(bf16[128,256]{1,0:T(8,128)(2,1)} %refs_10_.1) | copy-start | bytes 196612
  3.4 21.2 %all-to-all-start.1 = ((bf16[32,16,128]{2,1,0:T(8,128)(2,1)}), bf16[32,16,128]{2,1,0:T(8,128)(2,1)S(1)}, u32[]{:S(2)}, u32[]{:S(2)}) async-start(bf16[32,16,128]{2,1,0:T(8,128)(2,1)} %hub_pack.1), calls=%async_computation.1 | async-start | bytes 262144 | tf_op jit(solution)/shard_map/all_to_all | solution.py:778
  24.6 22.6 %all-to-all-start = ((bf16[64,32,128]{2,1,0:T(8,128)(2,1)}), bf16[64,32,128]{2,1,0:T(8,128)(2,1)S(1)}, u32[]{:S(2)}, u32[]{:S(2)}) async-start(bf16[64,32,128]{2,1,0:T(8,128)(2,1)} %halo_pack.1), calls=%async_computation | async-start | bytes 1048576 | tf_op jit(solution)/shard_map/all_to_all | solution.py:778
  30.1 6.8 %collective-permute-start = (bf16[32,16,128]{2,1,0:T(8,128)(2,1)S(1)}, bf16[32,16,128]{2,1,0:T(8,128)(2,1)S(1)}, u32[]{:S(2)}, u32[]{:S(2)}) collective-permute-start(bf16[32,16,128]{2,1,0:T(8,128)(2,1)S(1)} %all-to-all-done.1.refs_0_), channel_id=1, source_target_pairs={{0,1},{1,2},{2,3},{3,0},{4,5},{5,6},{6,7},{7,4},{8,9},{9,10},{10,1... | collective-permute-start | bytes 393224 | tf_op jit(solution)/shard_map/ppermute | solution.py:770
  31.7 9.1 %collective-permute-start.1 = (bf16[32,16,128]{2,1,0:T(8,128)(2,1)S(1)}, bf16[32,16,128]{2,1,0:T(8,128)(2,1)S(1)}, u32[]{:S(2)}, u32[]{:S(2)}) collective-permute-start(bf16[32,16,128]{2,1,0:T(8,128)(2,1)S(1)} %all-to-all-done.1.refs_0_), channel_id=1, source_target_pairs={{0,2},{1,3},{2,0},{3,1},{4,6},{5,7},{6,4},{7,5},{8,10},{9,11},{10,... | collective-permute-start | bytes 393224 | tf_op jit(solution)/shard_map/ppermute | solution.py:770
  34.4 6.3 %collective-permute-start.2 = (bf16[32,16,128]{2,1,0:T(8,128)(2,1)S(1)}, bf16[32,16,128]{2,1,0:T(8,128)(2,1)S(1)}, u32[]{:S(2)}, u32[]{:S(2)}) collective-permute-start(bf16[32,16,128]{2,1,0:T(8,128)(2,1)S(1)} %all-to-all-done.1.refs_0_), channel_id=1, source_target_pairs={{0,3},{1,0},{2,1},{3,2},{4,7},{5,4},{6,5},{7,6},{8,11},{9,8},{10,9... | collective-permute-start | bytes 393224 | tf_op jit(solution)/shard_map/ppermute | solution.py:770
  35.8 6.1 %collective-permute-start.3 = (bf16[32,16,128]{2,1,0:T(8,128)(2,1)S(1)}, bf16[32,16,128]{2,1,0:T(8,128)(2,1)S(1)}, u32[]{:S(2)}, u32[]{:S(2)}) collective-permute-start(bf16[32,16,128]{2,1,0:T(8,128)(2,1)S(1)} %all-to-all-done.1.refs_0_), channel_id=1, source_target_pairs={{0,4},{4,0},{1,5},{5,1},{2,6},{6,2},{3,7},{7,3},{8,12},{12,8},{9,1... | collective-permute-start | bytes 393224 | tf_op jit(solution)/shard_map/ppermute | solution.py:774
  36.9 5.0 %collective-permute-start.4 = (bf16[32,16,128]{2,1,0:T(8,128)(2,1)S(1)}, bf16[32,16,128]{2,1,0:T(8,128)(2,1)S(1)}, u32[]{:S(2)}, u32[]{:S(2)}) collective-permute-start(bf16[32,16,128]{2,1,0:T(8,128)(2,1)S(1)} %collective-permute-done.refs_1_), channel_id=1, source_target_pairs={{0,4},{4,0},{1,5},{5,1},{2,6},{6,2},{3,7},{7,3},{8,12},{12,8},{9,1... | collective-permute-start | bytes 393224 | tf_op jit(solution)/shard_map/ppermute | solution.py:774
  40.7 1.3 %collective-permute-start.5 = (bf16[32,16,128]{2,1,0:T(8,128)(2,1)S(1)}, bf16[32,16,128]{2,1,0:T(8,128)(2,1)S(1)}, u32[]{:S(2)}, u32[]{:S(2)}) collective-permute-start(bf16[32,16,128]{2,1,0:T(8,128)(2,1)S(1)} %collective-permute-done.1.refs_2_), channel_id=1, source_target_pairs={{0,4},{4,0},{1,5},{5,1},{2,6},{6,2},{3,7},{7,3},{8,12},{12,8},{9,1... | collective-permute-start | bytes 393224 | tf_op jit(solution)/shard_map/ppermute | solution.py:774
  40.7 1.5 %collective-permute-start.6 = (bf16[32,16,128]{2,1,0:T(8,128)(2,1)S(1)}, bf16[32,16,128]{2,1,0:T(8,128)(2,1)S(1)}, u32[]{:S(2)}, u32[]{:S(2)}) collective-permute-start(bf16[32,16,128]{2,1,0:T(8,128)(2,1)S(1)} %collective-permute-done.2.refs_3_), channel_id=1, source_target_pairs={{0,4},{4,0},{1,5},{5,1},{2,6},{6,2},{3,7},{7,3},{8,12},{12,8},{9,1... | collective-permute-start | bytes 393224 | tf_op jit(solution)/shard_map/ppermute | solution.py:774
  55.8 15.9 %all-to-all-start.2 = ((bf16[32,16,128]{2,1,0:T(8,128)(2,1)}), bf16[32,16,128]{2,1,0:T(8,128)(2,1)S(1)}, u32[]{:S(2)}, u32[]{:S(2)}) async-start(bf16[32,16,128]{2,1,0:T(8,128)(2,1)} %bitcast.3), calls=%async_computation.2 | async-start | bytes 262144 | tf_op jit(solution)/shard_map/all_to_all | solution.py:778
  66.6 34.3 %copy-start.6 = (s32[64,32]{0,1:T(8,128)S(1)}, s32[64,32]{0,1:T(8,128)}, u32[]{:S(2)}) copy-start(s32[64,32]{0,1:T(8,128)} %param.16) | copy-start | bytes 24580
  66.6 34.3 %copy-start.7 = (s32[64]{0:T(128)S(1)}, s32[64]{0:T(128)}, u32[]{:S(2)}) copy-start(s32[64]{0:T(128)} %send_counts.1) | copy-start | bytes 772
  66.7 34.6 %copy-start = (bf16[4096,128]{1,0:T(8,128)(2,1)S(1)}, bf16[4096,128]{1,0:T(8,128)(2,1)}, u32[]{:S(2)}) copy-start(bf16[4096,128]{1,0:T(8,128)(2,1)} %get-tuple-element.21.grad_agg) | copy-start | bytes 3145732
  66.7 34.6 %copy-start.5 = (s32[16]{0:T(128)S(1)}, s32[16]{0:T(128)}, u32[]{:S(2)}) copy-start(s32[16]{0:T(128)} %hub_rows.5) | copy-start | bytes 196
  71.7 22.5 %all-to-all-start.4 = ((bf16[64,32,128]{2,1,0:T(8,128)(2,1)}), bf16[64,32,128]{2,1,0:T(8,128)(2,1)S(1)}, u32[]{:S(2)}, u32[]{:S(2)}) async-start(bf16[64,32,128]{2,1,0:T(8,128)(2,1)} %get-tuple-element.30), calls=%async_computation.4 | async-start | bytes 1048576 | tf_op jit(solution)/shard_map/all_to_all | solution.py:778
  77.1 2.0 %collective-permute-start.7 = (bf16[4,32,16,128]{3,2,1,0:T(8,128)(2,1)S(1)}, bf16[4,32,16,128]{3,2,1,0:T(8,128)(2,1)S(1)}, u32[]{:S(2)}, u32[]{:S(2)}) collective-permute-start(bf16[4,32,16,128]{3,2,1,0:T(8,128)(2,1)S(1)} %get-tuple-element.23), channel_id=1, source_target_pairs={{0,4},{4,0},{1,5},{5,1},{2,6},{6,2},{3,7},{7,3},{8,12},{12,8},{9,1... | collective-permute-start | bytes 1572872 | tf_op jit(solution)/shard_map/ppermute | solution.py:774
  77.5 1.6 %collective-permute-start.8 = (bf16[2,16,128]{2,1,0:T(8,128)(2,1)S(1)}, bf16[2,16,128]{2,1,0:T(8,128)(2,1)S(1)}, u32[]{:S(2)}, u32[]{:S(2)}) collective-permute-start(bf16[2,16,128]{2,1,0:T(8,128)(2,1)S(1)} %fold.1.w_near), channel_id=1, source_target_pairs={{0,4},{4,0},{1,5},{5,1},{2,6},{6,2},{3,7},{7,3},{8,12},{12,8},{9,1... | collective-permute-start | bytes 24584 | tf_op jit(solution)/shard_map/ppermute | solution.py:774
  79.4 7.6 %collective-permute-start.9 = (bf16[34,16,128]{2,1,0:T(8,128)(2,1)S(1)}, bf16[34,16,128]{2,1,0:T(8,128)(2,1)S(1)}, u32[]{:S(2)}, u32[]{:S(2)}) collective-permute-start(bf16[34,16,128]{2,1,0:T(8,128)(2,1)S(1)} %get-tuple-element.26), channel_id=1, source_target_pairs={{0,1},{1,2},{2,3},{3,0},{4,5},{5,6},{6,7},{7,4},{8,9},{9,10},{10,1... | collective-permute-start | bytes 417800 | tf_op jit(solution)/shard_map/ppermute | solution.py:770
  80.8 8.9 %collective-permute-start.10 = (bf16[34,16,128]{2,1,0:T(8,128)(2,1)S(1)}, bf16[34,16,128]{2,1,0:T(8,128)(2,1)S(1)}, u32[]{:S(2)}, u32[]{:S(2)}) collective-permute-start(bf16[34,16,128]{2,1,0:T(8,128)(2,1)S(1)} %get-tuple-element.27), channel_id=1, source_target_pairs={{0,2},{1,3},{2,0},{3,1},{4,6},{5,7},{6,4},{7,5},{8,10},{9,11},{10,... | collective-permute-start | bytes 417800 | tf_op jit(solution)/shard_map/ppermute | solution.py:770
  83.0 7.0 %collective-permute-start.11 = (bf16[34,16,128]{2,1,0:T(8,128)(2,1)S(1)}, bf16[34,16,128]{2,1,0:T(8,128)(2,1)S(1)}, u32[]{:S(2)}, u32[]{:S(2)}) collective-permute-start(bf16[34,16,128]{2,1,0:T(8,128)(2,1)S(1)} %get-tuple-element.28), channel_id=1, source_target_pairs={{0,3},{1,0},{2,1},{3,2},{4,7},{5,4},{6,5},{7,6},{8,11},{9,8},{10,9... | collective-permute-start | bytes 417800 | tf_op jit(solution)/shard_map/ppermute | solution.py:770
  94.2 18.4 %all-to-all-start.3 = ((bf16[32,32,128]{2,1,0:T(8,128)(2,1)}), bf16[32,32,128]{2,1,0:T(8,128)(2,1)S(1)}, u32[]{:S(2)}, u32[]{:S(2)}) async-start(bf16[32,32,128]{2,1,0:T(8,128)(2,1)} %merge.1), calls=%async_computation.3 | async-start | bytes 524288 | tf_op jit(solution)/shard_map/all_to_all | solution.py:778

commit v8 on v7

--- a/solution.py
+++ b/solution.py
@@ -11,7 +11,7 @@
 BF16 = jnp.bfloat16
 F32 = jnp.float32
 CHUNK = 32
-ROWS = 1024
+SIZES = (1024, 1024, 1024, 512, 512)
 NEAR = 16
 TILE = 8
 PARTS = 4
@@ -220,13 +220,10 @@
         return carry
 
     lax.fori_loop(leading, chunks, more, 0)
-    grad_total[...] = jnp.zeros_like(grad_total)
-    per_chunk = ROWS // block
     for copy in late:
         copy.wait()
 
-    def outs(c):
-        rows = rows_at(c, ROWS)
+    def outs(rows):
         return [
             pltpu.make_async_copy(x.at[rows], y.at[rows], out_sems.at[n])
             for n, (x, y) in enumerate(
@@ -234,13 +231,13 @@
             )
         ]
 
-    def dense(c, carry):
-        rows = rows_at(c, ROWS)
-        blocks_at = pl.ds(c * per_chunk, per_chunk)
-        total = totals[blocks_at].reshape(ROWS, 2 * width)
+    def dense(start, size):
+        rows = pl.ds(start, size)
+        blocks_at = pl.ds(start // block, size // block)
+        total = totals[blocks_at].reshape(size, 2 * width)
         inverse = 1.0 / jnp.maximum(total[:, width:], 1.0)
         aggregate = (total[:, :width] * inverse).astype(BF16)
-        own = source_rows[blocks_at].reshape(ROWS, width)
+        own = source_rows[blocks_at].reshape(size, width)
         both = jnp.concatenate([own, aggregate], 1)
         preact = jnp.dot(both, w_both[...], preferred_element_type=F32)
         sigmoid = 0.5 * jnp.tanh(0.5 * preact) + 0.5
@@ -248,33 +245,34 @@
         hidden_all[rows] = activated.astype(BF16)
         slope = sigmoid + activated * (1.0 - sigmoid)
         grad_preact = (grads_in[rows].astype(F32) * slope).astype(BF16)
-        grad_total[...] += lax.dot_general(
+        term = lax.dot_general(
             both, grad_preact, (((0,), (0,)), ((), ())), preferred_element_type=F32
         )
+        grad_total[...] = term if start == 0 else grad_total[...] + term
         back = lax.dot_general(
             grad_preact, w_both[...], (((1,), (1,)), ((), ())), preferred_element_type=F32
         )
         self_all[rows] = back[:, :width]
         agg_all[rows] = (back[:, width:] * inverse).astype(BF16)
-        for copy in outs(c):
+        for copy in outs(rows):
             copy.start()
-        return carry
-
-    steps = node_rows // ROWS
-    for c in range(steps):
-        dense(c, 0)
+
+    parts_at = []
+    start = 0
+    for size in SIZES:
+        parts_at.append((start, size))
+        start += size
+    for start, size in parts_at:
+        dense(start, size)
     half = grad_total.shape[1] // 2
     w_all[: grad_total.shape[0]] = grad_total[:, :half].astype(BF16)
     w_all[grad_total.shape[0] :] = grad_total[:, half:].astype(BF16)
     w_copy = pltpu.make_async_copy(w_all, grad_w, sems.at[0])
     w_copy.start()
 
-    def drain(c, carry):
-        for copy in outs(c):
+    for start, size in parts_at:
+        for copy in outs(pl.ds(start, size)):
             copy.wait()
-        return carry
-
-    lax.fori_loop(0, steps, drain, 0)
     w_copy.wait()
 
 

time: 116 us -> 116 us (level)
  starting transfers between devices: 47.3 us -> 48.6 us
  transfers between devices with their start and end apart: 17 -> 17, of which waited for: 13 -> 13; matrix products, arithmetic and copies ran while one was open for 0% -> 0% of each run, Pallas kernels for 16% -> 15%
where the time goes in v8:
time: 116 us; the launch traced here: 115 us
  starting transfers between devices  48.6 us (42%)
  waiting for transfers between devices  34.2 us (29%)
  Pallas kernels  29.9 us (26%)
  between operations  1.67 us (1%)
    all_to_all x5, starting transfers between devices, swap(): return lax.all_to_all(value, axes, split_axis=0, concat_axis=0, tiled=True)  36.2 us
    all_to_all x5, waiting for transfers between devices, swap(): return lax.all_to_all(value, axes, split_axis=0, concat_axis=0, tiled=True)  22.7 us
    ppermute x6, starting transfers between devices, rep_shift(): lax.ppermute(value, 'rep', [(j, (j + shift) % REPS) for j in range(REPS)])  11.2 us
    ppermute x6, waiting for transfers between devices, rep_shift(): lax.ppermute(value, 'rep', [(j, (j + shift) % REPS) for j in range(REPS)])  9.98 us
    pallas_call x1, Pallas kernels, forward(): pl.pallas_call(forward_kernel, out_shape=shapes, in_specs=[smem()] * 3 +...  7.89 us
    pallas_call x1, Pallas kernels, own_rows(): pl.pallas_call(own_rows_kernel, out_shape=(jax.ShapeDtypeStruct((node_row...  6.56 us
    pallas_call x1, Pallas kernels, halo_pack(): pl.pallas_call(halo_pack_kernel, out_shape=jax.ShapeDtypeStruct((peers, s...  5.1 us
    pallas_call x1, Pallas kernels, backward_far(): pl.pallas_call(backward_far_kernel, out_shape=(halo, piece, piece), in_sp...  4.59 us
  transfers between devices with their start and end apart: 17, of which 13 were waited for; matrix products, arithmetic and copies ran while one was open for 0% of the time, Pallas kernels for 15%

profile of v8, /device:TPU:32, one launch (start us, length us, event | category | flops | bytes accessed | tf_op | source)
XLA Modules:
  0.0 114.7 jit_solution(12961123363925583699)
XLA Ops:
  0.7 2.7 %hub_pack.1 = bf16[32,16,128]{2,1,0:T(8,128)(2,1)} custom-call(s32[16]{0:T(128)} %hub_rows.5, bf16[4096,128]{1,0:T(8,128)(2,1)} %features.3), custom_call_target="tpu_custom_call" | custom-call | tf_op jit(solution)/shard_map/hub_pack/pallas_call | solution.py:80
  3.4 11.4 %all-to-all-start.1 = ((bf16[32,16,128]{2,1,0:T(8,128)(2,1)}), bf16[32,16,128]{2,1,0:T(8,128)(2,1)S(1)}, u32[]{:S(2)}, u32[]{:S(2)}) async-start(bf16[32,16,128]{2,1,0:T(8,128)(2,1)} %hub_pack.1), calls=%async_computation.1 | async-start | bytes 262144 | tf_op jit(solution)/shard_map/all_to_all | solution.py:776
  14.8 5.1 %halo_pack.1 = bf16[64,32,128]{2,1,0:T(8,128)(2,1)} custom-call(s32[32,64]{1,0:T(8,128)} %bitcast.8, s32[64]{0:T(128)} %send_counts.1, bf16[4096,128]{1,0:T(8,128)(2,1)} %features.3), custom_call_target="tpu_custom_call" | custom-call | tf_op jit(solution)/shard_map/halo_pack/pallas_call | solution.py:118
  19.9 4.7 %all-to-all-done.1.refs_0_ = bf16[32,16,128]{2,1,0:T(8,128)(2,1)S(1)} async-done(((bf16[32,16,128]{2,1,0:T(8,128)(2,1)}), bf16[32,16,128]{2,1,0:T(8,128)(2,1)S(1)}, u32[]{:S(2)}, u32[]{:S(2)}) %all-to-all-start.1) | async-done | bytes 131104 | tf_op jit(solution)/shard_map/all_to_all | solution.py:776
  24.6 5.5 %all-to-all-start = ((bf16[64,32,128]{2,1,0:T(8,128)(2,1)}), bf16[64,32,128]{2,1,0:T(8,128)(2,1)S(1)}, u32[]{:S(2)}, u32[]{:S(2)}) async-start(bf16[64,32,128]{2,1,0:T(8,128)(2,1)} %halo_pack.1), calls=%async_computation | async-start | bytes 1048576 | tf_op jit(solution)/shard_map/all_to_all | solution.py:776
  30.1 1.6 %collective-permute-start = (bf16[32,16,128]{2,1,0:T(8,128)(2,1)S(1)}, bf16[32,16,128]{2,1,0:T(8,128)(2,1)S(1)}, u32[]{:S(2)}, u32[]{:S(2)}) collective-permute-start(bf16[32,16,128]{2,1,0:T(8,128)(2,1)S(1)} %all-to-all-done.1.refs_0_), channel_id=1, source_target_pairs={{0,1},{1,2},{2,3},{3,0},{4,5},{5,6},{6,7},{7,4},{8,9},{9,10},{10,1... | collective-permute-start | bytes 393224 | tf_op jit(solution)/shard_map/ppermute | solution.py:768
  31.7 2.7 %collective-permute-start.1 = (bf16[32,16,128]{2,1,0:T(8,128)(2,1)S(1)}, bf16[32,16,128]{2,1,0:T(8,128)(2,1)S(1)}, u32[]{:S(2)}, u32[]{:S(2)}) collective-permute-start(bf16[32,16,128]{2,1,0:T(8,128)(2,1)S(1)} %all-to-all-done.1.refs_0_), channel_id=1, source_target_pairs={{0,2},{1,3},{2,0},{3,1},{4,6},{5,7},{6,4},{7,5},{8,10},{9,11},{10,... | collective-permute-start | bytes 393224 | tf_op jit(solution)/shard_map/ppermute | solution.py:768
  34.4 1.4 %collective-permute-start.2 = (bf16[32,16,128]{2,1,0:T(8,128)(2,1)S(1)}, bf16[32,16,128]{2,1,0:T(8,128)(2,1)S(1)}, u32[]{:S(2)}, u32[]{:S(2)}) collective-permute-start(bf16[32,16,128]{2,1,0:T(8,128)(2,1)S(1)} %all-to-all-done.1.refs_0_), channel_id=1, source_target_pairs={{0,3},{1,0},{2,1},{3,2},{4,7},{5,4},{6,5},{7,6},{8,11},{9,8},{10,9... | collective-permute-start | bytes 393224 | tf_op jit(solution)/shard_map/ppermute | solution.py:768
  35.8 0.0 collective-permute-start.3
  35.8 1.1 collective-permute-done.refs_1_
  36.9 0.0 collective-permute-start.4
  36.9 3.8 %collective-permute-done.1.refs_2_ = bf16[32,16,128]{2,1,0:T(8,128)(2,1)S(1)} collective-permute-done((bf16[32,16,128]{2,1,0:T(8,128)(2,1)S(1)}, bf16[32,16,128]{2,1,0:T(8,128)(2,1)S(1)}, u32[]{:S(2)}, u32[]{:S(2)}) %collective-permute-start.1) | collective-permute-done | bytes 131104 | tf_op jit(solution)/shard_map/ppermute | solution.py:768
  40.7 0.0 collective-permute-start.5
  40.7 0.5 collective-permute-start.6
  41.9 0.0 collective-permute-done.3.refs_4_
  41.9 0.2 collective-permute-done.5.refs_6_
  42.1 0.2 collective-permute-done.6.refs_7_
  42.3 4.9 %all-to-all-done = bf16[64,32,128]{2,1,0:T(8,128)(2,1)S(1)} async-done(((bf16[64,32,128]{2,1,0:T(8,128)(2,1)}), bf16[64,32,128]{2,1,0:T(8,128)(2,1)S(1)}, u32[]{:S(2)}, u32[]{:S(2)}) %all-to-all-start) | async-done | bytes 524320 | tf_op jit(solution)/shard_map/all_to_all | solution.py:776
  47.2 7.9 %forward.1 = (bf16[4096,256]{1,0:T(8,128)(2,1)}, bf16[4096,128]{1,0:T(8,128)(2,1)}, f32[4096,128]{1,0:T(8,128)}, bf16[512,128]{1,0:T(8,128)(2,1)}) custom-call(s32[128]{0:T(128)S(1)} %copy-done.3, s32[128]{0:T(128)S(1)} %copy-done.4, s32[1]{0:T(128)S(6)} %copy.21.count, bf16[128,128,128]{2,1,0:T(8,128)(2,1)} %weights.5, bf16[32,8,16,128]{3,2,1,0:T(8,128)(2,1)} %bitcast.7, ...), custom_call_target="tpu_custom_call" | custom-call | tf_op jit(solution)/shard_map/forward/pallas_call | solution.py:295
  55.1 6.8 %all-to-all-start.2 = ((bf16[32,16,128]{2,1,0:T(8,128)(2,1)}), bf16[32,16,128]{2,1,0:T(8,128)(2,1)S(1)}, u32[]{:S(2)}, u32[]{:S(2)}) async-start(bf16[32,16,128]{2,1,0:T(8,128)(2,1)} %bitcast.3), calls=%async_computation.2 | async-start | bytes 262144 | tf_op jit(solution)/shard_map/all_to_all | solution.py:776
  62.0 4.6 %backward_far.1 = (bf16[64,32,128]{2,1,0:T(8,128)(2,1)}, bf16[4,32,16,128]{3,2,1,0:T(8,128)(2,1)S(1)}, bf16[4,32,16,128]{3,2,1,0:T(8,128)(2,1)S(1)}) custom-call(s32[128]{0:T(128)S(1)} %copy-done.3, s32[128]{0:T(128)S(1)} %copy-done.4, s32[1]{0:T(128)S(6)} %copy.21.count, bf16[128,128,128]{2,1,0:T(8,128)(2,1)} %weights.5, ...), custom_call_target="tpu_custom_call" | custom-call | tf_op jit(solution)/shard_map/backward_far/pallas_call | solution.py:450
  66.5 0.0 copy-start.6
  66.6 0.0 copy-start.7
  66.6 0.0 copy-start
  66.6 0.0 copy-start.5
  66.6 5.0 %all-to-all-done.2.slices = bf16[32,16,128]{2,1,0:T(8,128)(2,1)S(1)} async-done(((bf16[32,16,128]{2,1,0:T(8,128)(2,1)}), bf16[32,16,128]{2,1,0:T(8,128)(2,1)S(1)}, u32[]{:S(2)}, u32[]{:S(2)}) %all-to-all-start.2) | async-done | bytes 131104 | tf_op jit(solution)/shard_map/all_to_all | solution.py:776
  71.6 5.8 %all-to-all-start.4 = ((bf16[64,32,128]{2,1,0:T(8,128)(2,1)}), bf16[64,32,128]{2,1,0:T(8,128)(2,1)S(1)}, u32[]{:S(2)}, u32[]{:S(2)}) async-start(bf16[64,32,128]{2,1,0:T(8,128)(2,1)} %get-tuple-element.30), calls=%async_computation.4 | async-start | bytes 1048576 | tf_op jit(solution)/shard_map/all_to_all | solution.py:776
  77.4 0.2 collective-permute-start.7
  77.7 0.2 fold.1.w_near
  77.8 0.4 collective-permute-start.8
  78.3 1.2 %collective-permute-done.8.w_far = bf16[2,16,128]{2,1,0:T(8,128)(2,1)S(1)} collective-permute-done((bf16[2,16,128]{2,1,0:T(8,128)(2,1)S(1)}, bf16[2,16,128]{2,1,0:T(8,128)(2,1)S(1)}, u32[]{:S(2)}, u32[]{:S(2)}) %collective-permute-start.8) | collective-permute-done | bytes 8224 | tf_op jit(solution)/shard_map/ppermute | solution.py:772
  79.5 0.3 join.1
  79.8 0.9 collective-permute-start.9
  80.7 2.6 %collective-permute-start.10 = (bf16[34,16,128]{2,1,0:T(8,128)(2,1)S(1)}, bf16[34,16,128]{2,1,0:T(8,128)(2,1)S(1)}, u32[]{:S(2)}, u32[]{:S(2)}) collective-permute-start(bf16[34,16,128]{2,1,0:T(8,128)(2,1)S(1)} %get-tuple-element.27), channel_id=1, source_target_pairs={{0,2},{1,3},{2,0},{3,1},{4,6},{5,7},{6,4},{7,5},{8,10},{9,11},{10,... | collective-permute-start | bytes 417800 | tf_op jit(solution)/shard_map/ppermute | solution.py:768
  83.3 1.9 %collective-permute-start.11 = (bf16[34,16,128]{2,1,0:T(8,128)(2,1)S(1)}, bf16[34,16,128]{2,1,0:T(8,128)(2,1)S(1)}, u32[]{:S(2)}, u32[]{:S(2)}) collective-permute-start(bf16[34,16,128]{2,1,0:T(8,128)(2,1)S(1)} %get-tuple-element.28), channel_id=1, source_target_pairs={{0,3},{1,0},{2,1},{3,2},{4,7},{5,4},{6,5},{7,6},{8,11},{9,8},{10,9... | collective-permute-start | bytes 417800 | tf_op jit(solution)/shard_map/ppermute | solution.py:768
  85.3 2.1 %collective-permute-done.9.hub1 = bf16[34,16,128]{2,1,0:T(8,128)(2,1)S(1)} collective-permute-done((bf16[34,16,128]{2,1,0:T(8,128)(2,1)S(1)}, bf16[34,16,128]{2,1,0:T(8,128)(2,1)S(1)}, u32[]{:S(2)}, u32[]{:S(2)}) %collective-permute-start.9) | collective-permute-done | bytes 139296 | tf_op jit(solution)/shard_map/ppermute | solution.py:768
  87.3 2.7 %collective-permute-done.10.hub2 = bf16[34,16,128]{2,1,0:T(8,128)(2,1)S(1)} collective-permute-done((bf16[34,16,128]{2,1,0:T(8,128)(2,1)S(1)}, bf16[34,16,128]{2,1,0:T(8,128)(2,1)S(1)}, u32[]{:S(2)}, u32[]{:S(2)}) %collective-permute-start.10) | collective-permute-done | bytes 139296 | tf_op jit(solution)/shard_map/ppermute | solution.py:768
  90.0 0.3 collective-permute-done.11.hub3
  90.4 1.0 merge.1
  91.3 3.2 %all-to-all-done.4 = bf16[64,32,128]{2,1,0:T(8,128)(2,1)S(1)} async-done(((bf16[64,32,128]{2,1,0:T(8,128)(2,1)}), bf16[64,32,128]{2,1,0:T(8,128)(2,1)S(1)}, u32[]{:S(2)}, u32[]{:S(2)}) %all-to-all-start.4) | async-done | bytes 524320 | tf_op jit(solution)/shard_map/all_to_all | solution.py:776
  94.5 6.7 %all-to-all-start.3 = ((bf16[32,32,128]{2,1,0:T(8,128)(2,1)}), bf16[32,32,128]{2,1,0:T(8,128)(2,1)S(1)}, u32[]{:S(2)}, u32[]{:S(2)}) async-start(bf16[32,32,128]{2,1,0:T(8,128)(2,1)} %merge.1), calls=%async_computation.3 | async-start | bytes 524288 | tf_op jit(solution)/shard_map/all_to_all | solution.py:776
  101.3 0.1 copy.18
  101.3 0.1 reshape.30.ids_across
  101.4 0.1 copy.19
  101.5 0.1 convert_element_type.6.ids_down
  101.6 6.6 %own_rows.1 = (f32[4096,128]{1,0:T(8,128)}, f32[128,128]{1,0:T(8,128)S(1)}) custom-call(s32[128]{0:T(128)S(1)} %copy-done.3, s32[128]{0:T(128)S(1)} %copy-done.4, s32[1]{0:T(128)S(6)} %copy.21.count, s32[16]{0:T(128)S(1)} %copy-done.5, bf16[128,128,128]{2,1,0:T(8,128)(2,1)} %weights.5, bf16[4096,128]{1,0:T(8,128)(2,1)S(1)} %copy-done, ...), custom_call_target="tpu_custom_call" | custom-call | tf_op jit(solution)/shard_map/own_rows/pallas_call | solution.py:574
  108.2 4.8 %all-to-all-done.3.received = bf16[32,32,128]{2,1,0:T(8,128)(2,1)S(1)} async-done(((bf16[32,32,128]{2,1,0:T(8,128)(2,1)}), bf16[32,32,128]{2,1,0:T(8,128)(2,1)S(1)}, u32[]{:S(2)}, u32[]{:S(2)}) %all-to-all-start.3) | async-done | bytes 262176 | tf_op jit(solution)/shard_map/all_to_all | solution.py:776
  113.0 1.6 %finish.1 = (f32[4096,128]{1,0:T(8,128)}, f32[128,256]{1,0:T(8,128)}, f32[128,256]{1,0:T(8,128)}) custom-call(s32[16]{0:T(128)S(1)} %copy-done.5, bf16[32,32,128]{2,1,0:T(8,128)(2,1)S(1)} %all-to-all-done.3.received, f32[128,128]{1,0:T(8,128)S(1)} %get-tuple-element.31.around, f32[4096,128]{1,0:T(8,128)} %get-tuple-element.32.grad_nodes), custom_call_target="tpu_custom_call", output_to_operand_aliasing={{0}: (3, {})} | custom-call | tf_op jit(solution)/shard_map/finish/pallas_call | solution.py:746
  (16 shorter events, 0.0 us)
Async XLA Ops:
  0.6 46.6 %copy-start.3 = (s32[128]{0:T(128)S(1)}, s32[128]{0:T(128)}, u32[]{:S(2)}) copy-start(s32[128]{0:T(128)} %targets.5) | copy-start | bytes 1540
  0.6 46.6 %copy-start.4 = (s32[128]{0:T(128)S(1)}, s32[128]{0:T(128)}, u32[]{:S(2)}) copy-start(s32[128]{0:T(128)} %sources.5) | copy-start | bytes 1540
  0.7 46.6 %copy-start.1 = (bf16[128,256]{1,0:T(8,128)(2,1)S(1)}, bf16[128,256]{1,0:T(8,128)(2,1)}, u32[]{:S(2)}) copy-start(bf16[128,256]{1,0:T(8,128)(2,1)} %refs_9_.1) | copy-start | bytes 196612
  0.7 46.6 %copy-start.2 = (bf16[128,256]{1,0:T(8,128)(2,1)S(1)}, bf16[128,256]{1,0:T(8,128)(2,1)}, u32[]{:S(2)}) copy-start(bf16[128,256]{1,0:T(8,128)(2,1)} %refs_10_.1) | copy-start | bytes 196612
  3.4 21.2 %all-to-all-start.1 = ((bf16[32,16,128]{2,1,0:T(8,128)(2,1)}), bf16[32,16,128]{2,1,0:T(8,128)(2,1)S(1)}, u32[]{:S(2)}, u32[]{:S(2)}) async-start(bf16[32,16,128]{2,1,0:T(8,128)(2,1)} %hub_pack.1), calls=%async_computation.1 | async-start | bytes 262144 | tf_op jit(solution)/shard_map/all_to_all | solution.py:776
  24.6 22.6 %all-to-all-start = ((bf16[64,32,128]{2,1,0:T(8,128)(2,1)}), bf16[64,32,128]{2,1,0:T(8,128)(2,1)S(1)}, u32[]{:S(2)}, u32[]{:S(2)}) async-start(bf16[64,32,128]{2,1,0:T(8,128)(2,1)} %halo_pack.1), calls=%async_computation | async-start | bytes 1048576 | tf_op jit(solution)/shard_map/all_to_all | solution.py:776
  30.1 6.8 %collective-permute-start = (bf16[32,16,128]{2,1,0:T(8,128)(2,1)S(1)}, bf16[32,16,128]{2,1,0:T(8,128)(2,1)S(1)}, u32[]{:S(2)}, u32[]{:S(2)}) collective-permute-start(bf16[32,16,128]{2,1,0:T(8,128)(2,1)S(1)} %all-to-all-done.1.refs_0_), channel_id=1, source_target_pairs={{0,1},{1,2},{2,3},{3,0},{4,5},{5,6},{6,7},{7,4},{8,9},{9,10},{10,1... | collective-permute-start | bytes 393224 | tf_op jit(solution)/shard_map/ppermute | solution.py:768
  31.7 9.1 %collective-permute-start.1 = (bf16[32,16,128]{2,1,0:T(8,128)(2,1)S(1)}, bf16[32,16,128]{2,1,0:T(8,128)(2,1)S(1)}, u32[]{:S(2)}, u32[]{:S(2)}) collective-permute-start(bf16[32,16,128]{2,1,0:T(8,128)(2,1)S(1)} %all-to-all-done.1.refs_0_), channel_id=1, source_target_pairs={{0,2},{1,3},{2,0},{3,1},{4,6},{5,7},{6,4},{7,5},{8,10},{9,11},{10,... | collective-permute-start | bytes 393224 | tf_op jit(solution)/shard_map/ppermute | solution.py:768
  34.4 6.3 %collective-permute-start.2 = (bf16[32,16,128]{2,1,0:T(8,128)(2,1)S(1)}, bf16[32,16,128]{2,1,0:T(8,128)(2,1)S(1)}, u32[]{:S(2)}, u32[]{:S(2)}) collective-permute-start(bf16[32,16,128]{2,1,0:T(8,128)(2,1)S(1)} %all-to-all-done.1.refs_0_), channel_id=1, source_target_pairs={{0,3},{1,0},{2,1},{3,2},{4,7},{5,4},{6,5},{7,6},{8,11},{9,8},{10,9... | collective-permute-start | bytes 393224 | tf_op jit(solution)/shard_map/ppermute | solution.py:768
  35.8 6.1 %collective-permute-start.3 = (bf16[32,16,128]{2,1,0:T(8,128)(2,1)S(1)}, bf16[32,16,128]{2,1,0:T(8,128)(2,1)S(1)}, u32[]{:S(2)}, u32[]{:S(2)}) collective-permute-start(bf16[32,16,128]{2,1,0:T(8,128)(2,1)S(1)} %all-to-all-done.1.refs_0_), channel_id=1, source_target_pairs={{0,4},{4,0},{1,5},{5,1},{2,6},{6,2},{3,7},{7,3},{8,12},{12,8},{9,1... | collective-permute-start | bytes 393224 | tf_op jit(solution)/shard_map/ppermute | solution.py:772
  36.9 5.0 %collective-permute-start.4 = (bf16[32,16,128]{2,1,0:T(8,128)(2,1)S(1)}, bf16[32,16,128]{2,1,0:T(8,128)(2,1)S(1)}, u32[]{:S(2)}, u32[]{:S(2)}) collective-permute-start(bf16[32,16,128]{2,1,0:T(8,128)(2,1)S(1)} %collective-permute-done.refs_1_), channel_id=1, source_target_pairs={{0,4},{4,0},{1,5},{5,1},{2,6},{6,2},{3,7},{7,3},{8,12},{12,8},{9,1... | collective-permute-start | bytes 393224 | tf_op jit(solution)/shard_map/ppermute | solution.py:772
  40.7 1.3 %collective-permute-start.5 = (bf16[32,16,128]{2,1,0:T(8,128)(2,1)S(1)}, bf16[32,16,128]{2,1,0:T(8,128)(2,1)S(1)}, u32[]{:S(2)}, u32[]{:S(2)}) collective-permute-start(bf16[32,16,128]{2,1,0:T(8,128)(2,1)S(1)} %collective-permute-done.1.refs_2_), channel_id=1, source_target_pairs={{0,4},{4,0},{1,5},{5,1},{2,6},{6,2},{3,7},{7,3},{8,12},{12,8},{9,1... | collective-permute-start | bytes 393224 | tf_op jit(solution)/shard_map/ppermute | solution.py:772
  40.7 1.5 %collective-permute-start.6 = (bf16[32,16,128]{2,1,0:T(8,128)(2,1)S(1)}, bf16[32,16,128]{2,1,0:T(8,128)(2,1)S(1)}, u32[]{:S(2)}, u32[]{:S(2)}) collective-permute-start(bf16[32,16,128]{2,1,0:T(8,128)(2,1)S(1)} %collective-permute-done.2.refs_3_), channel_id=1, source_target_pairs={{0,4},{4,0},{1,5},{5,1},{2,6},{6,2},{3,7},{7,3},{8,12},{12,8},{9,1... | collective-permute-start | bytes 393224 | tf_op jit(solution)/shard_map/ppermute | solution.py:772
  55.1 16.5 %all-to-all-start.2 = ((bf16[32,16,128]{2,1,0:T(8,128)(2,1)}), bf16[32,16,128]{2,1,0:T(8,128)(2,1)S(1)}, u32[]{:S(2)}, u32[]{:S(2)}) async-start(bf16[32,16,128]{2,1,0:T(8,128)(2,1)} %bitcast.3), calls=%async_computation.2 | async-start | bytes 262144 | tf_op jit(solution)/shard_map/all_to_all | solution.py:776
  66.5 34.7 %copy-start.6 = (s32[64,32]{0,1:T(8,128)S(1)}, s32[64,32]{0,1:T(8,128)}, u32[]{:S(2)}) copy-start(s32[64,32]{0,1:T(8,128)} %param.16) | copy-start | bytes 24580
  66.6 34.7 %copy-start.7 = (s32[64]{0:T(128)S(1)}, s32[64]{0:T(128)}, u32[]{:S(2)}) copy-start(s32[64]{0:T(128)} %send_counts.1) | copy-start | bytes 772
  66.6 35.0 %copy-start = (bf16[4096,128]{1,0:T(8,128)(2,1)S(1)}, bf16[4096,128]{1,0:T(8,128)(2,1)}, u32[]{:S(2)}) copy-start(bf16[4096,128]{1,0:T(8,128)(2,1)} %get-tuple-element.21.grad_agg) | copy-start | bytes 3145732
  66.6 35.0 %copy-start.5 = (s32[16]{0:T(128)S(1)}, s32[16]{0:T(128)}, u32[]{:S(2)}) copy-start(s32[16]{0:T(128)} %hub_rows.5) | copy-start | bytes 196
  71.6 22.9 %all-to-all-start.4 = ((bf16[64,32,128]{2,1,0:T(8,128)(2,1)}), bf16[64,32,128]{2,1,0:T(8,128)(2,1)S(1)}, u32[]{:S(2)}, u32[]{:S(2)}) async-start(bf16[64,32,128]{2,1,0:T(8,128)(2,1)} %get-tuple-element.30), calls=%async_computation.4 | async-start | bytes 1048576 | tf_op jit(solution)/shard_map/all_to_all | solution.py:776
  77.4 2.0 %collective-permute-start.7 = (bf16[4,32,16,128]{3,2,1,0:T(8,128)(2,1)S(1)}, bf16[4,32,16,128]{3,2,1,0:T(8,128)(2,1)S(1)}, u32[]{:S(2)}, u32[]{:S(2)}) collective-permute-start(bf16[4,32,16,128]{3,2,1,0:T(8,128)(2,1)S(1)} %get-tuple-element.23), channel_id=1, source_target_pairs={{0,4},{4,0},{1,5},{5,1},{2,6},{6,2},{3,7},{7,3},{8,12},{12,8},{9,1... | collective-permute-start | bytes 1572872 | tf_op jit(solution)/shard_map/ppermute | solution.py:772
  77.8 1.6 %collective-permute-start.8 = (bf16[2,16,128]{2,1,0:T(8,128)(2,1)S(1)}, bf16[2,16,128]{2,1,0:T(8,128)(2,1)S(1)}, u32[]{:S(2)}, u32[]{:S(2)}) collective-permute-start(bf16[2,16,128]{2,1,0:T(8,128)(2,1)S(1)} %fold.1.w_near), channel_id=1, source_target_pairs={{0,4},{4,0},{1,5},{5,1},{2,6},{6,2},{3,7},{7,3},{8,12},{12,8},{9,1... | collective-permute-start | bytes 24584 | tf_op jit(solution)/shard_map/ppermute | solution.py:772
  79.8 7.6 %collective-permute-start.9 = (bf16[34,16,128]{2,1,0:T(8,128)(2,1)S(1)}, bf16[34,16,128]{2,1,0:T(8,128)(2,1)S(1)}, u32[]{:S(2)}, u32[]{:S(2)}) collective-permute-start(bf16[34,16,128]{2,1,0:T(8,128)(2,1)S(1)} %get-tuple-element.26), channel_id=1, source_target_pairs={{0,1},{1,2},{2,3},{3,0},{4,5},{5,6},{6,7},{7,4},{8,9},{9,10},{10,1... | collective-permute-start | bytes 417800 | tf_op jit(solution)/shard_map/ppermute | solution.py:768
  80.7 9.3 %collective-permute-start.10 = (bf16[34,16,128]{2,1,0:T(8,128)(2,1)S(1)}, bf16[34,16,128]{2,1,0:T(8,128)(2,1)S(1)}, u32[]{:S(2)}, u32[]{:S(2)}) collective-permute-start(bf16[34,16,128]{2,1,0:T(8,128)(2,1)S(1)} %get-tuple-element.27), channel_id=1, source_target_pairs={{0,2},{1,3},{2,0},{3,1},{4,6},{5,7},{6,4},{7,5},{8,10},{9,11},{10,... | collective-permute-start | bytes 417800 | tf_op jit(solution)/shard_map/ppermute | solution.py:768
  83.3 7.0 %collective-permute-start.11 = (bf16[34,16,128]{2,1,0:T(8,128)(2,1)S(1)}, bf16[34,16,128]{2,1,0:T(8,128)(2,1)S(1)}, u32[]{:S(2)}, u32[]{:S(2)}) collective-permute-start(bf16[34,16,128]{2,1,0:T(8,128)(2,1)S(1)} %get-tuple-element.28), channel_id=1, source_target_pairs={{0,3},{1,0},{2,1},{3,2},{4,7},{5,4},{6,5},{7,6},{8,11},{9,8},{10,9... | collective-permute-start | bytes 417800 | tf_op jit(solution)/shard_map/ppermute | solution.py:768
  94.5 18.4 %all-to-all-start.3 = ((bf16[32,32,128]{2,1,0:T(8,128)(2,1)}), bf16[32,32,128]{2,1,0:T(8,128)(2,1)S(1)}, u32[]{:S(2)}, u32[]{:S(2)}) async-start(bf16[32,32,128]{2,1,0:T(8,128)(2,1)} %merge.1), calls=%async_computation.3 | async-start | bytes 524288 | tf_op jit(solution)/shard_map/all_to_all | solution.py:776
